TPU v7x, 256 devices: a whole 4x4x8 slice. The times are simulated.
256 devices in a mesh: pair: 2 (over y_lo), lat: 128 (over z, x, y_hi, core).
Axes of the slice: x: 4, y: 4 (y_hi: 2, y_lo: 2; y = y_hi * 2 + y_lo), z: 8, core: 2. Of those that a mesh axis runs over, the one named last changes fastest.
Arguments:
- activations: bfloat16 [2, 256, 8192], P('pair', 'lat'), may hold values from -6 to 6
- enc_weight: bfloat16 [2, 16384, 8192], P('pair', 'lat'), may hold values from -0.046875 to 0.046875
- enc_bias: float32 [16384], P('lat'), may hold values from -3 to 3
- dec_weight: bfloat16 [2, 16384, 8192], P('pair', 'lat'), may hold values from -0.046875 to 0.046875
- dec_bias: float32 [2, 8192], P('pair'), may hold values from -6 to 6
- block_list: int32 [256], P('lat'), may hold values from 0 to 1, as said below
- block_count: int32 [128], P('lat'), may hold values from 1 to 2, as said below
Outputs:
- d_enc_weight: bfloat16 [2, 16384, 8192], P('pair', 'lat')
- d_dec_weight: bfloat16 [2, 16384, 8192], P('pair', 'lat')
- d_enc_bias: float32 [16384], P('lat')
- d_dec_bias: float32 [2, 8192], P('pair')
Inputs may be any that keep to these rules, and one draw needn't show every extreme that they name: `block_list`: for each latent block, the first block_count entries of its list are distinct token blocks; the later entries are token blocks too and are not live. `block_count`: some latent block lists all 2 token blocks and some lists one.
All inputs are finite; a program needn't handle non-finite values.
Results may differ from a plain program's by a relative error of at most 0.0075.
Values may be sent and summed in bfloat16 or wider, within the bound.
No kernel may reach another device: no remote copies, remote signals or barrier semaphores. Data moves between devices by JAX's collectives and lax.ppermute only.
A program may use at most 128 MiB of HBM per device.

v0:
```python
import jax
import jax.numpy as jnp
import numpy as np
from jax import lax
from jax.experimental import pallas as pl
from jax.experimental.pallas import tpu as pltpu
from jax.sharding import PartitionSpec as P

BLK = 128
NZ, NX, NY, NC = 8, 4, 2, 2

epsilon = 1e-06
sparsity = 0.25
loss_scale = 0.0625

COLUMNS = ((0, 0), (0, 2), (0, 1), (0, -1), (-1, -1), (1, 1), (-1, 0), (1, 2))
ROW_Z = np.array([dz + 2 * k for _ in range(NC) for dz, _ in COLUMNS for k in range(4) for _ in range(4)], np.int32)


def place(z, x, y, c):
    return (((z % NZ) * NX + x % NX) * NY + y % NY) * NC + c % NC


def fetch(value, z=0, x=0, y=0, c=0):
    pairs = [
        (place(iz + z, ix + x, iy + y, ic + c), place(iz, ix, iy, ic))
        for iz in range(NZ)
        for ix in range(NX)
        for iy in range(NY)
        for ic in range(NC)
    ]
    return lax.ppermute(value, "lat", pairs)


def pack(pieces):
    rows = [piece.shape[0] for piece in pieces]

    def kernel(*refs):
        at = 0
        for ref, count in zip(refs[:-1], rows):
            refs[-1][at : at + count, :] = ref[...]
            at += count

    return pl.pallas_call(
        kernel,
        out_shape=jax.ShapeDtypeStruct((sum(rows), pieces[0].shape[1]), pieces[0].dtype),
        in_specs=[pl.BlockSpec(memory_space=pltpu.VMEM)] * len(pieces),
        out_specs=pl.BlockSpec(memory_space=pltpu.VMEM),
        compiler_params=pltpu.CompilerParams(vmem_limit_bytes=32 * 1024 * 1024),
    )(*pieces)


def gather_rows(own):
    four = jnp.concatenate([own, fetch(own, y=1)], axis=0)
    column = jnp.concatenate([four] + [fetch(four, z=k) for k in (2, 4, 6)], axis=0)
    two = fetch(column, x=2)
    first = pack([column, two, fetch(column, x=1), fetch(column, x=-1)])
    second = pack(
        [fetch(column, z=-1, x=-1), fetch(column, z=1, x=1), fetch(column, z=-1), fetch(two, z=1)]
    )
    return pack([first, second, fetch(first, c=1), fetch(second, c=1)])


def low(value):
    return value.astype(jnp.bfloat16)


def add(value, arrived):
    return value + arrived.astype(jnp.float32)


def scatter_rows(latent, dec):
    rows = latent.shape[0] // 2
    theirs = low(dot(latent[rows:], dec, (1, 0)))
    mine = add(dot(latent[:rows], dec, (1, 0)), fetch(theirs, c=1))
    c, two, up, down, diag, other, back, far = [mine[16 * k : 16 * k + 16] for k in range(8)]
    two = add(two, fetch(low(far), z=-1))
    c = add(c, fetch(low(up), x=-1))
    c = add(c, fetch(low(down), x=1))
    c = add(c, fetch(low(diag), z=1, x=1))
    c = add(c, fetch(low(other), z=-1, x=-1))
    c = add(c, fetch(low(back), z=1))
    c = add(c, fetch(low(two), x=2))
    four = c[0:4]
    for k in (1, 2, 3):
        four = add(four, fetch(low(c[4 * k : 4 * k + 4]), z=-2 * k))
    return four[0:2] + fetch(four[2:4], y=1)


def swap_pair(value):
    return lax.ppermute(value, "pair", [(0, 1), (1, 0)])


def dot(left, right, over):
    return lax.dot_general(left, right, ((over[:1], over[1:]), ((), ())), preferred_element_type=jnp.float32)


def on_device(activations, enc_weight, enc_bias, dec_weight, dec_bias, block_list, block_count):
    enc, dec = enc_weight[0], dec_weight[0]
    own = activations[0]
    act = gather_rows(own)
    tokens = act.shape[0]

    z_row = (lax.axis_index("lat") // (NX * NY * NC) + ROW_Z) % NZ
    block = z_row * (2 * NX * NY * NC) // BLK
    slots = jnp.arange(block_list.shape[0], dtype=jnp.int32) < block_count[0]
    live = jnp.any((block[:, None] == block_list[None, :]) & slots[None, :], axis=1)
    live = live.astype(jnp.float32)[:, None]

    norm_own = jnp.sqrt(jnp.sum(jnp.square(dec.astype(jnp.float32)), axis=1) + epsilon)
    pre_part = dot(act, enc, (1, 1))
    packed = jnp.concatenate([pre_part, jnp.broadcast_to(norm_own[None, :], (8, norm_own.shape[0]))], axis=0)
    packed = packed + swap_pair(packed)
    norm_sum = packed[tokens : tokens + 1]
    pre_act = packed[:tokens] + enc_bias[None, :]
    latent_act = jax.nn.softplus(pre_act) * live
    latent_low = low(latent_act)

    rebuilt = scatter_rows(latent_low, dec) + dec_bias
    err = gather_rows(low(loss_scale * (rebuilt - own.astype(jnp.float32))))

    grad_part = dot(err, dec, (1, 1))
    grad_sum = grad_part + swap_pair(grad_part)
    grad_latent = (grad_sum + loss_scale * sparsity * norm_sum) * live
    pre_grad = grad_latent * jax.nn.sigmoid(pre_act)
    pre_low = low(pre_grad)

    act_total = jnp.sum(latent_act, axis=0)
    d_dec = dot(latent_low, err, (0, 0))
    d_dec = d_dec + (loss_scale * sparsity * act_total / norm_own)[:, None] * dec.astype(jnp.float32)
    d_dec_bias = dot(jnp.ones((8, tokens), jnp.bfloat16), err, (1, 0))[0:1]
    d_enc = dot(pre_low, act, (0, 0))
    d_enc_bias = jnp.sum(pre_grad, axis=0)
    return low(d_enc)[None], low(d_dec)[None], d_enc_bias, d_dec_bias


def solution(mesh):
    placed = (
        P("pair", "lat", None),
        P("pair", "lat", None),
        P("lat"),
        P("pair", "lat", None),
        P("pair", None),
        P("lat"),
        P("lat"),
    )
    return jax.shard_map(
        on_device,
        mesh=mesh,
        in_specs=placed,
        out_specs=(P("pair", "lat", None), P("pair", "lat", None), P("lat"), P("pair", None)),
        check_vma=False,
    )
```

profile of v0, /device:TPU:1, one launch (start us, length us, event | category | flops | bytes accessed | tf_op | source)
XLA Modules:
  0.0 167.0 jit_solution(16367276983644001043)
XLA Ops:
  0.7 3.8 %collective-permute-start = (bf16[2,8192]{1,0:T(2,128)(2,1)}, bf16[2,8192]{1,0:T(2,128)(2,1)S(1)}, u32[]{:S(2)}, u32[]{:S(2)}) collective-permute-start(bf16[2,8192]{1,0:T(2,128)(2,1)} %bitcast.34), channel_id=1, source_target_pairs={{2,0},{3,1},{0,2},{1,3},{6,4},{7,5},{4,6},{5,7},{10,8},{11,9},{8,1... | collective-permute-start | bytes 98312 | tf_op jit(solution)/shard_map/ppermute | solution.py:32
  6.8 6.1 %collective-permute-start.1 = (bf16[4,8192]{1,0:T(4,128)(2,1)S(1)}, bf16[4,8192]{1,0:T(4,128)(2,1)S(1)}, u32[]{:S(2)}, u32[]{:S(2)}) collective-permute-start(bf16[4,8192]{1,0:T(4,128)(2,1)S(1)} %pad_maximum_fusion.1), channel_id=1, source_target_pairs={{32,0},{33,1},{34,2},{35,3},{36,4},{37,5},{38,6},{39,7},{40,8},{41... | collective-permute-start | bytes 196616 | tf_op jit(solution)/shard_map/ppermute | solution.py:32
  14.0 2.3 %collective-permute-start.3 = (bf16[4,8192]{1,0:T(4,128)(2,1)S(1)}, bf16[4,8192]{1,0:T(4,128)(2,1)S(1)}, u32[]{:S(2)}, u32[]{:S(2)}) collective-permute-start(bf16[4,8192]{1,0:T(4,128)(2,1)S(1)} %pad_maximum_fusion.1), channel_id=1, source_target_pairs={{96,0},{97,1},{98,2},{99,3},{100,4},{101,5},{102,6},{103,7},{104,8... | collective-permute-start | bytes 196616 | tf_op jit(solution)/shard_map/ppermute | solution.py:32
  16.2 4.0 %collective-permute-done.2 = bf16[4,8192]{1,0:T(4,128)(2,1)S(1)} collective-permute-done((bf16[4,8192]{1,0:T(4,128)(2,1)S(1)}, bf16[4,8192]{1,0:T(4,128)(2,1)S(1)}, u32[]{:S(2)}, u32[]{:S(2)}) %collective-permute-start.2) | collective-permute-done | bytes 65568 | tf_op jit(solution)/shard_map/ppermute | solution.py:32
  21.5 2.8 %collective-permute-start.4 = (bf16[16,8192]{1,0:T(8,128)(2,1)S(1)}, bf16[16,8192]{1,0:T(8,128)(2,1)S(1)}, u32[]{:S(2)}, u32[]{:S(2)}) collective-permute-start(bf16[16,8192]{1,0:T(8,128)(2,1)S(1)} %concatenate.18.refs_0_), channel_id=1, source_target_pairs={{8,0},{9,1},{10,2},{11,3},{12,4},{13,5},{14,6},{15,7},{0,8},{1,9},... | collective-permute-start | bytes 786440 | tf_op jit(solution)/shard_map/ppermute | solution.py:32
  26.4 4.1 %collective-permute-start.8 = (bf16[16,8192]{1,0:T(8,128)(2,1)S(1)}, bf16[16,8192]{1,0:T(8,128)(2,1)S(1)}, u32[]{:S(2)}, u32[]{:S(2)}) collective-permute-start(bf16[16,8192]{1,0:T(8,128)(2,1)S(1)} %concatenate.18.refs_0_), channel_id=1, source_target_pairs={{20,0},{21,1},{22,2},{23,3},{24,4},{25,5},{26,6},{27,7},{28,8},{29... | collective-permute-start | bytes 786440 | tf_op jit(solution)/shard_map/ppermute | solution.py:32
  30.5 8.0 %collective-permute-done.5.refs_2_ = bf16[16,8192]{1,0:T(8,128)(2,1)S(1)} collective-permute-done((bf16[16,8192]{1,0:T(8,128)(2,1)S(1)}, bf16[16,8192]{1,0:T(8,128)(2,1)S(1)}, u32[]{:S(2)}, u32[]{:S(2)}) %collective-permute-start.5) | collective-permute-done | bytes 262176 | tf_op jit(solution)/shard_map/ppermute | solution.py:32
  38.5 4.7 %collective-permute-start.10 = (bf16[16,8192]{1,0:T(8,128)(2,1)S(1)}, bf16[16,8192]{1,0:T(8,128)(2,1)S(1)}, u32[]{:S(2)}, u32[]{:S(2)}) collective-permute-start(bf16[16,8192]{1,0:T(8,128)(2,1)S(1)} %collective-permute-done.4.refs_1_), channel_id=1, source_target_pairs={{16,0},{17,1},{18,2},{19,3},{20,4},{21,5},{22,6},{23,7},{24,8},{25... | collective-permute-start | bytes 786440 | tf_op jit(solution)/shard_map/ppermute | solution.py:32
  43.3 2.1 %collective-permute-start.11 = (bf16[64,8192]{1,0:T(8,128)(2,1)S(1)}, bf16[64,8192]{1,0:T(8,128)(2,1)}, u32[]{:S(2)}, u32[]{:S(2)}) collective-permute-start(bf16[64,8192]{1,0:T(8,128)(2,1)S(1)} %shard_map.111.refs_0_), channel_id=1, source_target_pairs={{1,0},{0,1},{3,2},{2,3},{5,4},{4,5},{7,6},{6,7},{9,8},{8,9},{11,10... | collective-permute-start | bytes 3145736 | tf_op jit(solution)/shard_map/ppermute | solution.py:32
  48.1 3.1 %collective-permute-start.12 = (bf16[64,8192]{1,0:T(8,128)(2,1)}, bf16[64,8192]{1,0:T(8,128)(2,1)}, u32[]{:S(2)}, u32[]{:S(2)}) collective-permute-start(bf16[64,8192]{1,0:T(8,128)(2,1)} %shard_map.112.refs_1_), channel_id=1, source_target_pairs={{1,0},{0,1},{3,2},{2,3},{5,4},{4,5},{7,6},{6,7},{9,8},{8,9},{11,10... | collective-permute-start | bytes 3145736 | tf_op jit(solution)/shard_map/ppermute | solution.py:32
  54.0 2.1 %shard_map.113 = bf16[256,8192]{1,0:T(8,128)(2,1)S(1)} custom-call(bf16[64,8192]{1,0:T(8,128)(2,1)S(1)} %shard_map.111.refs_0_, bf16[64,8192]{1,0:T(8,128)(2,1)} %shard_map.112.refs_1_, bf16[64,8192]{1,0:T(8,128)(2,1)} %collective-permute-done.11.refs_2_, bf16[64,8192]{1,0:T(8,128)(2,1)} %collective-permute-done.12.refs_3_), custom_call_target="tpu_custom_call" | custom-call | tf_op jit(solution)/shard_map/pallas_call | solution.py:44
  59.1 3.6 %collective-permute-done.13 = f32[264,128]{1,0:T(8,128)S(1)} collective-permute-done((f32[264,128]{1,0:T(8,128)S(1)}, f32[264,128]{1,0:T(8,128)S(1)}, u32[]{:S(2)}, u32[]{:S(2)}) %collective-permute-start.13) | collective-permute-done | bytes 135200 | tf_op jit(solution)/shard_map/ppermute | solution.py:91
  64.7 3.8 %collective-permute-done.14 = bf16[128,8192]{1,0:T(8,128)(2,1)S(1)} collective-permute-done((bf16[128,8192]{1,0:T(8,128)(2,1)S(1)}, bf16[128,8192]{1,0:T(8,128)(2,1)S(1)}, u32[]{:S(2)}, u32[]{:S(2)}) %collective-permute-start.14) | collective-permute-done | bytes 2097184 | tf_op jit(solution)/shard_map/ppermute | solution.py:32
  70.2 2.1 %collective-permute-start.15 = (bf16[16,8192]{1,0:T(8,128)(2,1)S(1)}, bf16[16,8192]{1,0:T(8,128)(2,1)S(1)}, u32[]{:S(2)}, u32[]{:S(2)}) collective-permute-start(bf16[16,8192]{1,0:T(8,128)(2,1)S(1)} %get-tuple-element.8), channel_id=1, source_target_pairs={{12,0},{13,1},{14,2},{15,3},{0,4},{1,5},{2,6},{3,7},{4,8},{5,9},{6... | collective-permute-start | bytes 786440 | tf_op jit(solution)/shard_map/ppermute | solution.py:32
  73.6 3.5 %collective-permute-start.17 = (bf16[16,8192]{1,0:T(8,128)(2,1)S(1)}, bf16[16,8192]{1,0:T(8,128)(2,1)S(1)}, u32[]{:S(2)}, u32[]{:S(2)}) collective-permute-start(bf16[16,8192]{1,0:T(8,128)(2,1)S(1)} %get-tuple-element.12), channel_id=1, source_target_pairs={{20,0},{21,1},{22,2},{23,3},{24,4},{25,5},{26,6},{27,7},{28,8},{29... | collective-permute-start | bytes 786440 | tf_op jit(solution)/shard_map/ppermute | solution.py:32
  82.0 2.8 %collective-permute-done.16 = bf16[16,8192]{1,0:T(8,128)(2,1)S(1)} collective-permute-done((bf16[16,8192]{1,0:T(8,128)(2,1)S(1)}, bf16[16,8192]{1,0:T(8,128)(2,1)S(1)}, u32[]{:S(2)}, u32[]{:S(2)}) %collective-permute-start.16) | collective-permute-done | bytes 262176 | tf_op jit(solution)/shard_map/ppermute | solution.py:32
  84.8 2.2 %collective-permute-done.18 = bf16[16,8192]{1,0:T(8,128)(2,1)S(1)} collective-permute-done((bf16[16,8192]{1,0:T(8,128)(2,1)S(1)}, bf16[16,8192]{1,0:T(8,128)(2,1)S(1)}, u32[]{:S(2)}, u32[]{:S(2)}) %collective-permute-start.18) | collective-permute-done | bytes 262176 | tf_op jit(solution)/shard_map/ppermute | solution.py:32
  87.4 6.8 %collective-permute-done.21 = bf16[16,8192]{1,0:T(8,128)(2,1)S(1)} collective-permute-done((bf16[16,8192]{1,0:T(8,128)(2,1)S(1)}, bf16[16,8192]{1,0:T(8,128)(2,1)S(1)}, u32[]{:S(2)}, u32[]{:S(2)}) %collective-permute-start.21) | collective-permute-done | bytes 262176 | tf_op jit(solution)/shard_map/ppermute | solution.py:32
  94.6 2.4 %collective-permute-start.23 = (bf16[4,8192]{1,0:T(4,128)(2,1)S(1)}, bf16[4,8192]{1,0:T(4,128)(2,1)S(1)}, u32[]{:S(2)}, u32[]{:S(2)}) collective-permute-start(bf16[4,8192]{1,0:T(4,128)(2,1)S(1)} %get-tuple-element.16), channel_id=1, source_target_pairs={{64,0},{65,1},{66,2},{67,3},{68,4},{69,5},{70,6},{71,7},{72,8},{73... | collective-permute-start | bytes 196616 | tf_op jit(solution)/shard_map/ppermute | solution.py:32
  97.1 3.5 %collective-permute-start.24 = (bf16[4,8192]{1,0:T(4,128)(2,1)S(1)}, bf16[4,8192]{1,0:T(4,128)(2,1)S(1)}, u32[]{:S(2)}, u32[]{:S(2)}) collective-permute-start(bf16[4,8192]{1,0:T(4,128)(2,1)S(1)} %get-tuple-element.15), channel_id=1, source_target_pairs={{32,0},{33,1},{34,2},{35,3},{36,4},{37,5},{38,6},{39,7},{40,8},{41... | collective-permute-start | bytes 196616 | tf_op jit(solution)/shard_map/ppermute | solution.py:32
  103.6 3.0 %collective-permute-start.25 = (f32[2,8192]{1,0:T(2,128)S(1)}, f32[2,8192]{1,0:T(2,128)S(1)}, u32[]{:S(2)}, u32[]{:S(2)}) collective-permute-start(f32[2,8192]{1,0:T(2,128)S(1)} %slice.103), channel_id=1, source_target_pairs={{2,0},{3,1},{0,2},{1,3},{6,4},{7,5},{4,6},{5,7},{10,8},{11,9},{8,1... | collective-permute-start | bytes 196616 | tf_op jit(solution)/shard_map/ppermute | solution.py:32
  108.4 3.0 %collective-permute-start.26 = (bf16[2,8192]{1,0:T(2,128)(2,1)S(1)}, bf16[2,8192]{1,0:T(2,128)(2,1)S(1)}, u32[]{:S(2)}, u32[]{:S(2)}) collective-permute-start(bf16[2,8192]{1,0:T(2,128)(2,1)S(1)} %fusion.26), channel_id=1, source_target_pairs={{2,0},{3,1},{0,2},{1,3},{6,4},{7,5},{4,6},{5,7},{10,8},{11,9},{8,1... | collective-permute-start | bytes 98312 | tf_op jit(solution)/shard_map/ppermute | solution.py:32
  112.8 4.4 %collective-permute-start.27 = (bf16[4,8192]{1,0:T(4,128)(2,1)S(1)}, bf16[4,8192]{1,0:T(4,128)(2,1)S(1)}, u32[]{:S(2)}, u32[]{:S(2)}) collective-permute-start(bf16[4,8192]{1,0:T(4,128)(2,1)S(1)} %pad_maximum_fusion.2), channel_id=1, source_target_pairs={{32,0},{33,1},{34,2},{35,3},{36,4},{37,5},{38,6},{39,7},{40,8},{41... | collective-permute-start | bytes 196616 | tf_op jit(solution)/shard_map/ppermute | solution.py:32
  119.6 4.8 %collective-permute-done.28 = bf16[4,8192]{1,0:T(4,128)(2,1)S(1)} collective-permute-done((bf16[4,8192]{1,0:T(4,128)(2,1)S(1)}, bf16[4,8192]{1,0:T(4,128)(2,1)S(1)}, u32[]{:S(2)}, u32[]{:S(2)}) %collective-permute-start.28) | collective-permute-done | bytes 65568 | tf_op jit(solution)/shard_map/ppermute | solution.py:32
  124.6 4.6 %collective-permute-start.30 = (bf16[16,8192]{1,0:T(8,128)(2,1)S(1)}, bf16[16,8192]{1,0:T(8,128)(2,1)S(1)}, u32[]{:S(2)}, u32[]{:S(2)}) collective-permute-start(bf16[16,8192]{1,0:T(8,128)(2,1)S(1)} %concatenate.21.refs_0_), channel_id=1, source_target_pairs={{8,0},{9,1},{10,2},{11,3},{12,4},{13,5},{14,6},{15,7},{0,8},{1,9},... | collective-permute-start | bytes 786440 | tf_op jit(solution)/shard_map/ppermute | solution.py:32
  130.7 4.8 %collective-permute-start.34 = (bf16[16,8192]{1,0:T(8,128)(2,1)S(1)}, bf16[16,8192]{1,0:T(8,128)(2,1)S(1)}, u32[]{:S(2)}, u32[]{:S(2)}) collective-permute-start(bf16[16,8192]{1,0:T(8,128)(2,1)S(1)} %concatenate.21.refs_0_), channel_id=1, source_target_pairs={{20,0},{21,1},{22,2},{23,3},{24,4},{25,5},{26,6},{27,7},{28,8},{29... | collective-permute-start | bytes 786440 | tf_op jit(solution)/shard_map/ppermute | solution.py:32
  135.5 2.3 %collective-permute-done.31.refs_2_ = bf16[16,8192]{1,0:T(8,128)(2,1)S(1)} collective-permute-done((bf16[16,8192]{1,0:T(8,128)(2,1)S(1)}, bf16[16,8192]{1,0:T(8,128)(2,1)S(1)}, u32[]{:S(2)}, u32[]{:S(2)}) %collective-permute-start.31) | collective-permute-done | bytes 262176 | tf_op jit(solution)/shard_map/ppermute | solution.py:32
  140.2 8.0 %collective-permute-start.37 = (bf16[64,8192]{1,0:T(8,128)(2,1)S(1)}, bf16[64,8192]{1,0:T(8,128)(2,1)S(1)}, u32[]{:S(2)}, u32[]{:S(2)}) collective-permute-start(bf16[64,8192]{1,0:T(8,128)(2,1)S(1)} %shard_map.114.refs_0_), channel_id=1, source_target_pairs={{1,0},{0,1},{3,2},{2,3},{5,4},{4,5},{7,6},{6,7},{9,8},{8,9},{11,10... | collective-permute-start | bytes 3145736 | tf_op jit(solution)/shard_map/ppermute | solution.py:32
  148.3 4.6 %collective-permute-start.38 = (bf16[64,8192]{1,0:T(8,128)(2,1)S(1)}, bf16[64,8192]{1,0:T(8,128)(2,1)S(1)}, u32[]{:S(2)}, u32[]{:S(2)}) collective-permute-start(bf16[64,8192]{1,0:T(8,128)(2,1)S(1)} %shard_map.115.refs_1_), channel_id=1, source_target_pairs={{1,0},{0,1},{3,2},{2,3},{5,4},{4,5},{7,6},{6,7},{9,8},{8,9},{11,10... | collective-permute-start | bytes 3145736 | tf_op jit(solution)/shard_map/ppermute | solution.py:32
  153.0 2.3 %collective-permute-done.38.refs_3_ = bf16[64,8192]{1,0:T(8,128)(2,1)S(1)} collective-permute-done((bf16[64,8192]{1,0:T(8,128)(2,1)S(1)}, bf16[64,8192]{1,0:T(8,128)(2,1)S(1)}, u32[]{:S(2)}, u32[]{:S(2)}) %collective-permute-start.38) | collective-permute-done | bytes 1048608 | tf_op jit(solution)/shard_map/ppermute | solution.py:32
  159.4 2.1 %collective-permute-done.39 = f32[256,128]{1,0:T(8,128)S(1)} collective-permute-done((f32[256,128]{1,0:T(8,128)S(1)}, f32[256,128]{1,0:T(8,128)S(1)}, u32[]{:S(2)}, u32[]{:S(2)}) %collective-permute-start.39) | collective-permute-done | bytes 131104 | tf_op jit(solution)/shard_map/ppermute | solution.py:91
  162.3 2.6 %fusion.2 = bf16[1,128,8192]{2,1,0:T(8,128)(2,1)} fusion(bf16[256,128]{1,0:T(8,128)(2,1)S(1)} %fusion.30, bf16[256,8192]{1,0:T(8,128)(2,1)S(1)} %shard_map.116, bf16[1,128,8192]{2,1,0:T(8,128)(2,1)S(1)} %copy-done.4, f32[128]{0:T(128)S(1)} %rsqrt_multiply_fusion), kind=kOutput, calls=%fused_computation.5 | convolution fusion | flops 541065216 | bytes 8454656 | tf_op jit(solution)/shard_map/dot_general | solution.py:95
  (105 shorter events, 44.9 us)
Async XLA Ops:
  6.8 9.4 %collective-permute-start.1 = (bf16[4,8192]{1,0:T(4,128)(2,1)S(1)}, bf16[4,8192]{1,0:T(4,128)(2,1)S(1)}, u32[]{:S(2)}, u32[]{:S(2)}) collective-permute-start(bf16[4,8192]{1,0:T(4,128)(2,1)S(1)} %pad_maximum_fusion.1), channel_id=1, source_target_pairs={{32,0},{33,1},{34,2},{35,3},{36,4},{37,5},{38,6},{39,7},{40,8},{41... | collective-permute-start | bytes 196616 | tf_op jit(solution)/shard_map/ppermute | solution.py:32
  13.0 7.2 %collective-permute-start.2 = (bf16[4,8192]{1,0:T(4,128)(2,1)S(1)}, bf16[4,8192]{1,0:T(4,128)(2,1)S(1)}, u32[]{:S(2)}, u32[]{:S(2)}) collective-permute-start(bf16[4,8192]{1,0:T(4,128)(2,1)S(1)} %pad_maximum_fusion.1), channel_id=1, source_target_pairs={{64,0},{65,1},{66,2},{67,3},{68,4},{69,5},{70,6},{71,7},{72,8},{73... | collective-permute-start | bytes 196616 | tf_op jit(solution)/shard_map/ppermute | solution.py:32
  14.0 6.5 %collective-permute-start.3 = (bf16[4,8192]{1,0:T(4,128)(2,1)S(1)}, bf16[4,8192]{1,0:T(4,128)(2,1)S(1)}, u32[]{:S(2)}, u32[]{:S(2)}) collective-permute-start(bf16[4,8192]{1,0:T(4,128)(2,1)S(1)} %pad_maximum_fusion.1), channel_id=1, source_target_pairs={{96,0},{97,1},{98,2},{99,3},{100,4},{101,5},{102,6},{103,7},{104,8... | collective-permute-start | bytes 196616 | tf_op jit(solution)/shard_map/ppermute | solution.py:32
  21.5 9.0 %collective-permute-start.4 = (bf16[16,8192]{1,0:T(8,128)(2,1)S(1)}, bf16[16,8192]{1,0:T(8,128)(2,1)S(1)}, u32[]{:S(2)}, u32[]{:S(2)}) collective-permute-start(bf16[16,8192]{1,0:T(8,128)(2,1)S(1)} %concatenate.18.refs_0_), channel_id=1, source_target_pairs={{8,0},{9,1},{10,2},{11,3},{12,4},{13,5},{14,6},{15,7},{0,8},{1,9},... | collective-permute-start | bytes 786440 | tf_op jit(solution)/shard_map/ppermute | solution.py:32
  24.2 14.3 %collective-permute-start.5 = (bf16[16,8192]{1,0:T(8,128)(2,1)S(1)}, bf16[16,8192]{1,0:T(8,128)(2,1)S(1)}, u32[]{:S(2)}, u32[]{:S(2)}) collective-permute-start(bf16[16,8192]{1,0:T(8,128)(2,1)S(1)} %concatenate.18.refs_0_), channel_id=1, source_target_pairs={{4,0},{5,1},{6,2},{7,3},{8,4},{9,5},{10,6},{11,7},{12,8},{13,9},{1... | collective-permute-start | bytes 786440 | tf_op jit(solution)/shard_map/ppermute | solution.py:32
  25.1 18.1 %collective-permute-start.6 = (bf16[16,8192]{1,0:T(8,128)(2,1)S(1)}, bf16[16,8192]{1,0:T(8,128)(2,1)S(1)}, u32[]{:S(2)}, u32[]{:S(2)}) collective-permute-start(bf16[16,8192]{1,0:T(8,128)(2,1)S(1)} %concatenate.18.refs_0_), channel_id=1, source_target_pairs={{12,0},{13,1},{14,2},{15,3},{0,4},{1,5},{2,6},{3,7},{4,8},{5,9},{6... | collective-permute-start | bytes 786440 | tf_op jit(solution)/shard_map/ppermute | solution.py:32
  25.7 19.7 %collective-permute-start.7 = (bf16[16,8192]{1,0:T(8,128)(2,1)S(1)}, bf16[16,8192]{1,0:T(8,128)(2,1)S(1)}, u32[]{:S(2)}, u32[]{:S(2)}) collective-permute-start(bf16[16,8192]{1,0:T(8,128)(2,1)S(1)} %concatenate.18.refs_0_), channel_id=1, source_target_pairs={{124,0},{125,1},{126,2},{127,3},{112,4},{113,5},{114,6},{115,7},{1... | collective-permute-start | bytes 786440 | tf_op jit(solution)/shard_map/ppermute | solution.py:32
  26.4 19.0 %collective-permute-start.8 = (bf16[16,8192]{1,0:T(8,128)(2,1)S(1)}, bf16[16,8192]{1,0:T(8,128)(2,1)S(1)}, u32[]{:S(2)}, u32[]{:S(2)}) collective-permute-start(bf16[16,8192]{1,0:T(8,128)(2,1)S(1)} %concatenate.18.refs_0_), channel_id=1, source_target_pairs={{20,0},{21,1},{22,2},{23,3},{24,4},{25,5},{26,6},{27,7},{28,8},{29... | collective-permute-start | bytes 786440 | tf_op jit(solution)/shard_map/ppermute | solution.py:32
  30.5 15.0 %collective-permute-start.9 = (bf16[16,8192]{1,0:T(8,128)(2,1)S(1)}, bf16[16,8192]{1,0:T(8,128)(2,1)S(1)}, u32[]{:S(2)}, u32[]{:S(2)}) collective-permute-start(bf16[16,8192]{1,0:T(8,128)(2,1)S(1)} %concatenate.18.refs_0_), channel_id=1, source_target_pairs={{112,0},{113,1},{114,2},{115,3},{116,4},{117,5},{118,6},{119,7},{1... | collective-permute-start | bytes 786440 | tf_op jit(solution)/shard_map/ppermute | solution.py:32
  38.5 8.5 %collective-permute-start.10 = (bf16[16,8192]{1,0:T(8,128)(2,1)S(1)}, bf16[16,8192]{1,0:T(8,128)(2,1)S(1)}, u32[]{:S(2)}, u32[]{:S(2)}) collective-permute-start(bf16[16,8192]{1,0:T(8,128)(2,1)S(1)} %collective-permute-done.4.refs_1_), channel_id=1, source_target_pairs={{16,0},{17,1},{18,2},{19,3},{20,4},{21,5},{22,6},{23,7},{24,8},{25... | collective-permute-start | bytes 786440 | tf_op jit(solution)/shard_map/ppermute | solution.py:32
  43.3 10.7 %collective-permute-start.11 = (bf16[64,8192]{1,0:T(8,128)(2,1)S(1)}, bf16[64,8192]{1,0:T(8,128)(2,1)}, u32[]{:S(2)}, u32[]{:S(2)}) collective-permute-start(bf16[64,8192]{1,0:T(8,128)(2,1)S(1)} %shard_map.111.refs_0_), channel_id=1, source_target_pairs={{1,0},{0,1},{3,2},{2,3},{5,4},{4,5},{7,6},{6,7},{9,8},{8,9},{11,10... | collective-permute-start | bytes 3145736 | tf_op jit(solution)/shard_map/ppermute | solution.py:32
  69.3 9.5 %collective-permute-start.20 = (bf16[16,8192]{1,0:T(8,128)(2,1)S(1)}, bf16[16,8192]{1,0:T(8,128)(2,1)S(1)}, u32[]{:S(2)}, u32[]{:S(2)}) collective-permute-start(bf16[16,8192]{1,0:T(8,128)(2,1)S(1)} %get-tuple-element.9), channel_id=1, source_target_pairs={{112,0},{113,1},{114,2},{115,3},{116,4},{117,5},{118,6},{119,7},{1... | collective-permute-start | bytes 786440 | tf_op jit(solution)/shard_map/ppermute | solution.py:32
  70.2 9.8 %collective-permute-start.15 = (bf16[16,8192]{1,0:T(8,128)(2,1)S(1)}, bf16[16,8192]{1,0:T(8,128)(2,1)S(1)}, u32[]{:S(2)}, u32[]{:S(2)}) collective-permute-start(bf16[16,8192]{1,0:T(8,128)(2,1)S(1)} %get-tuple-element.8), channel_id=1, source_target_pairs={{12,0},{13,1},{14,2},{15,3},{0,4},{1,5},{2,6},{3,7},{4,8},{5,9},{6... | collective-permute-start | bytes 786440 | tf_op jit(solution)/shard_map/ppermute | solution.py:32
  72.3 12.5 %collective-permute-start.16 = (bf16[16,8192]{1,0:T(8,128)(2,1)S(1)}, bf16[16,8192]{1,0:T(8,128)(2,1)S(1)}, u32[]{:S(2)}, u32[]{:S(2)}) collective-permute-start(bf16[16,8192]{1,0:T(8,128)(2,1)S(1)} %get-tuple-element.13), channel_id=1, source_target_pairs={{4,0},{5,1},{6,2},{7,3},{8,4},{9,5},{10,6},{11,7},{12,8},{13,9},{1... | collective-permute-start | bytes 786440 | tf_op jit(solution)/shard_map/ppermute | solution.py:32
  73.6 11.2 %collective-permute-start.17 = (bf16[16,8192]{1,0:T(8,128)(2,1)S(1)}, bf16[16,8192]{1,0:T(8,128)(2,1)S(1)}, u32[]{:S(2)}, u32[]{:S(2)}) collective-permute-start(bf16[16,8192]{1,0:T(8,128)(2,1)S(1)} %get-tuple-element.12), channel_id=1, source_target_pairs={{20,0},{21,1},{22,2},{23,3},{24,4},{25,5},{26,6},{27,7},{28,8},{29... | collective-permute-start | bytes 786440 | tf_op jit(solution)/shard_map/ppermute | solution.py:32
  77.1 9.9 %collective-permute-start.18 = (bf16[16,8192]{1,0:T(8,128)(2,1)S(1)}, bf16[16,8192]{1,0:T(8,128)(2,1)S(1)}, u32[]{:S(2)}, u32[]{:S(2)}) collective-permute-start(bf16[16,8192]{1,0:T(8,128)(2,1)S(1)} %get-tuple-element.11), channel_id=1, source_target_pairs={{124,0},{125,1},{126,2},{127,3},{112,4},{113,5},{114,6},{115,7},{1... | collective-permute-start | bytes 786440 | tf_op jit(solution)/shard_map/ppermute | solution.py:32
  78.8 8.6 %collective-permute-start.19 = (bf16[16,8192]{1,0:T(8,128)(2,1)S(1)}, bf16[16,8192]{1,0:T(8,128)(2,1)S(1)}, u32[]{:S(2)}, u32[]{:S(2)}) collective-permute-start(bf16[16,8192]{1,0:T(8,128)(2,1)S(1)} %get-tuple-element.10), channel_id=1, source_target_pairs={{16,0},{17,1},{18,2},{19,3},{20,4},{21,5},{22,6},{23,7},{24,8},{25... | collective-permute-start | bytes 786440 | tf_op jit(solution)/shard_map/ppermute | solution.py:32
  80.0 14.2 %collective-permute-start.21 = (bf16[16,8192]{1,0:T(8,128)(2,1)S(1)}, bf16[16,8192]{1,0:T(8,128)(2,1)S(1)}, u32[]{:S(2)}, u32[]{:S(2)}) collective-permute-start(bf16[16,8192]{1,0:T(8,128)(2,1)S(1)} %fusion.13), channel_id=1, source_target_pairs={{8,0},{9,1},{10,2},{11,3},{12,4},{13,5},{14,6},{15,7},{0,8},{1,9},... | collective-permute-start | bytes 786440 | tf_op jit(solution)/shard_map/ppermute | solution.py:32
  94.5 6.6 %collective-permute-start.22 = (bf16[4,8192]{1,0:T(4,128)(2,1)S(1)}, bf16[4,8192]{1,0:T(4,128)(2,1)S(1)}, u32[]{:S(2)}, u32[]{:S(2)}) collective-permute-start(bf16[4,8192]{1,0:T(4,128)(2,1)S(1)} %get-tuple-element.14), channel_id=1, source_target_pairs={{96,0},{97,1},{98,2},{99,3},{100,4},{101,5},{102,6},{103,7},{104,8... | collective-permute-start | bytes 196616 | tf_op jit(solution)/shard_map/ppermute | solution.py:32
  94.6 7.4 %collective-permute-start.23 = (bf16[4,8192]{1,0:T(4,128)(2,1)S(1)}, bf16[4,8192]{1,0:T(4,128)(2,1)S(1)}, u32[]{:S(2)}, u32[]{:S(2)}) collective-permute-start(bf16[4,8192]{1,0:T(4,128)(2,1)S(1)} %get-tuple-element.16), channel_id=1, source_target_pairs={{64,0},{65,1},{66,2},{67,3},{68,4},{69,5},{70,6},{71,7},{72,8},{73... | collective-permute-start | bytes 196616 | tf_op jit(solution)/shard_map/ppermute | solution.py:32
  97.1 6.4 %collective-permute-start.24 = (bf16[4,8192]{1,0:T(4,128)(2,1)S(1)}, bf16[4,8192]{1,0:T(4,128)(2,1)S(1)}, u32[]{:S(2)}, u32[]{:S(2)}) collective-permute-start(bf16[4,8192]{1,0:T(4,128)(2,1)S(1)} %get-tuple-element.15), channel_id=1, source_target_pairs={{32,0},{33,1},{34,2},{35,3},{36,4},{37,5},{38,6},{39,7},{40,8},{41... | collective-permute-start | bytes 196616 | tf_op jit(solution)/shard_map/ppermute | solution.py:32
  112.8 6.8 %collective-permute-start.27 = (bf16[4,8192]{1,0:T(4,128)(2,1)S(1)}, bf16[4,8192]{1,0:T(4,128)(2,1)S(1)}, u32[]{:S(2)}, u32[]{:S(2)}) collective-permute-start(bf16[4,8192]{1,0:T(4,128)(2,1)S(1)} %pad_maximum_fusion.2), channel_id=1, source_target_pairs={{32,0},{33,1},{34,2},{35,3},{36,4},{37,5},{38,6},{39,7},{40,8},{41... | collective-permute-start | bytes 196616 | tf_op jit(solution)/shard_map/ppermute | solution.py:32
  117.2 7.2 %collective-permute-start.28 = (bf16[4,8192]{1,0:T(4,128)(2,1)S(1)}, bf16[4,8192]{1,0:T(4,128)(2,1)S(1)}, u32[]{:S(2)}, u32[]{:S(2)}) collective-permute-start(bf16[4,8192]{1,0:T(4,128)(2,1)S(1)} %pad_maximum_fusion.2), channel_id=1, source_target_pairs={{64,0},{65,1},{66,2},{67,3},{68,4},{69,5},{70,6},{71,7},{72,8},{73... | collective-permute-start | bytes 196616 | tf_op jit(solution)/shard_map/ppermute | solution.py:32
  124.6 10.9 %collective-permute-start.30 = (bf16[16,8192]{1,0:T(8,128)(2,1)S(1)}, bf16[16,8192]{1,0:T(8,128)(2,1)S(1)}, u32[]{:S(2)}, u32[]{:S(2)}) collective-permute-start(bf16[16,8192]{1,0:T(8,128)(2,1)S(1)} %concatenate.21.refs_0_), channel_id=1, source_target_pairs={{8,0},{9,1},{10,2},{11,3},{12,4},{13,5},{14,6},{15,7},{0,8},{1,9},... | collective-permute-start | bytes 786440 | tf_op jit(solution)/shard_map/ppermute | solution.py:32
  129.2 8.6 %collective-permute-start.31 = (bf16[16,8192]{1,0:T(8,128)(2,1)S(1)}, bf16[16,8192]{1,0:T(8,128)(2,1)S(1)}, u32[]{:S(2)}, u32[]{:S(2)}) collective-permute-start(bf16[16,8192]{1,0:T(8,128)(2,1)S(1)} %concatenate.21.refs_0_), channel_id=1, source_target_pairs={{4,0},{5,1},{6,2},{7,3},{8,4},{9,5},{10,6},{11,7},{12,8},{13,9},{1... | collective-permute-start | bytes 786440 | tf_op jit(solution)/shard_map/ppermute | solution.py:32
  129.2 10.9 %collective-permute-start.32 = (bf16[16,8192]{1,0:T(8,128)(2,1)S(1)}, bf16[16,8192]{1,0:T(8,128)(2,1)S(1)}, u32[]{:S(2)}, u32[]{:S(2)}) collective-permute-start(bf16[16,8192]{1,0:T(8,128)(2,1)S(1)} %concatenate.21.refs_0_), channel_id=1, source_target_pairs={{12,0},{13,1},{14,2},{15,3},{0,4},{1,5},{2,6},{3,7},{4,8},{5,9},{6... | collective-permute-start | bytes 786440 | tf_op jit(solution)/shard_map/ppermute | solution.py:32
  130.7 17.5 %collective-permute-start.33 = (bf16[16,8192]{1,0:T(8,128)(2,1)S(1)}, bf16[16,8192]{1,0:T(8,128)(2,1)S(1)}, u32[]{:S(2)}, u32[]{:S(2)}) collective-permute-start(bf16[16,8192]{1,0:T(8,128)(2,1)S(1)} %concatenate.21.refs_0_), channel_id=1, source_target_pairs={{124,0},{125,1},{126,2},{127,3},{112,4},{113,5},{114,6},{115,7},{1... | collective-permute-start | bytes 786440 | tf_op jit(solution)/shard_map/ppermute | solution.py:32
  130.7 17.5 %collective-permute-start.34 = (bf16[16,8192]{1,0:T(8,128)(2,1)S(1)}, bf16[16,8192]{1,0:T(8,128)(2,1)S(1)}, u32[]{:S(2)}, u32[]{:S(2)}) collective-permute-start(bf16[16,8192]{1,0:T(8,128)(2,1)S(1)} %concatenate.21.refs_0_), channel_id=1, source_target_pairs={{20,0},{21,1},{22,2},{23,3},{24,4},{25,5},{26,6},{27,7},{28,8},{29... | collective-permute-start | bytes 786440 | tf_op jit(solution)/shard_map/ppermute | solution.py:32
  135.5 12.7 %collective-permute-start.35 = (bf16[16,8192]{1,0:T(8,128)(2,1)S(1)}, bf16[16,8192]{1,0:T(8,128)(2,1)S(1)}, u32[]{:S(2)}, u32[]{:S(2)}) collective-permute-start(bf16[16,8192]{1,0:T(8,128)(2,1)S(1)} %concatenate.21.refs_0_), channel_id=1, source_target_pairs={{112,0},{113,1},{114,2},{115,3},{116,4},{117,5},{118,6},{119,7},{1... | collective-permute-start | bytes 786440 | tf_op jit(solution)/shard_map/ppermute | solution.py:32
  137.8 10.4 %collective-permute-start.36 = (bf16[16,8192]{1,0:T(8,128)(2,1)S(1)}, bf16[16,8192]{1,0:T(8,128)(2,1)S(1)}, u32[]{:S(2)}, u32[]{:S(2)}) collective-permute-start(bf16[16,8192]{1,0:T(8,128)(2,1)S(1)} %collective-permute-done.30.refs_1_), channel_id=1, source_target_pairs={{16,0},{17,1},{18,2},{19,3},{20,4},{21,5},{22,6},{23,7},{24,8},{25... | collective-permute-start | bytes 786440 | tf_op jit(solution)/shard_map/ppermute | solution.py:32
  140.2 12.8 %collective-permute-start.37 = (bf16[64,8192]{1,0:T(8,128)(2,1)S(1)}, bf16[64,8192]{1,0:T(8,128)(2,1)S(1)}, u32[]{:S(2)}, u32[]{:S(2)}) collective-permute-start(bf16[64,8192]{1,0:T(8,128)(2,1)S(1)} %shard_map.114.refs_0_), channel_id=1, source_target_pairs={{1,0},{0,1},{3,2},{2,3},{5,4},{4,5},{7,6},{6,7},{9,8},{8,9},{11,10... | collective-permute-start | bytes 3145736 | tf_op jit(solution)/shard_map/ppermute | solution.py:32
  148.3 6.9 %collective-permute-start.38 = (bf16[64,8192]{1,0:T(8,128)(2,1)S(1)}, bf16[64,8192]{1,0:T(8,128)(2,1)S(1)}, u32[]{:S(2)}, u32[]{:S(2)}) collective-permute-start(bf16[64,8192]{1,0:T(8,128)(2,1)S(1)} %shard_map.115.refs_1_), channel_id=1, source_target_pairs={{1,0},{0,1},{3,2},{2,3},{5,4},{4,5},{7,6},{6,7},{9,8},{8,9},{11,10... | collective-permute-start | bytes 3145736 | tf_op jit(solution)/shard_map/ppermute | solution.py:32
  (18 other events, 257.2 us)
where the time goes:
time: 167 us
  starting transfers between devices  89.8 us (54%)
  waiting for transfers between devices  56.2 us (34%)
  matrix products  9.86 us (6%)
  other arithmetic  4.33 us (3%)
  Pallas kernels  3.64 us (2%)
    ppermute x38, starting transfers between devices, fetch(): return lax.ppermute(value, 'lat', pairs)  86.9 us
    ppermute x38, waiting for transfers between devices, fetch(): return lax.ppermute(value, 'lat', pairs)  50.5 us
    dot_general x7, matrix products, dot(): lax.dot_general(left, right, ((over[:1], over[1:]), ((), ())), preferred_...  9.86 us
    ppermute x2, waiting for transfers between devices, swap_pair(): return lax.ppermute(value, 'pair', [(0, 1), (1, 0)])  5.74 us
    pallas_call x6, Pallas kernels, pack(): pl.pallas_call(kernel, out_shape=jax.ShapeDtypeStruct((sum(rows), pieces[...  3.64 us
  transfers between devices with their start and end apart: 40, of which 22 were waited for; matrix products, arithmetic and copies ran while one was open for 2% of the time, Pallas kernels for 1%

commit v1 on v0

v1 whole, which is shorter than its diff:
```python
import jax
import jax.numpy as jnp
import numpy as np
from jax import lax
from jax.experimental import pallas as pl
from jax.experimental.pallas import tpu as pltpu
from jax.sharding import PartitionSpec as P

BLK = 128
NZ, NX, NY, NC = 8, 4, 2, 2

epsilon = 1e-06
sparsity = 0.25
loss_scale = 0.0625

ROW_BLOCK = np.arange(2 * BLK) % 8 // 4


def place(z, x, y, c):
    return (((z % NZ) * NX + x % NX) * NY + y % NY) * NC + c % NC


def fetch(value, z=0, x=0, y=0, c=0, mirror=False):
    pairs = []
    for iz in range(NZ):
        for ix in range(NX):
            for iy in range(NY):
                for ic in range(NC):
                    sign = -1 if mirror and ic == 1 else 1
                    pairs.append((place(iz + sign * z, ix + sign * x, iy + y, ic + c), place(iz, ix, iy, ic)))
    return lax.ppermute(value, "lat", pairs)


def pack(pieces):
    rows = [piece.shape[0] for piece in pieces]

    def kernel(*refs):
        at = 0
        for ref, count in zip(refs[:-1], rows):
            refs[-1][at : at + count, :] = ref[...]
            at += count

    return pl.pallas_call(
        kernel,
        out_shape=jax.ShapeDtypeStruct((sum(rows), pieces[0].shape[1]), pieces[0].dtype),
        in_specs=[pl.BlockSpec(memory_space=pltpu.VMEM)] * len(pieces),
        out_specs=pl.BlockSpec(memory_space=pltpu.VMEM),
        compiler_params=pltpu.CompilerParams(vmem_limit_bytes=32 * 1024 * 1024),
    )(*pieces)


def by_z(value):
    near = [value] + [fetch(value, z=k) for k in (2, 4, 6)]
    turn = lax.axis_index("lat") // (2 * NX * NY * NC)
    return [lax.select_n(turn, *[near[(k - first) % 4] for first in range(4)]) for k in range(4)]


AROUND = (dict(x=1), dict(z=1), dict(x=1, z=1))
BACK = (dict(x=-1), dict(z=-1), dict(x=-1, z=-1))


def gather_rows(octet):
    group = pack([octet, fetch(octet, y=1), fetch(octet, x=2), fetch(octet, x=2, y=1)])
    groups = [group] + [fetch(group, mirror=True, **to) for to in AROUND]
    return groups + [fetch(each, c=1) for each in groups]


def low(value):
    return value.astype(jnp.bfloat16)


def add(value, arrived):
    return value + arrived.astype(jnp.float32)


def scatter_rows(latent, dec):
    rows = latent.shape[0] // 2
    theirs = low(dot(latent[rows:], dec, (1, 0)))
    mine = dot(latent[:rows], dec, (1, 0))
    groups = [add(mine[at : at + 32], fetch(theirs[at : at + 32], c=1)) for at in (96, 64, 32, 0)][::-1]
    group = groups[0]
    for each, to in zip(groups[:0:-1], BACK[::-1]):
        group = add(group, fetch(low(each), mirror=True, **to))
    octet = add(group[0:8], fetch(low(group[8:16]), y=1))
    octet = add(octet, fetch(low(group[16:24]), x=2))
    octet = add(octet, fetch(low(group[24:32]), x=2, y=1))
    parts = [part.astype(jnp.float32) for part in by_z(low(octet))]
    return parts[0] + parts[1] + parts[2] + parts[3]


def swap_pair(value):
    return lax.ppermute(value, "pair", [(0, 1), (1, 0)])


def dot(left, right, over):
    return lax.dot_general(left, right, ((over[:1], over[1:]), ((), ())), preferred_element_type=jnp.float32)


def on_device(activations, enc_weight, enc_bias, dec_weight, dec_bias, block_list, block_count):
    enc, dec = enc_weight[0], dec_weight[0]
    own = activations[0]
    tokens = 2 * BLK
    norm_own = jnp.sqrt(jnp.sum(jnp.square(dec.astype(jnp.float32)), axis=1) + epsilon)
    own_octet = jnp.concatenate(by_z(own), axis=0)
    act_groups = gather_rows(own_octet)

    slots = jnp.arange(block_list.shape[0], dtype=jnp.int32) < block_count[0]
    live = jnp.any((ROW_BLOCK[:, None] == block_list[None, :]) & slots[None, :], axis=1)
    live = live.astype(jnp.float32)[:, None]

    act_halves = [pack(act_groups[:4]), pack(act_groups[4:])]
    pre_part = [dot(half, enc, (1, 1)) for half in act_halves]
    packed = jnp.concatenate(pre_part + [jnp.broadcast_to(norm_own[None, :], (8, norm_own.shape[0]))], axis=0)
    arrived, act = lax.optimization_barrier((swap_pair(packed), pack(act_halves)))
    packed = packed + arrived
    norm_sum = packed[tokens : tokens + 1]
    pre_act = packed[:tokens] + enc_bias[None, :]
    latent_act = jax.nn.softplus(pre_act) * live
    latent_low = low(latent_act)

    rebuilt = scatter_rows(latent_low, dec) + dec_bias
    err_groups = gather_rows(low(loss_scale * (rebuilt - own_octet.astype(jnp.float32))))

    err_halves = [pack(err_groups[:4]), pack(err_groups[4:])]
    grad_part = jnp.concatenate([dot(half, dec, (1, 1)) for half in err_halves], axis=0)
    err = pack(err_halves)
    act_total = jnp.sum(latent_act, axis=0)
    d_dec = dot(latent_low, err, (0, 0))
    d_dec = d_dec + (loss_scale * sparsity * act_total / norm_own)[:, None] * dec.astype(jnp.float32)
    d_dec_bias = dot(jnp.ones((8, tokens), jnp.bfloat16), err, (1, 0))[0:1]
    arrived, d_dec, d_dec_bias = lax.optimization_barrier((swap_pair(grad_part), low(d_dec), d_dec_bias))
    grad_sum = grad_part + arrived
    grad_latent = (grad_sum + loss_scale * sparsity * norm_sum) * live
    pre_grad = grad_latent * jax.nn.sigmoid(pre_act)
    pre_low = low(pre_grad)

    d_enc = dot(pre_low, act, (0, 0))
    d_enc_bias = jnp.sum(pre_grad, axis=0)
    return low(d_enc)[None], d_dec[None], d_enc_bias, d_dec_bias


def solution(mesh):
    placed = (
        P("pair", "lat", None),
        P("pair", "lat", None),
        P("lat"),
        P("pair", "lat", None),
        P("pair", None),
        P("lat"),
        P("lat"),
    )
    return jax.shard_map(
        on_device,
        mesh=mesh,
        in_specs=placed,
        out_specs=(P("pair", "lat", None), P("pair", "lat", None), P("lat"), P("pair", None)),
        check_vma=False,
    )
```

time: 167 us -> 146 us (0.87)
  starting transfers between devices: 89.8 us -> 75.6 us
  waiting for transfers between devices: 56.2 us -> 51.1 us
  Pallas kernels: 3.64 us -> 1.16 us
    ppermute x38 -> x36, starting transfers between devices: 86.9 us -> 74.5 us  [fetch(): return lax.ppermute(value, 'lat', pairs)]
    ppermute x38 -> x36, waiting for transfers between devices: 50.5 us -> 46.7 us  [fetch(): return lax.ppermute(value, 'lat', pairs)]
    pallas_call x6 -> x8, Pallas kernels: 3.64 us -> 1.16 us  [pack(): pl.pallas_call(kernel, out_shape=jax.ShapeDtypeStruct((sum(rows), pieces[...]
    ppermute x2, starting transfers between devices: 2.94 us -> 1.14 us  [swap_pair(): return lax.ppermute(value, 'pair', [(0, 1), (1, 0)])]
    dot_general x7 -> x9, matrix products: 9.86 us -> 10.2 us  [dot(): lax.dot_general(left, right, ((over[:1], over[1:]), ((), ())), preferred_...]
  transfers between devices with their start and end apart: 40 -> 38, of which waited for: 22 -> 27; matrix products, arithmetic and copies ran while one was open for 2% -> 6% of each run, Pallas kernels for 1% -> 0%
where the time goes in v1:
time: 146 us; the launch traced here: 145 us
  starting transfers between devices  75.6 us (52%)
  waiting for transfers between devices  51.1 us (35%)
  matrix products  10.2 us (7%)
  other arithmetic  5.04 us (3%)
  between operations  1.57 us (1%)
    ppermute x36, starting transfers between devices, fetch(): return lax.ppermute(value, 'lat', pairs)  74.5 us
    ppermute x36, waiting for transfers between devices, fetch(): return lax.ppermute(value, 'lat', pairs)  46.7 us
    dot_general x9, matrix products, dot(): lax.dot_general(left, right, ((over[:1], over[1:]), ((), ())), preferred_...  10.2 us
    ppermute x2, waiting for transfers between devices, swap_pair(): return lax.ppermute(value, 'pair', [(0, 1), (1, 0)])  4.41 us
  transfers between devices with their start and end apart: 38, of which 27 were waited for; matrix products, arithmetic and copies ran while one was open for 6% of the time, Pallas kernels for 0%

profile of v1, /device:TPU:1, one launch (start us, length us, event | category | flops | bytes accessed | tf_op | source)
XLA Modules:
  0.0 144.9 jit_solution(6411270758121875154)
XLA Ops:
  0.6 7.8 %collective-permute-start.1 = (bf16[2,8192]{1,0:T(2,128)(2,1)}, bf16[2,8192]{1,0:T(2,128)(2,1)S(1)}, u32[]{:S(2)}, u32[]{:S(2)}) collective-permute-start(bf16[2,8192]{1,0:T(2,128)(2,1)} %bitcast.40), channel_id=1, source_target_pairs={{64,0},{65,1},{66,2},{67,3},{68,4},{69,5},{70,6},{71,7},{72,8},{73... | collective-permute-start | bytes 98312 | tf_op jit(solution)/shard_map/ppermute | solution.py:31
  8.5 2.4 %collective-permute-start = (bf16[2,8192]{1,0:T(2,128)(2,1)}, bf16[2,8192]{1,0:T(2,128)(2,1)S(1)}, u32[]{:S(2)}, u32[]{:S(2)}) collective-permute-start(bf16[2,8192]{1,0:T(2,128)(2,1)} %bitcast.42), channel_id=1, source_target_pairs={{96,0},{97,1},{98,2},{99,3},{100,4},{101,5},{102,6},{103,7},{104,8... | collective-permute-start | bytes 98312 | tf_op jit(solution)/shard_map/ppermute | solution.py:31
  14.7 5.5 %collective-permute-start.5 = (bf16[8,8192]{1,0:T(8,128)(2,1)S(1)}, bf16[8,8192]{1,0:T(8,128)(2,1)S(1)}, u32[]{:S(2)}, u32[]{:S(2)}) collective-permute-start(bf16[8,8192]{1,0:T(8,128)(2,1)S(1)} %pad_maximum_fusion.1.refs_0_), channel_id=1, source_target_pairs={{10,0},{11,1},{8,2},{9,3},{14,4},{15,5},{12,6},{13,7},{2,8},{3,9},... | collective-permute-start | bytes 393224 | tf_op jit(solution)/shard_map/ppermute | solution.py:31
  20.6 2.0 %collective-permute-done.5.refs_3_ = bf16[8,8192]{1,0:T(8,128)(2,1)S(1)} collective-permute-done((bf16[8,8192]{1,0:T(8,128)(2,1)S(1)}, bf16[8,8192]{1,0:T(8,128)(2,1)S(1)}, u32[]{:S(2)}, u32[]{:S(2)}) %collective-permute-start.5) | collective-permute-done | bytes 131104 | tf_op jit(solution)/shard_map/ppermute | solution.py:31
  22.6 4.2 %collective-permute-done.4.refs_2_ = bf16[8,8192]{1,0:T(8,128)(2,1)S(1)} collective-permute-done((bf16[8,8192]{1,0:T(8,128)(2,1)S(1)}, bf16[8,8192]{1,0:T(8,128)(2,1)S(1)}, u32[]{:S(2)}, u32[]{:S(2)}) %collective-permute-start.4) | collective-permute-done | bytes 131104 | tf_op jit(solution)/shard_map/ppermute | solution.py:31
  26.8 2.4 %collective-permute-start.8 = (bf16[32,8192]{1,0:T(8,128)(2,1)S(1)}, bf16[32,8192]{1,0:T(8,128)(2,1)S(1)}, u32[]{:S(2)}, u32[]{:S(2)}) collective-permute-start(bf16[32,8192]{1,0:T(8,128)(2,1)S(1)} %shard_map.111.refs_0_), channel_id=1, source_target_pairs={{20,0},{125,1},{22,2},{127,3},{24,4},{113,5},{26,6},{115,7},{28,8}... | collective-permute-start | bytes 1572872 | tf_op jit(solution)/shard_map/ppermute | solution.py:31
  31.1 2.1 %fusion.2 = f32[128]{0:T(128)S(1)} fusion(bf16[1,128,8192]{2,1,0:T(8,128)(2,1)} %param.11), kind=kLoop, calls=%fused_computation.7 | loop fusion | flops 3145600 | bytes 2097664 | tf_op jit(solution)/shard_map/reduce_sum | solution.py:103
  33.2 4.3 %collective-permute-start.9 = (bf16[32,8192]{1,0:T(8,128)(2,1)S(1)}, bf16[32,8192]{1,0:T(8,128)(2,1)S(1)}, u32[]{:S(2)}, u32[]{:S(2)}) collective-permute-start(bf16[32,8192]{1,0:T(8,128)(2,1)S(1)} %shard_map.111.refs_0_), channel_id=1, source_target_pairs={{1,0},{0,1},{3,2},{2,3},{5,4},{4,5},{7,6},{6,7},{9,8},{8,9},{11,10... | collective-permute-start | bytes 1572872 | tf_op jit(solution)/shard_map/ppermute | solution.py:31
  38.3 1.9 %collective-permute-start.12 = (bf16[32,8192]{1,0:T(8,128)(2,1)S(1)}, bf16[32,8192]{1,0:T(8,128)(2,1)S(1)}, u32[]{:S(2)}, u32[]{:S(2)}) collective-permute-start(bf16[32,8192]{1,0:T(8,128)(2,1)S(1)} %collective-permute-done.8.refs_3_), channel_id=1, source_target_pairs={{1,0},{0,1},{3,2},{2,3},{5,4},{4,5},{7,6},{6,7},{9,8},{8,9},{11,10... | collective-permute-start | bytes 1572872 | tf_op jit(solution)/shard_map/ppermute | solution.py:31
  40.2 2.6 %collective-permute-done.7.refs_2_ = bf16[32,8192]{1,0:T(8,128)(2,1)S(1)} collective-permute-done((bf16[32,8192]{1,0:T(8,128)(2,1)S(1)}, bf16[32,8192]{1,0:T(8,128)(2,1)S(1)}, u32[]{:S(2)}, u32[]{:S(2)}) %collective-permute-start.7) | collective-permute-done | bytes 524320 | tf_op jit(solution)/shard_map/ppermute | solution.py:31
  42.8 4.0 %collective-permute-start.11 = (bf16[32,8192]{1,0:T(8,128)(2,1)S(1)}, bf16[32,8192]{1,0:T(8,128)(2,1)S(1)}, u32[]{:S(2)}, u32[]{:S(2)}) collective-permute-start(bf16[32,8192]{1,0:T(8,128)(2,1)S(1)} %collective-permute-done.7.refs_2_), channel_id=1, source_target_pairs={{1,0},{0,1},{3,2},{2,3},{5,4},{4,5},{7,6},{6,7},{9,8},{8,9},{11,10... | collective-permute-start | bytes 1572872 | tf_op jit(solution)/shard_map/ppermute | solution.py:31
  51.0 4.0 %collective-permute-done.13 = f32[264,128]{1,0:T(8,128)S(1)} collective-permute-done((f32[264,128]{1,0:T(8,128)S(1)}, f32[264,128]{1,0:T(8,128)S(1)}, u32[]{:S(2)}, u32[]{:S(2)}) %collective-permute-start.13) | collective-permute-done | bytes 135200 | tf_op jit(solution)/shard_map/ppermute | solution.py:92
  60.7 3.9 %collective-permute-start.16 = (bf16[32,8192]{1,0:T(8,128)(2,1)S(1)}, bf16[32,8192]{1,0:T(8,128)(2,1)S(1)}, u32[]{:S(2)}, u32[]{:S(2)}) collective-permute-start(bf16[32,8192]{1,0:T(8,128)(2,1)S(1)} %get-tuple-element.18), channel_id=1, source_target_pairs={{124,0},{21,1},{126,2},{23,3},{112,4},{25,5},{114,6},{27,7},{116,8... | collective-permute-start | bytes 1572872 | tf_op jit(solution)/shard_map/ppermute | solution.py:31
  65.0 5.8 %collective-permute-done.16 = bf16[32,8192]{1,0:T(8,128)(2,1)S(1)} collective-permute-done((bf16[32,8192]{1,0:T(8,128)(2,1)S(1)}, bf16[32,8192]{1,0:T(8,128)(2,1)S(1)}, u32[]{:S(2)}, u32[]{:S(2)}) %collective-permute-start.16) | collective-permute-done | bytes 524320 | tf_op jit(solution)/shard_map/ppermute | solution.py:31
  70.7 4.9 %collective-permute-done.20 = bf16[32,8192]{1,0:T(8,128)(2,1)S(1)} collective-permute-done((bf16[32,8192]{1,0:T(8,128)(2,1)S(1)}, bf16[32,8192]{1,0:T(8,128)(2,1)S(1)}, u32[]{:S(2)}, u32[]{:S(2)}) %collective-permute-start.20) | collective-permute-done | bytes 524320 | tf_op jit(solution)/shard_map/ppermute | solution.py:31
  77.9 2.3 %collective-permute-start.23 = (bf16[8,8192]{1,0:T(8,128)(2,1)S(1)}, bf16[8,8192]{1,0:T(8,128)(2,1)S(1)}, u32[]{:S(2)}, u32[]{:S(2)}) collective-permute-start(bf16[8,8192]{1,0:T(8,128)(2,1)S(1)} %get-tuple-element.26), channel_id=1, source_target_pairs={{10,0},{11,1},{8,2},{9,3},{14,4},{15,5},{12,6},{13,7},{2,8},{3,9},... | collective-permute-start | bytes 393224 | tf_op jit(solution)/shard_map/ppermute | solution.py:31
  80.3 2.2 %collective-permute-start.22 = (bf16[8,8192]{1,0:T(8,128)(2,1)S(1)}, bf16[8,8192]{1,0:T(8,128)(2,1)S(1)}, u32[]{:S(2)}, u32[]{:S(2)}) collective-permute-start(bf16[8,8192]{1,0:T(8,128)(2,1)S(1)} %get-tuple-element.27), channel_id=1, source_target_pairs={{8,0},{9,1},{10,2},{11,3},{12,4},{13,5},{14,6},{15,7},{0,8},{1,9},... | collective-permute-start | bytes 393224 | tf_op jit(solution)/shard_map/ppermute | solution.py:31
  82.4 3.3 %collective-permute-done.23 = bf16[8,8192]{1,0:T(8,128)(2,1)S(1)} collective-permute-done((bf16[8,8192]{1,0:T(8,128)(2,1)S(1)}, bf16[8,8192]{1,0:T(8,128)(2,1)S(1)}, u32[]{:S(2)}, u32[]{:S(2)}) %collective-permute-start.23) | collective-permute-done | bytes 131104 | tf_op jit(solution)/shard_map/ppermute | solution.py:31
  86.3 2.0 %collective-permute-start.26 = (bf16[8,8192]{1,0:T(8,128)(2,1)S(1)}, bf16[8,8192]{1,0:T(8,128)(2,1)S(1)}, u32[]{:S(2)}, u32[]{:S(2)}) collective-permute-start(bf16[8,8192]{1,0:T(8,128)(2,1)S(1)} %fusion.22), channel_id=1, source_target_pairs={{32,0},{33,1},{34,2},{35,3},{36,4},{37,5},{38,6},{39,7},{40,8},{41... | collective-permute-start | bytes 393224 | tf_op jit(solution)/shard_map/ppermute | solution.py:31
  88.4 3.2 %collective-permute-start.25 = (bf16[8,8192]{1,0:T(8,128)(2,1)S(1)}, bf16[8,8192]{1,0:T(8,128)(2,1)S(1)}, u32[]{:S(2)}, u32[]{:S(2)}) collective-permute-start(bf16[8,8192]{1,0:T(8,128)(2,1)S(1)} %fusion.22), channel_id=1, source_target_pairs={{64,0},{65,1},{66,2},{67,3},{68,4},{69,5},{70,6},{71,7},{72,8},{73... | collective-permute-start | bytes 393224 | tf_op jit(solution)/shard_map/ppermute | solution.py:31
  91.5 2.3 %collective-permute-start.24 = (bf16[8,8192]{1,0:T(8,128)(2,1)S(1)}, bf16[8,8192]{1,0:T(8,128)(2,1)S(1)}, u32[]{:S(2)}, u32[]{:S(2)}) collective-permute-start(bf16[8,8192]{1,0:T(8,128)(2,1)S(1)} %fusion.22), channel_id=1, source_target_pairs={{96,0},{97,1},{98,2},{99,3},{100,4},{101,5},{102,6},{103,7},{104,8... | collective-permute-start | bytes 393224 | tf_op jit(solution)/shard_map/ppermute | solution.py:31
  93.8 2.3 %collective-permute-done.25 = bf16[8,8192]{1,0:T(8,128)(2,1)S(1)} collective-permute-done((bf16[8,8192]{1,0:T(8,128)(2,1)S(1)}, bf16[8,8192]{1,0:T(8,128)(2,1)S(1)}, u32[]{:S(2)}, u32[]{:S(2)}) %collective-permute-start.25) | collective-permute-done | bytes 131104 | tf_op jit(solution)/shard_map/ppermute | solution.py:31
  98.0 5.1 %collective-permute-start.29 = (bf16[8,8192]{1,0:T(8,128)(2,1)S(1)}, bf16[8,8192]{1,0:T(8,128)(2,1)S(1)}, u32[]{:S(2)}, u32[]{:S(2)}) collective-permute-start(bf16[8,8192]{1,0:T(8,128)(2,1)S(1)} %multiply_convert_fusion.refs_0_), channel_id=1, source_target_pairs={{10,0},{11,1},{8,2},{9,3},{14,4},{15,5},{12,6},{13,7},{2,8},{3,9},... | collective-permute-start | bytes 393224 | tf_op jit(solution)/shard_map/ppermute | solution.py:31
  103.2 2.2 %collective-permute-start.27 = (bf16[8,8192]{1,0:T(8,128)(2,1)S(1)}, bf16[8,8192]{1,0:T(8,128)(2,1)S(1)}, u32[]{:S(2)}, u32[]{:S(2)}) collective-permute-start(bf16[8,8192]{1,0:T(8,128)(2,1)S(1)} %multiply_convert_fusion.refs_0_), channel_id=1, source_target_pairs={{2,0},{3,1},{0,2},{1,3},{6,4},{7,5},{4,6},{5,7},{10,8},{11,9},{8,1... | collective-permute-start | bytes 393224 | tf_op jit(solution)/shard_map/ppermute | solution.py:31
  105.8 2.6 %collective-permute-done.28.refs_2_ = bf16[8,8192]{1,0:T(8,128)(2,1)S(1)} collective-permute-done((bf16[8,8192]{1,0:T(8,128)(2,1)S(1)}, bf16[8,8192]{1,0:T(8,128)(2,1)S(1)}, u32[]{:S(2)}, u32[]{:S(2)}) %collective-permute-start.28) | collective-permute-done | bytes 131104 | tf_op jit(solution)/shard_map/ppermute | solution.py:31
  108.6 11.8 %collective-permute-start.32 = (bf16[32,8192]{1,0:T(8,128)(2,1)S(1)}, bf16[32,8192]{1,0:T(8,128)(2,1)S(1)}, u32[]{:S(2)}, u32[]{:S(2)}) collective-permute-start(bf16[32,8192]{1,0:T(8,128)(2,1)S(1)} %shard_map.115.refs_0_), channel_id=1, source_target_pairs={{20,0},{125,1},{22,2},{127,3},{24,4},{113,5},{26,6},{115,7},{28,8}... | collective-permute-start | bytes 1572872 | tf_op jit(solution)/shard_map/ppermute | solution.py:31
  120.8 2.0 %collective-permute-start.33 = (bf16[32,8192]{1,0:T(8,128)(2,1)S(1)}, bf16[32,8192]{1,0:T(8,128)(2,1)S(1)}, u32[]{:S(2)}, u32[]{:S(2)}) collective-permute-start(bf16[32,8192]{1,0:T(8,128)(2,1)S(1)} %shard_map.115.refs_0_), channel_id=1, source_target_pairs={{1,0},{0,1},{3,2},{2,3},{5,4},{4,5},{7,6},{6,7},{9,8},{8,9},{11,10... | collective-permute-start | bytes 1572872 | tf_op jit(solution)/shard_map/ppermute | solution.py:31
  122.8 4.2 %collective-permute-done.32.refs_3_ = bf16[32,8192]{1,0:T(8,128)(2,1)S(1)} collective-permute-done((bf16[32,8192]{1,0:T(8,128)(2,1)S(1)}, bf16[32,8192]{1,0:T(8,128)(2,1)S(1)}, u32[]{:S(2)}, u32[]{:S(2)}) %collective-permute-start.32) | collective-permute-done | bytes 524320 | tf_op jit(solution)/shard_map/ppermute | solution.py:31
  128.6 3.5 %collective-permute-done.31.refs_2_ = bf16[32,8192]{1,0:T(8,128)(2,1)S(1)} collective-permute-done((bf16[32,8192]{1,0:T(8,128)(2,1)S(1)}, bf16[32,8192]{1,0:T(8,128)(2,1)S(1)}, u32[]{:S(2)}, u32[]{:S(2)}) %collective-permute-start.31) | collective-permute-done | bytes 524320 | tf_op jit(solution)/shard_map/ppermute | solution.py:31
  132.2 1.8 %collective-permute-start.35 = (bf16[32,8192]{1,0:T(8,128)(2,1)S(1)}, bf16[32,8192]{1,0:T(8,128)(2,1)S(1)}, u32[]{:S(2)}, u32[]{:S(2)}) collective-permute-start(bf16[32,8192]{1,0:T(8,128)(2,1)S(1)} %collective-permute-done.31.refs_2_), channel_id=1, source_target_pairs={{1,0},{0,1},{3,2},{2,3},{5,4},{4,5},{7,6},{6,7},{9,8},{8,9},{11,10... | collective-permute-start | bytes 1572872 | tf_op jit(solution)/shard_map/ppermute | solution.py:31
  137.9 2.6 %fusion = bf16[128,8192]{1,0:T(8,128)(2,1)} fusion(bf16[256,128]{1,0:T(8,128)(2,1)S(1)} %get-tuple-element.29, bf16[256,8192]{1,0:T(8,128)(2,1)S(1)} %shard_map.118, bf16[1,128,8192]{2,1,0:T(8,128)(2,1)S(1)} %copy-done.1, f32[128]{0:T(128)S(1)} %rsqrt_multiply_fusion), kind=kOutput, calls=%fused_computation.1 | convolution fusion | flops 541065216 | bytes 8454656 | tf_op jit(solution)/shard_map/dot_general | solution.py:96
  142.9 2.1 %fusion.1 = bf16[1,128,8192]{2,1,0:T(8,128)(2,1)} fusion(bf16[256,8192]{1,0:T(8,128)(2,1)S(1)} %shard_map.114, bf16[256,128]{1,0:T(8,128)(2,1)S(1)} %get-tuple-element.15), kind=kOutput, calls=%fused_computation.4 | convolution fusion | flops 537919488 | bytes 6356992 | tf_op jit(solution)/shard_map/dot_general | solution.py:96
  (94 shorter events, 30.3 us)
Async XLA Ops:
  0.6 10.2 %collective-permute-start.1 = (bf16[2,8192]{1,0:T(2,128)(2,1)}, bf16[2,8192]{1,0:T(2,128)(2,1)S(1)}, u32[]{:S(2)}, u32[]{:S(2)}) collective-permute-start(bf16[2,8192]{1,0:T(2,128)(2,1)} %bitcast.40), channel_id=1, source_target_pairs={{64,0},{65,1},{66,2},{67,3},{68,4},{69,5},{70,6},{71,7},{72,8},{73... | collective-permute-start | bytes 98312 | tf_op jit(solution)/shard_map/ppermute | solution.py:31
  8.5 3.9 %collective-permute-start.2 = (bf16[2,8192]{1,0:T(2,128)(2,1)}, bf16[2,8192]{1,0:T(2,128)(2,1)S(1)}, u32[]{:S(2)}, u32[]{:S(2)}) collective-permute-start(bf16[2,8192]{1,0:T(2,128)(2,1)} %bitcast.41), channel_id=1, source_target_pairs={{32,0},{33,1},{34,2},{35,3},{36,4},{37,5},{38,6},{39,7},{40,8},{41... | collective-permute-start | bytes 98312 | tf_op jit(solution)/shard_map/ppermute | solution.py:31
  8.5 5.2 %collective-permute-start = (bf16[2,8192]{1,0:T(2,128)(2,1)}, bf16[2,8192]{1,0:T(2,128)(2,1)S(1)}, u32[]{:S(2)}, u32[]{:S(2)}) collective-permute-start(bf16[2,8192]{1,0:T(2,128)(2,1)} %bitcast.42), channel_id=1, source_target_pairs={{96,0},{97,1},{98,2},{99,3},{100,4},{101,5},{102,6},{103,7},{104,8... | collective-permute-start | bytes 98312 | tf_op jit(solution)/shard_map/ppermute | solution.py:31
  14.7 7.8 %collective-permute-start.5 = (bf16[8,8192]{1,0:T(8,128)(2,1)S(1)}, bf16[8,8192]{1,0:T(8,128)(2,1)S(1)}, u32[]{:S(2)}, u32[]{:S(2)}) collective-permute-start(bf16[8,8192]{1,0:T(8,128)(2,1)S(1)} %pad_maximum_fusion.1.refs_0_), channel_id=1, source_target_pairs={{10,0},{11,1},{8,2},{9,3},{14,4},{15,5},{12,6},{13,7},{2,8},{3,9},... | collective-permute-start | bytes 393224 | tf_op jit(solution)/shard_map/ppermute | solution.py:31
  20.2 6.6 %collective-permute-start.4 = (bf16[8,8192]{1,0:T(8,128)(2,1)S(1)}, bf16[8,8192]{1,0:T(8,128)(2,1)S(1)}, u32[]{:S(2)}, u32[]{:S(2)}) collective-permute-start(bf16[8,8192]{1,0:T(8,128)(2,1)S(1)} %pad_maximum_fusion.1.refs_0_), channel_id=1, source_target_pairs={{8,0},{9,1},{10,2},{11,3},{12,4},{13,5},{14,6},{15,7},{0,8},{1,9},... | collective-permute-start | bytes 393224 | tf_op jit(solution)/shard_map/ppermute | solution.py:31
  20.4 6.3 %collective-permute-start.3 = (bf16[8,8192]{1,0:T(8,128)(2,1)S(1)}, bf16[8,8192]{1,0:T(8,128)(2,1)S(1)}, u32[]{:S(2)}, u32[]{:S(2)}) collective-permute-start(bf16[8,8192]{1,0:T(8,128)(2,1)S(1)} %pad_maximum_fusion.1.refs_0_), channel_id=1, source_target_pairs={{2,0},{3,1},{0,2},{1,3},{6,4},{7,5},{4,6},{5,7},{10,8},{11,9},{8,1... | collective-permute-start | bytes 393224 | tf_op jit(solution)/shard_map/ppermute | solution.py:31
  26.8 11.5 %collective-permute-start.8 = (bf16[32,8192]{1,0:T(8,128)(2,1)S(1)}, bf16[32,8192]{1,0:T(8,128)(2,1)S(1)}, u32[]{:S(2)}, u32[]{:S(2)}) collective-permute-start(bf16[32,8192]{1,0:T(8,128)(2,1)S(1)} %shard_map.111.refs_0_), channel_id=1, source_target_pairs={{20,0},{125,1},{22,2},{127,3},{24,4},{113,5},{26,6},{115,7},{28,8}... | collective-permute-start | bytes 1572872 | tf_op jit(solution)/shard_map/ppermute | solution.py:31
  29.2 13.5 %collective-permute-start.7 = (bf16[32,8192]{1,0:T(8,128)(2,1)S(1)}, bf16[32,8192]{1,0:T(8,128)(2,1)S(1)}, u32[]{:S(2)}, u32[]{:S(2)}) collective-permute-start(bf16[32,8192]{1,0:T(8,128)(2,1)S(1)} %shard_map.111.refs_0_), channel_id=1, source_target_pairs={{16,0},{113,1},{18,2},{115,3},{20,4},{117,5},{22,6},{119,7},{24,8}... | collective-permute-start | bytes 1572872 | tf_op jit(solution)/shard_map/ppermute | solution.py:31
  29.4 17.3 %collective-permute-start.6 = (bf16[32,8192]{1,0:T(8,128)(2,1)S(1)}, bf16[32,8192]{1,0:T(8,128)(2,1)S(1)}, u32[]{:S(2)}, u32[]{:S(2)}) collective-permute-start(bf16[32,8192]{1,0:T(8,128)(2,1)S(1)} %shard_map.111.refs_0_), channel_id=1, source_target_pairs={{4,0},{13,1},{6,2},{15,3},{8,4},{1,5},{10,6},{3,7},{12,8},{5,9},{1... | collective-permute-start | bytes 1572872 | tf_op jit(solution)/shard_map/ppermute | solution.py:31
  33.2 14.4 %collective-permute-start.9 = (bf16[32,8192]{1,0:T(8,128)(2,1)S(1)}, bf16[32,8192]{1,0:T(8,128)(2,1)S(1)}, u32[]{:S(2)}, u32[]{:S(2)}) collective-permute-start(bf16[32,8192]{1,0:T(8,128)(2,1)S(1)} %shard_map.111.refs_0_), channel_id=1, source_target_pairs={{1,0},{0,1},{3,2},{2,3},{5,4},{4,5},{7,6},{6,7},{9,8},{8,9},{11,10... | collective-permute-start | bytes 1572872 | tf_op jit(solution)/shard_map/ppermute | solution.py:31
  38.3 9.3 %collective-permute-start.12 = (bf16[32,8192]{1,0:T(8,128)(2,1)S(1)}, bf16[32,8192]{1,0:T(8,128)(2,1)S(1)}, u32[]{:S(2)}, u32[]{:S(2)}) collective-permute-start(bf16[32,8192]{1,0:T(8,128)(2,1)S(1)} %collective-permute-done.8.refs_3_), channel_id=1, source_target_pairs={{1,0},{0,1},{3,2},{2,3},{5,4},{4,5},{7,6},{6,7},{9,8},{8,9},{11,10... | collective-permute-start | bytes 1572872 | tf_op jit(solution)/shard_map/ppermute | solution.py:31
  42.8 5.5 %collective-permute-start.11 = (bf16[32,8192]{1,0:T(8,128)(2,1)S(1)}, bf16[32,8192]{1,0:T(8,128)(2,1)S(1)}, u32[]{:S(2)}, u32[]{:S(2)}) collective-permute-start(bf16[32,8192]{1,0:T(8,128)(2,1)S(1)} %collective-permute-done.7.refs_2_), channel_id=1, source_target_pairs={{1,0},{0,1},{3,2},{2,3},{5,4},{4,5},{7,6},{6,7},{9,8},{8,9},{11,10... | collective-permute-start | bytes 1572872 | tf_op jit(solution)/shard_map/ppermute | solution.py:31
  49.9 5.1 %collective-permute-start.13 = (f32[264,128]{1,0:T(8,128)S(1)}, f32[264,128]{1,0:T(8,128)S(1)}, u32[]{:S(2)}, u32[]{:S(2)}) collective-permute-start(f32[264,128]{1,0:T(8,128)S(1)} %pad_maximum_fusion), channel_id=1, source_target_pairs={{0,128},{128,0},{1,129},{129,1},{2,130},{130,2},{3,131},{131,3},{4... | collective-permute-start | bytes 405512 | tf_op jit(solution)/shard_map/ppermute | solution.py:92
  57.9 7.1 %collective-permute-start.14 = (bf16[32,8192]{1,0:T(8,128)(2,1)S(1)}, bf16[32,8192]{1,0:T(8,128)(2,1)S(1)}, u32[]{:S(2)}, u32[]{:S(2)}) collective-permute-start(bf16[32,8192]{1,0:T(8,128)(2,1)S(1)} %get-tuple-element.21), channel_id=1, source_target_pairs={{1,0},{0,1},{3,2},{2,3},{5,4},{4,5},{7,6},{6,7},{9,8},{8,9},{11,10... | collective-permute-start | bytes 1572872 | tf_op jit(solution)/shard_map/ppermute | solution.py:31
  60.7 10.1 %collective-permute-start.16 = (bf16[32,8192]{1,0:T(8,128)(2,1)S(1)}, bf16[32,8192]{1,0:T(8,128)(2,1)S(1)}, u32[]{:S(2)}, u32[]{:S(2)}) collective-permute-start(bf16[32,8192]{1,0:T(8,128)(2,1)S(1)} %get-tuple-element.18), channel_id=1, source_target_pairs={{124,0},{21,1},{126,2},{23,3},{112,4},{25,5},{114,6},{27,7},{116,8... | collective-permute-start | bytes 1572872 | tf_op jit(solution)/shard_map/ppermute | solution.py:31
  64.6 11.0 %collective-permute-start.20 = (bf16[32,8192]{1,0:T(8,128)(2,1)S(1)}, bf16[32,8192]{1,0:T(8,128)(2,1)S(1)}, u32[]{:S(2)}, u32[]{:S(2)}) collective-permute-start(bf16[32,8192]{1,0:T(8,128)(2,1)S(1)} %get-tuple-element.19), channel_id=1, source_target_pairs={{12,0},{5,1},{14,2},{7,3},{0,4},{9,5},{2,6},{11,7},{4,8},{13,9},{6... | collective-permute-start | bytes 1572872 | tf_op jit(solution)/shard_map/ppermute | solution.py:31
  64.6 11.8 %collective-permute-start.18 = (bf16[32,8192]{1,0:T(8,128)(2,1)S(1)}, bf16[32,8192]{1,0:T(8,128)(2,1)S(1)}, u32[]{:S(2)}, u32[]{:S(2)}) collective-permute-start(bf16[32,8192]{1,0:T(8,128)(2,1)S(1)} %get-tuple-element.20), channel_id=1, source_target_pairs={{112,0},{17,1},{114,2},{19,3},{116,4},{21,5},{118,6},{23,7},{120,8... | collective-permute-start | bytes 1572872 | tf_op jit(solution)/shard_map/ppermute | solution.py:31
  76.7 5.7 %collective-permute-start.21 = (bf16[8,8192]{1,0:T(8,128)(2,1)S(1)}, bf16[8,8192]{1,0:T(8,128)(2,1)S(1)}, u32[]{:S(2)}, u32[]{:S(2)}) collective-permute-start(bf16[8,8192]{1,0:T(8,128)(2,1)S(1)} %get-tuple-element.25), channel_id=1, source_target_pairs={{2,0},{3,1},{0,2},{1,3},{6,4},{7,5},{4,6},{5,7},{10,8},{11,9},{8,1... | collective-permute-start | bytes 393224 | tf_op jit(solution)/shard_map/ppermute | solution.py:31
  77.9 7.8 %collective-permute-start.23 = (bf16[8,8192]{1,0:T(8,128)(2,1)S(1)}, bf16[8,8192]{1,0:T(8,128)(2,1)S(1)}, u32[]{:S(2)}, u32[]{:S(2)}) collective-permute-start(bf16[8,8192]{1,0:T(8,128)(2,1)S(1)} %get-tuple-element.26), channel_id=1, source_target_pairs={{10,0},{11,1},{8,2},{9,3},{14,4},{15,5},{12,6},{13,7},{2,8},{3,9},... | collective-permute-start | bytes 393224 | tf_op jit(solution)/shard_map/ppermute | solution.py:31
  80.3 6.0 %collective-permute-start.22 = (bf16[8,8192]{1,0:T(8,128)(2,1)S(1)}, bf16[8,8192]{1,0:T(8,128)(2,1)S(1)}, u32[]{:S(2)}, u32[]{:S(2)}) collective-permute-start(bf16[8,8192]{1,0:T(8,128)(2,1)S(1)} %get-tuple-element.27), channel_id=1, source_target_pairs={{8,0},{9,1},{10,2},{11,3},{12,4},{13,5},{14,6},{15,7},{0,8},{1,9},... | collective-permute-start | bytes 393224 | tf_op jit(solution)/shard_map/ppermute | solution.py:31
  86.3 7.5 %collective-permute-start.26 = (bf16[8,8192]{1,0:T(8,128)(2,1)S(1)}, bf16[8,8192]{1,0:T(8,128)(2,1)S(1)}, u32[]{:S(2)}, u32[]{:S(2)}) collective-permute-start(bf16[8,8192]{1,0:T(8,128)(2,1)S(1)} %fusion.22), channel_id=1, source_target_pairs={{32,0},{33,1},{34,2},{35,3},{36,4},{37,5},{38,6},{39,7},{40,8},{41... | collective-permute-start | bytes 393224 | tf_op jit(solution)/shard_map/ppermute | solution.py:31
  88.4 7.7 %collective-permute-start.25 = (bf16[8,8192]{1,0:T(8,128)(2,1)S(1)}, bf16[8,8192]{1,0:T(8,128)(2,1)S(1)}, u32[]{:S(2)}, u32[]{:S(2)}) collective-permute-start(bf16[8,8192]{1,0:T(8,128)(2,1)S(1)} %fusion.22), channel_id=1, source_target_pairs={{64,0},{65,1},{66,2},{67,3},{68,4},{69,5},{70,6},{71,7},{72,8},{73... | collective-permute-start | bytes 393224 | tf_op jit(solution)/shard_map/ppermute | solution.py:31
  91.5 6.1 %collective-permute-start.24 = (bf16[8,8192]{1,0:T(8,128)(2,1)S(1)}, bf16[8,8192]{1,0:T(8,128)(2,1)S(1)}, u32[]{:S(2)}, u32[]{:S(2)}) collective-permute-start(bf16[8,8192]{1,0:T(8,128)(2,1)S(1)} %fusion.22), channel_id=1, source_target_pairs={{96,0},{97,1},{98,2},{99,3},{100,4},{101,5},{102,6},{103,7},{104,8... | collective-permute-start | bytes 393224 | tf_op jit(solution)/shard_map/ppermute | solution.py:31
  98.0 7.8 %collective-permute-start.29 = (bf16[8,8192]{1,0:T(8,128)(2,1)S(1)}, bf16[8,8192]{1,0:T(8,128)(2,1)S(1)}, u32[]{:S(2)}, u32[]{:S(2)}) collective-permute-start(bf16[8,8192]{1,0:T(8,128)(2,1)S(1)} %multiply_convert_fusion.refs_0_), channel_id=1, source_target_pairs={{10,0},{11,1},{8,2},{9,3},{14,4},{15,5},{12,6},{13,7},{2,8},{3,9},... | collective-permute-start | bytes 393224 | tf_op jit(solution)/shard_map/ppermute | solution.py:31
  103.1 5.3 %collective-permute-start.28 = (bf16[8,8192]{1,0:T(8,128)(2,1)S(1)}, bf16[8,8192]{1,0:T(8,128)(2,1)S(1)}, u32[]{:S(2)}, u32[]{:S(2)}) collective-permute-start(bf16[8,8192]{1,0:T(8,128)(2,1)S(1)} %multiply_convert_fusion.refs_0_), channel_id=1, source_target_pairs={{8,0},{9,1},{10,2},{11,3},{12,4},{13,5},{14,6},{15,7},{0,8},{1,9},... | collective-permute-start | bytes 393224 | tf_op jit(solution)/shard_map/ppermute | solution.py:31
  103.2 5.3 %collective-permute-start.27 = (bf16[8,8192]{1,0:T(8,128)(2,1)S(1)}, bf16[8,8192]{1,0:T(8,128)(2,1)S(1)}, u32[]{:S(2)}, u32[]{:S(2)}) collective-permute-start(bf16[8,8192]{1,0:T(8,128)(2,1)S(1)} %multiply_convert_fusion.refs_0_), channel_id=1, source_target_pairs={{2,0},{3,1},{0,2},{1,3},{6,4},{7,5},{4,6},{5,7},{10,8},{11,9},{8,1... | collective-permute-start | bytes 393224 | tf_op jit(solution)/shard_map/ppermute | solution.py:31
  108.6 18.3 %collective-permute-start.32 = (bf16[32,8192]{1,0:T(8,128)(2,1)S(1)}, bf16[32,8192]{1,0:T(8,128)(2,1)S(1)}, u32[]{:S(2)}, u32[]{:S(2)}) collective-permute-start(bf16[32,8192]{1,0:T(8,128)(2,1)S(1)} %shard_map.115.refs_0_), channel_id=1, source_target_pairs={{20,0},{125,1},{22,2},{127,3},{24,4},{113,5},{26,6},{115,7},{28,8}... | collective-permute-start | bytes 1572872 | tf_op jit(solution)/shard_map/ppermute | solution.py:31
  120.4 11.8 %collective-permute-start.31 = (bf16[32,8192]{1,0:T(8,128)(2,1)S(1)}, bf16[32,8192]{1,0:T(8,128)(2,1)S(1)}, u32[]{:S(2)}, u32[]{:S(2)}) collective-permute-start(bf16[32,8192]{1,0:T(8,128)(2,1)S(1)} %shard_map.115.refs_0_), channel_id=1, source_target_pairs={{16,0},{113,1},{18,2},{115,3},{20,4},{117,5},{22,6},{119,7},{24,8}... | collective-permute-start | bytes 1572872 | tf_op jit(solution)/shard_map/ppermute | solution.py:31
  120.4 13.6 %collective-permute-start.30 = (bf16[32,8192]{1,0:T(8,128)(2,1)S(1)}, bf16[32,8192]{1,0:T(8,128)(2,1)S(1)}, u32[]{:S(2)}, u32[]{:S(2)}) collective-permute-start(bf16[32,8192]{1,0:T(8,128)(2,1)S(1)} %shard_map.115.refs_0_), channel_id=1, source_target_pairs={{4,0},{13,1},{6,2},{15,3},{8,4},{1,5},{10,6},{3,7},{12,8},{5,9},{1... | collective-permute-start | bytes 1572872 | tf_op jit(solution)/shard_map/ppermute | solution.py:31
  120.8 14.2 %collective-permute-start.33 = (bf16[32,8192]{1,0:T(8,128)(2,1)S(1)}, bf16[32,8192]{1,0:T(8,128)(2,1)S(1)}, u32[]{:S(2)}, u32[]{:S(2)}) collective-permute-start(bf16[32,8192]{1,0:T(8,128)(2,1)S(1)} %shard_map.115.refs_0_), channel_id=1, source_target_pairs={{1,0},{0,1},{3,2},{2,3},{5,4},{4,5},{7,6},{6,7},{9,8},{8,9},{11,10... | collective-permute-start | bytes 1572872 | tf_op jit(solution)/shard_map/ppermute | solution.py:31
  126.9 8.1 %collective-permute-start.36 = (bf16[32,8192]{1,0:T(8,128)(2,1)S(1)}, bf16[32,8192]{1,0:T(8,128)(2,1)S(1)}, u32[]{:S(2)}, u32[]{:S(2)}) collective-permute-start(bf16[32,8192]{1,0:T(8,128)(2,1)S(1)} %collective-permute-done.32.refs_3_), channel_id=1, source_target_pairs={{1,0},{0,1},{3,2},{2,3},{5,4},{4,5},{7,6},{6,7},{9,8},{8,9},{11,10... | collective-permute-start | bytes 1572872 | tf_op jit(solution)/shard_map/ppermute | solution.py:31
  137.4 4.8 %collective-permute-start.37 = (f32[256,128]{1,0:T(8,128)S(1)}, f32[256,128]{1,0:T(8,128)S(1)}, u32[]{:S(2)}, u32[]{:S(2)}) collective-permute-start(f32[256,128]{1,0:T(8,128)S(1)} %pad_maximum_fusion.2), channel_id=1, source_target_pairs={{0,128},{128,0},{1,129},{129,1},{2,130},{130,2},{3,131},{131,3},{4... | collective-permute-start | bytes 393224 | tf_op jit(solution)/shard_map/ppermute | solution.py:92
  (12 other events, 106.9 us)

commit v2 on v1

--- a/solution.py
+++ b/solution.py
@@ -13,22 +13,30 @@
 sparsity = 0.25
 loss_scale = 0.0625
 
-ROW_BLOCK = np.arange(2 * BLK) % 8 // 4
+EVEN_Z = ((0, 0, 0), (2, 0, 0), (6, 0, 0), (4, 0, 0))
+EVEN_XY = ((0, 0, 0), (0, 0, 1), (0, 2, 0), (0, 2, 1))
+TURNS = [[(0, 1, 3, 2)[(i - own) % 4] for i in range(4)] for own in range(4)]
+TURNS += [[i ^ own for i in range(4)] for own in range(4)]
+OCTET_Z = np.array([dz + 2 * k for dz in (0, 0, -1, -1) for k in (0, 1, 3, 2)], np.int32)
 
 
 def place(z, x, y, c):
     return (((z % NZ) * NX + x % NX) * NY + y % NY) * NC + c % NC
 
 
-def fetch(value, z=0, x=0, y=0, c=0, mirror=False):
+def fetch(value, *offsets, c=0):
     pairs = []
     for iz in range(NZ):
         for ix in range(NX):
             for iy in range(NY):
                 for ic in range(NC):
-                    sign = -1 if mirror and ic == 1 else 1
-                    pairs.append((place(iz + sign * z, ix + sign * x, iy + y, ic + c), place(iz, ix, iy, ic)))
+                    z, x, y = offsets[ic % len(offsets)]
+                    pairs.append((place(iz + z, ix + x, iy + y, ic + c), place(iz, ix, iy, ic)))
     return lax.ppermute(value, "lat", pairs)
+
+
+def swap_core(value):
+    return fetch(value, (0, 0, 0), c=1)
 
 
 def pack(pieces):
@@ -49,20 +57,25 @@
     )(*pieces)
 
 
-def by_z(value):
-    near = [value] + [fetch(value, z=k) for k in (2, 4, 6)]
-    turn = lax.axis_index("lat") // (2 * NX * NY * NC)
-    return [lax.select_n(turn, *[near[(k - first) % 4] for first in range(4)]) for k in range(4)]
+def position():
+    at = lax.axis_index("lat")
+    return at // (NX * NY * NC), at // (NY * NC) % NX, at // NC % NY, at % NC
 
 
-AROUND = (dict(x=1), dict(z=1), dict(x=1, z=1))
-BACK = (dict(x=-1), dict(z=-1), dict(x=-1, z=-1))
+def by_partner(value):
+    near = [value] + [fetch(value, EVEN_Z[k], EVEN_XY[k]) for k in (1, 2, 3)]
+    z, x, y, core = position()
+    own = jnp.where(core == 0, z // 2, 4 + x // 2 * 2 + y)
+    return [lax.select_n(own, *[near[turn[i]] for turn in TURNS]) for i in range(4)]
+
+
+AROUND = (((0, 1, 0), (0, -1, 0)), ((1, 0, 0), (-1, 0, 0)), ((1, 1, 0), (-1, -1, 0)))
 
 
 def gather_rows(octet):
-    group = pack([octet, fetch(octet, y=1), fetch(octet, x=2), fetch(octet, x=2, y=1)])
-    groups = [group] + [fetch(group, mirror=True, **to) for to in AROUND]
-    return groups + [fetch(each, c=1) for each in groups]
+    group = pack([octet] + [fetch(octet, EVEN_XY[k], EVEN_Z[k]) for k in (1, 2, 3)])
+    groups = [group] + [fetch(group, *to) for to in AROUND]
+    return groups + [swap_core(each) for each in groups]
 
 
 def low(value):
@@ -77,14 +90,16 @@
     rows = latent.shape[0] // 2
     theirs = low(dot(latent[rows:], dec, (1, 0)))
     mine = dot(latent[:rows], dec, (1, 0))
-    groups = [add(mine[at : at + 32], fetch(theirs[at : at + 32], c=1)) for at in (96, 64, 32, 0)][::-1]
-    group = groups[0]
-    for each, to in zip(groups[:0:-1], BACK[::-1]):
-        group = add(group, fetch(low(each), mirror=True, **to))
-    octet = add(group[0:8], fetch(low(group[8:16]), y=1))
-    octet = add(octet, fetch(low(group[16:24]), x=2))
-    octet = add(octet, fetch(low(group[24:32]), x=2, y=1))
-    parts = [part.astype(jnp.float32) for part in by_z(low(octet))]
+    sent = low(add(mine[96:], swap_core(theirs[96:])))
+    theirs, sent = lax.optimization_barrier((theirs[:96], sent))
+    rest = add(mine[:96], swap_core(theirs))
+    group = add(rest[:32], fetch(sent, *AROUND[2][::-1]))
+    group = add(group, fetch(low(rest[64:]), *AROUND[1][::-1]))
+    group = add(group, fetch(low(rest[32:64]), *AROUND[0][::-1]))
+    octet = group[0:8]
+    for k, back in ((3, 3), (2, 1), (1, 2)):
+        octet = add(octet, fetch(low(group[8 * k : 8 * k + 8]), EVEN_XY[k], EVEN_Z[back]))
+    parts = [part.astype(jnp.float32) for part in by_partner(low(octet))]
     return parts[0] + parts[1] + parts[2] + parts[3]
 
 
@@ -101,18 +116,23 @@
     own = activations[0]
     tokens = 2 * BLK
     norm_own = jnp.sqrt(jnp.sum(jnp.square(dec.astype(jnp.float32)), axis=1) + epsilon)
-    own_octet = jnp.concatenate(by_z(own), axis=0)
+    own_octet = jnp.concatenate(by_partner(own), axis=0)
     act_groups = gather_rows(own_octet)
 
     slots = jnp.arange(block_list.shape[0], dtype=jnp.int32) < block_count[0]
-    live = jnp.any((ROW_BLOCK[:, None] == block_list[None, :]) & slots[None, :], axis=1)
+    z, _, _, core = position()
+    by_octet = jnp.repeat((z + OCTET_Z) % NZ, 8)
+    kinds = [jnp.tile(jnp.arange(NZ, dtype=jnp.int32), tokens // 2 // NZ), by_octet]
+    z_row = jnp.concatenate([jnp.where(core == own, kinds[0], kinds[1]) for own in (0, 1)])
+    block = z_row // (NZ // 2)
+    live = jnp.any((block[:, None] == block_list[None, :]) & slots[None, :], axis=1)
     live = live.astype(jnp.float32)[:, None]
 
     act_halves = [pack(act_groups[:4]), pack(act_groups[4:])]
     pre_part = [dot(half, enc, (1, 1)) for half in act_halves]
     packed = jnp.concatenate(pre_part + [jnp.broadcast_to(norm_own[None, :], (8, norm_own.shape[0]))], axis=0)
-    arrived, act = lax.optimization_barrier((swap_pair(packed), pack(act_halves)))
-    packed = packed + arrived
+    arrived, act = lax.optimization_barrier((swap_pair(low(packed)), pack(act_halves)))
+    packed = add(packed, arrived)
     norm_sum = packed[tokens : tokens + 1]
     pre_act = packed[:tokens] + enc_bias[None, :]
     latent_act = jax.nn.softplus(pre_act) * live
@@ -128,8 +148,8 @@
     d_dec = dot(latent_low, err, (0, 0))
     d_dec = d_dec + (loss_scale * sparsity * act_total / norm_own)[:, None] * dec.astype(jnp.float32)
     d_dec_bias = dot(jnp.ones((8, tokens), jnp.bfloat16), err, (1, 0))[0:1]
-    arrived, d_dec, d_dec_bias = lax.optimization_barrier((swap_pair(grad_part), low(d_dec), d_dec_bias))
-    grad_sum = grad_part + arrived
+    arrived, d_dec, d_dec_bias = lax.optimization_barrier((swap_pair(low(grad_part)), low(d_dec), d_dec_bias))
+    grad_sum = add(grad_part, arrived)
     grad_latent = (grad_sum + loss_scale * sparsity * norm_sum) * live
     pre_grad = grad_latent * jax.nn.sigmoid(pre_act)
     pre_low = low(pre_grad)

time: 146 us -> 138 us (0.945)
  waiting for transfers between devices: 51.1 us -> 42.8 us
    ppermute x36 -> x34, waiting for transfers between devices: 46.7 us -> 40.4 us  [fetch(): return lax.ppermute(value, 'lat', pairs)]
    ppermute x2, waiting for transfers between devices: 4.41 us -> 2.35 us  [swap_pair(): return lax.ppermute(value, 'pair', [(0, 1), (1, 0)])]
    ppermute x36 -> x34, starting transfers between devices: 74.5 us -> 73.5 us  [fetch(): return lax.ppermute(value, 'lat', pairs)]
  transfers between devices with their start and end apart: 38 -> 36, of which waited for: 27 -> 20; matrix products, arithmetic and copies ran while one was open for 6% -> 7% of each run, Pallas kernels for 0% -> 0%
where the time goes in v2:
time: 138 us; the launch traced here: 137 us
  starting transfers between devices  75.1 us (54%)
  waiting for transfers between devices  42.8 us (31%)
  matrix products  10.2 us (7%)
  other arithmetic  6.16 us (4%)
  between operations  1.66 us (1%)
    ppermute x34, starting transfers between devices, fetch(): return lax.ppermute(value, 'lat', pairs)  73.5 us
    ppermute x34, waiting for transfers between devices, fetch(): return lax.ppermute(value, 'lat', pairs)  40.4 us
    dot_general x9, matrix products, dot(): lax.dot_general(left, right, ((over[:1], over[1:]), ((), ())), preferred_...  10.2 us
  transfers between devices with their start and end apart: 36, of which 20 were waited for; matrix products, arithmetic and copies ran while one was open for 7% of the time, Pallas kernels for 0%

profile of v2, /device:TPU:1, one launch (start us, length us, event | category | flops | bytes accessed | tf_op | source)
XLA Modules:
  0.0 137.5 jit_solution(11893099850726129634)
XLA Ops:
  0.6 6.3 %collective-permute-start.1 = (bf16[2,8192]{1,0:T(2,128)(2,1)}, bf16[2,8192]{1,0:T(2,128)(2,1)S(1)}, u32[]{:S(2)}, u32[]{:S(2)}) collective-permute-start(bf16[2,8192]{1,0:T(2,128)(2,1)} %bitcast.40), channel_id=1, source_target_pairs={{64,0},{11,1},{66,2},{9,3},{68,4},{15,5},{70,6},{13,7},{72,8},{3,9... | collective-permute-start | bytes 98312 | tf_op jit(solution)/shard_map/ppermute | solution.py:35
  8.8 2.8 %collective-permute-done.2 = bf16[2,8192]{1,0:T(2,128)(2,1)S(1)} collective-permute-done((bf16[2,8192]{1,0:T(2,128)(2,1)}, bf16[2,8192]{1,0:T(2,128)(2,1)S(1)}, u32[]{:S(2)}, u32[]{:S(2)}) %collective-permute-start.2) | collective-permute-done | bytes 32800 | tf_op jit(solution)/shard_map/ppermute | solution.py:35
  12.8 6.9 %collective-permute-start.5 = (bf16[8,8192]{1,0:T(8,128)(2,1)S(1)}, bf16[8,8192]{1,0:T(8,128)(2,1)S(1)}, u32[]{:S(2)}, u32[]{:S(2)}) collective-permute-start(bf16[8,8192]{1,0:T(8,128)(2,1)S(1)} %pad_maximum_fusion.1.refs_0_), channel_id=1, source_target_pairs={{10,0},{65,1},{8,2},{67,3},{14,4},{69,5},{12,6},{71,7},{2,8},{73,9... | collective-permute-start | bytes 393224 | tf_op jit(solution)/shard_map/ppermute | solution.py:35
  20.8 2.4 %collective-permute-start.3 = (bf16[8,8192]{1,0:T(8,128)(2,1)S(1)}, bf16[8,8192]{1,0:T(8,128)(2,1)S(1)}, u32[]{:S(2)}, u32[]{:S(2)}) collective-permute-start(bf16[8,8192]{1,0:T(8,128)(2,1)S(1)} %pad_maximum_fusion.1.refs_0_), channel_id=1, source_target_pairs={{2,0},{33,1},{0,2},{35,3},{6,4},{37,5},{4,6},{39,7},{10,8},{41,9},... | collective-permute-start | bytes 393224 | tf_op jit(solution)/shard_map/ppermute | solution.py:35
  23.4 2.9 %collective-permute-done.4.refs_2_ = bf16[8,8192]{1,0:T(8,128)(2,1)S(1)} collective-permute-done((bf16[8,8192]{1,0:T(8,128)(2,1)S(1)}, bf16[8,8192]{1,0:T(8,128)(2,1)S(1)}, u32[]{:S(2)}, u32[]{:S(2)}) %collective-permute-start.4) | collective-permute-done | bytes 131104 | tf_op jit(solution)/shard_map/ppermute | solution.py:35
  28.9 2.1 %fusion.2 = f32[128]{0:T(128)S(1)} fusion(bf16[1,128,8192]{2,1,0:T(8,128)(2,1)} %param.11), kind=kLoop, calls=%fused_computation.7 | loop fusion | flops 3145600 | bytes 2097664 | tf_op jit(solution)/shard_map/reduce_sum | solution.py:118
  31.0 6.0 %collective-permute-start.9 = (bf16[32,8192]{1,0:T(8,128)(2,1)S(1)}, bf16[32,8192]{1,0:T(8,128)(2,1)S(1)}, u32[]{:S(2)}, u32[]{:S(2)}) collective-permute-start(bf16[32,8192]{1,0:T(8,128)(2,1)S(1)} %shard_map.111.refs_0_), channel_id=1, source_target_pairs={{1,0},{0,1},{3,2},{2,3},{5,4},{4,5},{7,6},{6,7},{9,8},{8,9},{11,10... | collective-permute-start | bytes 1572872 | tf_op jit(solution)/shard_map/ppermute | solution.py:35
  38.5 1.7 %collective-permute-start.12 = (bf16[32,8192]{1,0:T(8,128)(2,1)S(1)}, bf16[32,8192]{1,0:T(8,128)(2,1)S(1)}, u32[]{:S(2)}, u32[]{:S(2)}) collective-permute-start(bf16[32,8192]{1,0:T(8,128)(2,1)S(1)} %collective-permute-done.8.refs_3_), channel_id=1, source_target_pairs={{1,0},{0,1},{3,2},{2,3},{5,4},{4,5},{7,6},{6,7},{9,8},{8,9},{11,10... | collective-permute-start | bytes 1572872 | tf_op jit(solution)/shard_map/ppermute | solution.py:35
  40.2 2.0 %collective-permute-done.7.refs_2_ = bf16[32,8192]{1,0:T(8,128)(2,1)S(1)} collective-permute-done((bf16[32,8192]{1,0:T(8,128)(2,1)S(1)}, bf16[32,8192]{1,0:T(8,128)(2,1)S(1)}, u32[]{:S(2)}, u32[]{:S(2)}) %collective-permute-start.7) | collective-permute-done | bytes 524320 | tf_op jit(solution)/shard_map/ppermute | solution.py:35
  42.2 4.5 %collective-permute-start.11 = (bf16[32,8192]{1,0:T(8,128)(2,1)S(1)}, bf16[32,8192]{1,0:T(8,128)(2,1)S(1)}, u32[]{:S(2)}, u32[]{:S(2)}) collective-permute-start(bf16[32,8192]{1,0:T(8,128)(2,1)S(1)} %collective-permute-done.7.refs_2_), channel_id=1, source_target_pairs={{1,0},{0,1},{3,2},{2,3},{5,4},{4,5},{7,6},{6,7},{9,8},{8,9},{11,10... | collective-permute-start | bytes 1572872 | tf_op jit(solution)/shard_map/ppermute | solution.py:35
  50.9 2.3 %collective-permute-done.13 = bf16[264,128]{1,0:T(8,128)(2,1)S(1)} collective-permute-done((bf16[264,128]{1,0:T(8,128)(2,1)S(1)}, bf16[264,128]{1,0:T(8,128)(2,1)S(1)}, u32[]{:S(2)}, u32[]{:S(2)}) %collective-permute-start.13) | collective-permute-done | bytes 67616 | tf_op jit(solution)/shard_map/ppermute | solution.py:107
  57.9 3.8 %collective-permute-start.16 = (bf16[32,8192]{1,0:T(8,128)(2,1)S(1)}, bf16[32,8192]{1,0:T(8,128)(2,1)S(1)}, u32[]{:S(2)}, u32[]{:S(2)}) collective-permute-start(bf16[32,8192]{1,0:T(8,128)(2,1)S(1)} %fusion.16), channel_id=1, source_target_pairs={{124,0},{21,1},{126,2},{23,3},{112,4},{25,5},{114,6},{27,7},{116,8... | collective-permute-start | bytes 1572872 | tf_op jit(solution)/shard_map/ppermute | solution.py:35
  62.3 1.8 %collective-permute-start.17 = (bf16[32,8192]{1,0:T(8,128)(2,1)S(1)}, bf16[32,8192]{1,0:T(8,128)(2,1)S(1)}, u32[]{:S(2)}, u32[]{:S(2)}) collective-permute-start(bf16[32,8192]{1,0:T(8,128)(2,1)S(1)} %get-tuple-element.24), channel_id=1, source_target_pairs={{112,0},{17,1},{114,2},{19,3},{116,4},{21,5},{118,6},{23,7},{120,8... | collective-permute-start | bytes 1572872 | tf_op jit(solution)/shard_map/ppermute | solution.py:35
  65.6 2.2 %collective-permute-done.16 = bf16[32,8192]{1,0:T(8,128)(2,1)S(1)} collective-permute-done((bf16[32,8192]{1,0:T(8,128)(2,1)S(1)}, bf16[32,8192]{1,0:T(8,128)(2,1)S(1)}, u32[]{:S(2)}, u32[]{:S(2)}) %collective-permute-start.16) | collective-permute-done | bytes 524320 | tf_op jit(solution)/shard_map/ppermute | solution.py:35
  67.9 5.6 %collective-permute-done.17 = bf16[32,8192]{1,0:T(8,128)(2,1)S(1)} collective-permute-done((bf16[32,8192]{1,0:T(8,128)(2,1)S(1)}, bf16[32,8192]{1,0:T(8,128)(2,1)S(1)}, u32[]{:S(2)}, u32[]{:S(2)}) %collective-permute-start.17) | collective-permute-done | bytes 524320 | tf_op jit(solution)/shard_map/ppermute | solution.py:35
  73.8 4.5 %collective-permute-start.19 = (bf16[8,8192]{1,0:T(8,128)(2,1)S(1)}, bf16[8,8192]{1,0:T(8,128)(2,1)S(1)}, u32[]{:S(2)}, u32[]{:S(2)}) collective-permute-start(bf16[8,8192]{1,0:T(8,128)(2,1)S(1)} %get-tuple-element.26), channel_id=1, source_target_pairs={{10,0},{65,1},{8,2},{67,3},{14,4},{69,5},{12,6},{71,7},{2,8},{73,9... | collective-permute-start | bytes 393224 | tf_op jit(solution)/shard_map/ppermute | solution.py:35
  78.3 3.6 %collective-permute-start.20 = (bf16[8,8192]{1,0:T(8,128)(2,1)S(1)}, bf16[8,8192]{1,0:T(8,128)(2,1)S(1)}, u32[]{:S(2)}, u32[]{:S(2)}) collective-permute-start(bf16[8,8192]{1,0:T(8,128)(2,1)S(1)} %get-tuple-element.28), channel_id=1, source_target_pairs={{8,0},{33,1},{10,2},{35,3},{12,4},{37,5},{14,6},{39,7},{0,8},{41,9... | collective-permute-start | bytes 393224 | tf_op jit(solution)/shard_map/ppermute | solution.py:35
  81.9 2.7 %collective-permute-done.21 = bf16[8,8192]{1,0:T(8,128)(2,1)S(1)} collective-permute-done((bf16[8,8192]{1,0:T(8,128)(2,1)S(1)}, bf16[8,8192]{1,0:T(8,128)(2,1)S(1)}, u32[]{:S(2)}, u32[]{:S(2)}) %collective-permute-start.21) | collective-permute-done | bytes 131104 | tf_op jit(solution)/shard_map/ppermute | solution.py:35
  84.6 2.1 %collective-permute-done.20 = bf16[8,8192]{1,0:T(8,128)(2,1)S(1)} collective-permute-done((bf16[8,8192]{1,0:T(8,128)(2,1)S(1)}, bf16[8,8192]{1,0:T(8,128)(2,1)S(1)}, u32[]{:S(2)}, u32[]{:S(2)}) %collective-permute-start.20) | collective-permute-done | bytes 131104 | tf_op jit(solution)/shard_map/ppermute | solution.py:35
  87.4 2.3 %collective-permute-start.23 = (bf16[8,8192]{1,0:T(8,128)(2,1)S(1)}, bf16[8,8192]{1,0:T(8,128)(2,1)S(1)}, u32[]{:S(2)}, u32[]{:S(2)}) collective-permute-start(bf16[8,8192]{1,0:T(8,128)(2,1)S(1)} %fusion.19), channel_id=1, source_target_pairs={{64,0},{11,1},{66,2},{9,3},{68,4},{15,5},{70,6},{13,7},{72,8},{3,9... | collective-permute-start | bytes 393224 | tf_op jit(solution)/shard_map/ppermute | solution.py:35
  89.8 2.8 %collective-permute-start.22 = (bf16[8,8192]{1,0:T(8,128)(2,1)S(1)}, bf16[8,8192]{1,0:T(8,128)(2,1)S(1)}, u32[]{:S(2)}, u32[]{:S(2)}) collective-permute-start(bf16[8,8192]{1,0:T(8,128)(2,1)S(1)} %fusion.19), channel_id=1, source_target_pairs={{96,0},{9,1},{98,2},{11,3},{100,4},{13,5},{102,6},{15,7},{104,8},{... | collective-permute-start | bytes 393224 | tf_op jit(solution)/shard_map/ppermute | solution.py:35
  92.5 2.6 %collective-permute-done.23 = bf16[8,8192]{1,0:T(8,128)(2,1)S(1)} collective-permute-done((bf16[8,8192]{1,0:T(8,128)(2,1)S(1)}, bf16[8,8192]{1,0:T(8,128)(2,1)S(1)}, u32[]{:S(2)}, u32[]{:S(2)}) %collective-permute-start.23) | collective-permute-done | bytes 131104 | tf_op jit(solution)/shard_map/ppermute | solution.py:35
  96.8 3.7 %collective-permute-start.27 = (bf16[8,8192]{1,0:T(8,128)(2,1)S(1)}, bf16[8,8192]{1,0:T(8,128)(2,1)S(1)}, u32[]{:S(2)}, u32[]{:S(2)}) collective-permute-start(bf16[8,8192]{1,0:T(8,128)(2,1)S(1)} %multiply_convert_fusion.refs_0_), channel_id=1, source_target_pairs={{10,0},{65,1},{8,2},{67,3},{14,4},{69,5},{12,6},{71,7},{2,8},{73,9... | collective-permute-start | bytes 393224 | tf_op jit(solution)/shard_map/ppermute | solution.py:35
  100.5 2.1 %collective-permute-start.26 = (bf16[8,8192]{1,0:T(8,128)(2,1)S(1)}, bf16[8,8192]{1,0:T(8,128)(2,1)S(1)}, u32[]{:S(2)}, u32[]{:S(2)}) collective-permute-start(bf16[8,8192]{1,0:T(8,128)(2,1)S(1)} %multiply_convert_fusion.refs_0_), channel_id=1, source_target_pairs={{8,0},{97,1},{10,2},{99,3},{12,4},{101,5},{14,6},{103,7},{0,8},{10... | collective-permute-start | bytes 393224 | tf_op jit(solution)/shard_map/ppermute | solution.py:35
  104.8 4.1 %collective-permute-done.26.refs_2_ = bf16[8,8192]{1,0:T(8,128)(2,1)S(1)} collective-permute-done((bf16[8,8192]{1,0:T(8,128)(2,1)S(1)}, bf16[8,8192]{1,0:T(8,128)(2,1)S(1)}, u32[]{:S(2)}, u32[]{:S(2)}) %collective-permute-start.26) | collective-permute-done | bytes 131104 | tf_op jit(solution)/shard_map/ppermute | solution.py:35
  109.0 2.6 %collective-permute-start.29 = (bf16[32,8192]{1,0:T(8,128)(2,1)S(1)}, bf16[32,8192]{1,0:T(8,128)(2,1)S(1)}, u32[]{:S(2)}, u32[]{:S(2)}) collective-permute-start(bf16[32,8192]{1,0:T(8,128)(2,1)S(1)} %shard_map.115.refs_0_), channel_id=1, source_target_pairs={{16,0},{113,1},{18,2},{115,3},{20,4},{117,5},{22,6},{119,7},{24,8}... | collective-permute-start | bytes 1572872 | tf_op jit(solution)/shard_map/ppermute | solution.py:35
  111.6 5.4 %collective-permute-start.31 = (bf16[32,8192]{1,0:T(8,128)(2,1)S(1)}, bf16[32,8192]{1,0:T(8,128)(2,1)S(1)}, u32[]{:S(2)}, u32[]{:S(2)}) collective-permute-start(bf16[32,8192]{1,0:T(8,128)(2,1)S(1)} %shard_map.115.refs_0_), channel_id=1, source_target_pairs={{1,0},{0,1},{3,2},{2,3},{5,4},{4,5},{7,6},{6,7},{9,8},{8,9},{11,10... | collective-permute-start | bytes 1572872 | tf_op jit(solution)/shard_map/ppermute | solution.py:35
  117.0 3.4 %collective-permute-done.30.refs_3_ = bf16[32,8192]{1,0:T(8,128)(2,1)S(1)} collective-permute-done((bf16[32,8192]{1,0:T(8,128)(2,1)S(1)}, bf16[32,8192]{1,0:T(8,128)(2,1)S(1)}, u32[]{:S(2)}, u32[]{:S(2)}) %collective-permute-start.30) | collective-permute-done | bytes 524320 | tf_op jit(solution)/shard_map/ppermute | solution.py:35
  121.7 3.0 %collective-permute-done.29.refs_2_ = bf16[32,8192]{1,0:T(8,128)(2,1)S(1)} collective-permute-done((bf16[32,8192]{1,0:T(8,128)(2,1)S(1)}, bf16[32,8192]{1,0:T(8,128)(2,1)S(1)}, u32[]{:S(2)}, u32[]{:S(2)}) %collective-permute-start.29) | collective-permute-done | bytes 524320 | tf_op jit(solution)/shard_map/ppermute | solution.py:35
  124.8 1.7 %collective-permute-start.33 = (bf16[32,8192]{1,0:T(8,128)(2,1)S(1)}, bf16[32,8192]{1,0:T(8,128)(2,1)S(1)}, u32[]{:S(2)}, u32[]{:S(2)}) collective-permute-start(bf16[32,8192]{1,0:T(8,128)(2,1)S(1)} %collective-permute-done.29.refs_2_), channel_id=1, source_target_pairs={{1,0},{0,1},{3,2},{2,3},{5,4},{4,5},{7,6},{6,7},{9,8},{8,9},{11,10... | collective-permute-start | bytes 1572872 | tf_op jit(solution)/shard_map/ppermute | solution.py:35
  130.9 2.6 %fusion = bf16[128,8192]{1,0:T(8,128)(2,1)} fusion(bf16[256,128]{1,0:T(8,128)(2,1)S(1)} %get-tuple-element.30, bf16[256,8192]{1,0:T(8,128)(2,1)S(1)} %shard_map.118, bf16[1,128,8192]{2,1,0:T(8,128)(2,1)S(1)} %copy-done.1, f32[128]{0:T(128)S(1)} %rsqrt_multiply_fusion), kind=kOutput, calls=%fused_computation.1 | convolution fusion | flops 541065216 | bytes 8454656 | tf_op jit(solution)/shard_map/dot_general | solution.py:111
  135.4 2.1 %fusion.1 = bf16[1,128,8192]{2,1,0:T(8,128)(2,1)} fusion(bf16[256,8192]{1,0:T(8,128)(2,1)S(1)} %shard_map.114, bf16[256,128]{1,0:T(8,128)(2,1)S(1)} %get-tuple-element.19), kind=kOutput, calls=%fused_computation.4 | convolution fusion | flops 537919488 | bytes 6356992 | tf_op jit(solution)/shard_map/dot_general | solution.py:111
  (99 shorter events, 31.0 us)
Async XLA Ops:
  0.6 8.1 %collective-permute-start.1 = (bf16[2,8192]{1,0:T(2,128)(2,1)}, bf16[2,8192]{1,0:T(2,128)(2,1)S(1)}, u32[]{:S(2)}, u32[]{:S(2)}) collective-permute-start(bf16[2,8192]{1,0:T(2,128)(2,1)} %bitcast.40), channel_id=1, source_target_pairs={{64,0},{11,1},{66,2},{9,3},{68,4},{15,5},{70,6},{13,7},{72,8},{3,9... | collective-permute-start | bytes 98312 | tf_op jit(solution)/shard_map/ppermute | solution.py:35
  6.9 4.7 %collective-permute-start.2 = (bf16[2,8192]{1,0:T(2,128)(2,1)}, bf16[2,8192]{1,0:T(2,128)(2,1)S(1)}, u32[]{:S(2)}, u32[]{:S(2)}) collective-permute-start(bf16[2,8192]{1,0:T(2,128)(2,1)} %bitcast.41), channel_id=1, source_target_pairs={{32,0},{3,1},{34,2},{1,3},{36,4},{7,5},{38,6},{5,7},{40,8},{11,9},... | collective-permute-start | bytes 98312 | tf_op jit(solution)/shard_map/ppermute | solution.py:35
  7.0 4.6 %collective-permute-start = (bf16[2,8192]{1,0:T(2,128)(2,1)}, bf16[2,8192]{1,0:T(2,128)(2,1)S(1)}, u32[]{:S(2)}, u32[]{:S(2)}) collective-permute-start(bf16[2,8192]{1,0:T(2,128)(2,1)} %bitcast.42), channel_id=1, source_target_pairs={{96,0},{9,1},{98,2},{11,3},{100,4},{13,5},{102,6},{15,7},{104,8},{... | collective-permute-start | bytes 98312 | tf_op jit(solution)/shard_map/ppermute | solution.py:35
  12.8 10.6 %collective-permute-start.5 = (bf16[8,8192]{1,0:T(8,128)(2,1)S(1)}, bf16[8,8192]{1,0:T(8,128)(2,1)S(1)}, u32[]{:S(2)}, u32[]{:S(2)}) collective-permute-start(bf16[8,8192]{1,0:T(8,128)(2,1)S(1)} %pad_maximum_fusion.1.refs_0_), channel_id=1, source_target_pairs={{10,0},{65,1},{8,2},{67,3},{14,4},{69,5},{12,6},{71,7},{2,8},{73,9... | collective-permute-start | bytes 393224 | tf_op jit(solution)/shard_map/ppermute | solution.py:35
  19.6 6.7 %collective-permute-start.4 = (bf16[8,8192]{1,0:T(8,128)(2,1)S(1)}, bf16[8,8192]{1,0:T(8,128)(2,1)S(1)}, u32[]{:S(2)}, u32[]{:S(2)}) collective-permute-start(bf16[8,8192]{1,0:T(8,128)(2,1)S(1)} %pad_maximum_fusion.1.refs_0_), channel_id=1, source_target_pairs={{8,0},{97,1},{10,2},{99,3},{12,4},{101,5},{14,6},{103,7},{0,8},{10... | collective-permute-start | bytes 393224 | tf_op jit(solution)/shard_map/ppermute | solution.py:35
  20.8 6.1 %collective-permute-start.3 = (bf16[8,8192]{1,0:T(8,128)(2,1)S(1)}, bf16[8,8192]{1,0:T(8,128)(2,1)S(1)}, u32[]{:S(2)}, u32[]{:S(2)}) collective-permute-start(bf16[8,8192]{1,0:T(8,128)(2,1)S(1)} %pad_maximum_fusion.1.refs_0_), channel_id=1, source_target_pairs={{2,0},{33,1},{0,2},{35,3},{6,4},{37,5},{4,6},{39,7},{10,8},{41,9},... | collective-permute-start | bytes 393224 | tf_op jit(solution)/shard_map/ppermute | solution.py:35
  27.0 11.5 %collective-permute-start.8 = (bf16[32,8192]{1,0:T(8,128)(2,1)S(1)}, bf16[32,8192]{1,0:T(8,128)(2,1)S(1)}, u32[]{:S(2)}, u32[]{:S(2)}) collective-permute-start(bf16[32,8192]{1,0:T(8,128)(2,1)S(1)} %shard_map.111.refs_0_), channel_id=1, source_target_pairs={{20,0},{125,1},{22,2},{127,3},{24,4},{113,5},{26,6},{115,7},{28,8}... | collective-permute-start | bytes 1572872 | tf_op jit(solution)/shard_map/ppermute | solution.py:35
  28.0 14.2 %collective-permute-start.7 = (bf16[32,8192]{1,0:T(8,128)(2,1)S(1)}, bf16[32,8192]{1,0:T(8,128)(2,1)S(1)}, u32[]{:S(2)}, u32[]{:S(2)}) collective-permute-start(bf16[32,8192]{1,0:T(8,128)(2,1)S(1)} %shard_map.111.refs_0_), channel_id=1, source_target_pairs={{16,0},{113,1},{18,2},{115,3},{20,4},{117,5},{22,6},{119,7},{24,8}... | collective-permute-start | bytes 1572872 | tf_op jit(solution)/shard_map/ppermute | solution.py:35
  28.6 18.1 %collective-permute-start.6 = (bf16[32,8192]{1,0:T(8,128)(2,1)S(1)}, bf16[32,8192]{1,0:T(8,128)(2,1)S(1)}, u32[]{:S(2)}, u32[]{:S(2)}) collective-permute-start(bf16[32,8192]{1,0:T(8,128)(2,1)S(1)} %shard_map.111.refs_0_), channel_id=1, source_target_pairs={{4,0},{13,1},{6,2},{15,3},{8,4},{1,5},{10,6},{3,7},{12,8},{5,9},{1... | collective-permute-start | bytes 1572872 | tf_op jit(solution)/shard_map/ppermute | solution.py:35
  31.0 16.6 %collective-permute-start.9 = (bf16[32,8192]{1,0:T(8,128)(2,1)S(1)}, bf16[32,8192]{1,0:T(8,128)(2,1)S(1)}, u32[]{:S(2)}, u32[]{:S(2)}) collective-permute-start(bf16[32,8192]{1,0:T(8,128)(2,1)S(1)} %shard_map.111.refs_0_), channel_id=1, source_target_pairs={{1,0},{0,1},{3,2},{2,3},{5,4},{4,5},{7,6},{6,7},{9,8},{8,9},{11,10... | collective-permute-start | bytes 1572872 | tf_op jit(solution)/shard_map/ppermute | solution.py:35
  38.5 9.1 %collective-permute-start.12 = (bf16[32,8192]{1,0:T(8,128)(2,1)S(1)}, bf16[32,8192]{1,0:T(8,128)(2,1)S(1)}, u32[]{:S(2)}, u32[]{:S(2)}) collective-permute-start(bf16[32,8192]{1,0:T(8,128)(2,1)S(1)} %collective-permute-done.8.refs_3_), channel_id=1, source_target_pairs={{1,0},{0,1},{3,2},{2,3},{5,4},{4,5},{7,6},{6,7},{9,8},{8,9},{11,10... | collective-permute-start | bytes 1572872 | tf_op jit(solution)/shard_map/ppermute | solution.py:35
  42.2 6.1 %collective-permute-start.11 = (bf16[32,8192]{1,0:T(8,128)(2,1)S(1)}, bf16[32,8192]{1,0:T(8,128)(2,1)S(1)}, u32[]{:S(2)}, u32[]{:S(2)}) collective-permute-start(bf16[32,8192]{1,0:T(8,128)(2,1)S(1)} %collective-permute-done.7.refs_2_), channel_id=1, source_target_pairs={{1,0},{0,1},{3,2},{2,3},{5,4},{4,5},{7,6},{6,7},{9,8},{8,9},{11,10... | collective-permute-start | bytes 1572872 | tf_op jit(solution)/shard_map/ppermute | solution.py:35
  49.9 3.4 %collective-permute-start.13 = (bf16[264,128]{1,0:T(8,128)(2,1)S(1)}, bf16[264,128]{1,0:T(8,128)(2,1)S(1)}, u32[]{:S(2)}, u32[]{:S(2)}) collective-permute-start(bf16[264,128]{1,0:T(8,128)(2,1)S(1)} %fusion.22), channel_id=1, source_target_pairs={{0,128},{128,0},{1,129},{129,1},{2,130},{130,2},{3,131},{131,3},{4... | collective-permute-start | bytes 202760 | tf_op jit(solution)/shard_map/ppermute | solution.py:107
  57.4 4.3 %collective-permute-start.15 = (bf16[96,8192]{1,0:T(8,128)(2,1)S(1)}, bf16[96,8192]{1,0:T(8,128)(2,1)S(1)}, u32[]{:S(2)}, u32[]{:S(2)}) collective-permute-start(bf16[96,8192]{1,0:T(8,128)(2,1)S(1)} %slice.75), channel_id=1, source_target_pairs={{1,0},{0,1},{3,2},{2,3},{5,4},{4,5},{7,6},{6,7},{9,8},{8,9},{11,10... | collective-permute-start | bytes 4718600 | tf_op jit(solution)/shard_map/ppermute | solution.py:35
  57.9 10.0 %collective-permute-start.16 = (bf16[32,8192]{1,0:T(8,128)(2,1)S(1)}, bf16[32,8192]{1,0:T(8,128)(2,1)S(1)}, u32[]{:S(2)}, u32[]{:S(2)}) collective-permute-start(bf16[32,8192]{1,0:T(8,128)(2,1)S(1)} %fusion.16), channel_id=1, source_target_pairs={{124,0},{21,1},{126,2},{23,3},{112,4},{25,5},{114,6},{27,7},{116,8... | collective-permute-start | bytes 1572872 | tf_op jit(solution)/shard_map/ppermute | solution.py:35
  62.3 11.3 %collective-permute-start.17 = (bf16[32,8192]{1,0:T(8,128)(2,1)S(1)}, bf16[32,8192]{1,0:T(8,128)(2,1)S(1)}, u32[]{:S(2)}, u32[]{:S(2)}) collective-permute-start(bf16[32,8192]{1,0:T(8,128)(2,1)S(1)} %get-tuple-element.24), channel_id=1, source_target_pairs={{112,0},{17,1},{114,2},{19,3},{116,4},{21,5},{118,6},{23,7},{120,8... | collective-permute-start | bytes 1572872 | tf_op jit(solution)/shard_map/ppermute | solution.py:35
  64.0 9.5 %collective-permute-start.18 = (bf16[32,8192]{1,0:T(8,128)(2,1)S(1)}, bf16[32,8192]{1,0:T(8,128)(2,1)S(1)}, u32[]{:S(2)}, u32[]{:S(2)}) collective-permute-start(bf16[32,8192]{1,0:T(8,128)(2,1)S(1)} %get-tuple-element.25), channel_id=1, source_target_pairs={{12,0},{5,1},{14,2},{7,3},{0,4},{9,5},{2,6},{11,7},{4,8},{13,9},{6... | collective-permute-start | bytes 1572872 | tf_op jit(solution)/shard_map/ppermute | solution.py:35
  73.8 8.1 %collective-permute-start.19 = (bf16[8,8192]{1,0:T(8,128)(2,1)S(1)}, bf16[8,8192]{1,0:T(8,128)(2,1)S(1)}, u32[]{:S(2)}, u32[]{:S(2)}) collective-permute-start(bf16[8,8192]{1,0:T(8,128)(2,1)S(1)} %get-tuple-element.26), channel_id=1, source_target_pairs={{10,0},{65,1},{8,2},{67,3},{14,4},{69,5},{12,6},{71,7},{2,8},{73,9... | collective-permute-start | bytes 393224 | tf_op jit(solution)/shard_map/ppermute | solution.py:35
  78.3 6.3 %collective-permute-start.21 = (bf16[8,8192]{1,0:T(8,128)(2,1)S(1)}, bf16[8,8192]{1,0:T(8,128)(2,1)S(1)}, u32[]{:S(2)}, u32[]{:S(2)}) collective-permute-start(bf16[8,8192]{1,0:T(8,128)(2,1)S(1)} %get-tuple-element.27), channel_id=1, source_target_pairs={{2,0},{97,1},{0,2},{99,3},{6,4},{101,5},{4,6},{103,7},{10,8},{105,... | collective-permute-start | bytes 393224 | tf_op jit(solution)/shard_map/ppermute | solution.py:35
  78.3 8.4 %collective-permute-start.20 = (bf16[8,8192]{1,0:T(8,128)(2,1)S(1)}, bf16[8,8192]{1,0:T(8,128)(2,1)S(1)}, u32[]{:S(2)}, u32[]{:S(2)}) collective-permute-start(bf16[8,8192]{1,0:T(8,128)(2,1)S(1)} %get-tuple-element.28), channel_id=1, source_target_pairs={{8,0},{33,1},{10,2},{35,3},{12,4},{37,5},{14,6},{39,7},{0,8},{41,9... | collective-permute-start | bytes 393224 | tf_op jit(solution)/shard_map/ppermute | solution.py:35
  86.8 5.7 %collective-permute-start.24 = (bf16[8,8192]{1,0:T(8,128)(2,1)S(1)}, bf16[8,8192]{1,0:T(8,128)(2,1)S(1)}, u32[]{:S(2)}, u32[]{:S(2)}) collective-permute-start(bf16[8,8192]{1,0:T(8,128)(2,1)S(1)} %fusion.19), channel_id=1, source_target_pairs={{32,0},{3,1},{34,2},{1,3},{36,4},{7,5},{38,6},{5,7},{40,8},{11,9},... | collective-permute-start | bytes 393224 | tf_op jit(solution)/shard_map/ppermute | solution.py:35
  87.4 7.7 %collective-permute-start.23 = (bf16[8,8192]{1,0:T(8,128)(2,1)S(1)}, bf16[8,8192]{1,0:T(8,128)(2,1)S(1)}, u32[]{:S(2)}, u32[]{:S(2)}) collective-permute-start(bf16[8,8192]{1,0:T(8,128)(2,1)S(1)} %fusion.19), channel_id=1, source_target_pairs={{64,0},{11,1},{66,2},{9,3},{68,4},{15,5},{70,6},{13,7},{72,8},{3,9... | collective-permute-start | bytes 393224 | tf_op jit(solution)/shard_map/ppermute | solution.py:35
  89.8 6.5 %collective-permute-start.22 = (bf16[8,8192]{1,0:T(8,128)(2,1)S(1)}, bf16[8,8192]{1,0:T(8,128)(2,1)S(1)}, u32[]{:S(2)}, u32[]{:S(2)}) collective-permute-start(bf16[8,8192]{1,0:T(8,128)(2,1)S(1)} %fusion.19), channel_id=1, source_target_pairs={{96,0},{9,1},{98,2},{11,3},{100,4},{13,5},{102,6},{15,7},{104,8},{... | collective-permute-start | bytes 393224 | tf_op jit(solution)/shard_map/ppermute | solution.py:35
  96.8 8.0 %collective-permute-start.27 = (bf16[8,8192]{1,0:T(8,128)(2,1)S(1)}, bf16[8,8192]{1,0:T(8,128)(2,1)S(1)}, u32[]{:S(2)}, u32[]{:S(2)}) collective-permute-start(bf16[8,8192]{1,0:T(8,128)(2,1)S(1)} %multiply_convert_fusion.refs_0_), channel_id=1, source_target_pairs={{10,0},{65,1},{8,2},{67,3},{14,4},{69,5},{12,6},{71,7},{2,8},{73,9... | collective-permute-start | bytes 393224 | tf_op jit(solution)/shard_map/ppermute | solution.py:35
  100.5 8.3 %collective-permute-start.26 = (bf16[8,8192]{1,0:T(8,128)(2,1)S(1)}, bf16[8,8192]{1,0:T(8,128)(2,1)S(1)}, u32[]{:S(2)}, u32[]{:S(2)}) collective-permute-start(bf16[8,8192]{1,0:T(8,128)(2,1)S(1)} %multiply_convert_fusion.refs_0_), channel_id=1, source_target_pairs={{8,0},{97,1},{10,2},{99,3},{12,4},{101,5},{14,6},{103,7},{0,8},{10... | collective-permute-start | bytes 393224 | tf_op jit(solution)/shard_map/ppermute | solution.py:35
  102.6 6.2 %collective-permute-start.25 = (bf16[8,8192]{1,0:T(8,128)(2,1)S(1)}, bf16[8,8192]{1,0:T(8,128)(2,1)S(1)}, u32[]{:S(2)}, u32[]{:S(2)}) collective-permute-start(bf16[8,8192]{1,0:T(8,128)(2,1)S(1)} %multiply_convert_fusion.refs_0_), channel_id=1, source_target_pairs={{2,0},{33,1},{0,2},{35,3},{6,4},{37,5},{4,6},{39,7},{10,8},{41,9},... | collective-permute-start | bytes 393224 | tf_op jit(solution)/shard_map/ppermute | solution.py:35
  108.9 11.5 %collective-permute-start.30 = (bf16[32,8192]{1,0:T(8,128)(2,1)S(1)}, bf16[32,8192]{1,0:T(8,128)(2,1)S(1)}, u32[]{:S(2)}, u32[]{:S(2)}) collective-permute-start(bf16[32,8192]{1,0:T(8,128)(2,1)S(1)} %shard_map.115.refs_0_), channel_id=1, source_target_pairs={{20,0},{125,1},{22,2},{127,3},{24,4},{113,5},{26,6},{115,7},{28,8}... | collective-permute-start | bytes 1572872 | tf_op jit(solution)/shard_map/ppermute | solution.py:35
  109.0 15.8 %collective-permute-start.29 = (bf16[32,8192]{1,0:T(8,128)(2,1)S(1)}, bf16[32,8192]{1,0:T(8,128)(2,1)S(1)}, u32[]{:S(2)}, u32[]{:S(2)}) collective-permute-start(bf16[32,8192]{1,0:T(8,128)(2,1)S(1)} %shard_map.115.refs_0_), channel_id=1, source_target_pairs={{16,0},{113,1},{18,2},{115,3},{20,4},{117,5},{22,6},{119,7},{24,8}... | collective-permute-start | bytes 1572872 | tf_op jit(solution)/shard_map/ppermute | solution.py:35
  111.6 14.9 %collective-permute-start.28 = (bf16[32,8192]{1,0:T(8,128)(2,1)S(1)}, bf16[32,8192]{1,0:T(8,128)(2,1)S(1)}, u32[]{:S(2)}, u32[]{:S(2)}) collective-permute-start(bf16[32,8192]{1,0:T(8,128)(2,1)S(1)} %shard_map.115.refs_0_), channel_id=1, source_target_pairs={{4,0},{13,1},{6,2},{15,3},{8,4},{1,5},{10,6},{3,7},{12,8},{5,9},{1... | collective-permute-start | bytes 1572872 | tf_op jit(solution)/shard_map/ppermute | solution.py:35
  111.6 16.6 %collective-permute-start.31 = (bf16[32,8192]{1,0:T(8,128)(2,1)S(1)}, bf16[32,8192]{1,0:T(8,128)(2,1)S(1)}, u32[]{:S(2)}, u32[]{:S(2)}) collective-permute-start(bf16[32,8192]{1,0:T(8,128)(2,1)S(1)} %shard_map.115.refs_0_), channel_id=1, source_target_pairs={{1,0},{0,1},{3,2},{2,3},{5,4},{4,5},{7,6},{6,7},{9,8},{8,9},{11,10... | collective-permute-start | bytes 1572872 | tf_op jit(solution)/shard_map/ppermute | solution.py:35
  120.4 7.7 %collective-permute-start.34 = (bf16[32,8192]{1,0:T(8,128)(2,1)S(1)}, bf16[32,8192]{1,0:T(8,128)(2,1)S(1)}, u32[]{:S(2)}, u32[]{:S(2)}) collective-permute-start(bf16[32,8192]{1,0:T(8,128)(2,1)S(1)} %collective-permute-done.30.refs_3_), channel_id=1, source_target_pairs={{1,0},{0,1},{3,2},{2,3},{5,4},{4,5},{7,6},{6,7},{9,8},{8,9},{11,10... | collective-permute-start | bytes 1572872 | tf_op jit(solution)/shard_map/ppermute | solution.py:35
  129.9 4.8 %collective-permute-start.35 = (bf16[256,128]{1,0:T(8,128)(2,1)S(1)}, bf16[256,128]{1,0:T(8,128)(2,1)S(1)}, u32[]{:S(2)}, u32[]{:S(2)}) collective-permute-start(bf16[256,128]{1,0:T(8,128)(2,1)S(1)} %fusion.21), channel_id=1, source_target_pairs={{0,128},{128,0},{1,129},{129,1},{2,130},{130,2},{3,131},{131,3},{4... | collective-permute-start | bytes 196616 | tf_op jit(solution)/shard_map/ppermute | solution.py:107
  (9 other events, 87.0 us)

commit v3 on v2

v3 whole, which is shorter than its diff:
```python
import jax
import jax.numpy as jnp
import numpy as np
from jax import lax
from jax.experimental import pallas as pl
from jax.experimental.pallas import tpu as pltpu
from jax.sharding import PartitionSpec as P

BLK = 128
NZ, NX, NY, NC = 8, 4, 2, 2

epsilon = 1e-06
sparsity = 0.25
loss_scale = 0.0625

EVEN_Z = ((0, 0, 0), (2, 0, 0), (6, 0, 0), (4, 0, 0))
EVEN_XY = ((0, 0, 0), (0, 0, 1), (0, 2, 0), (0, 2, 1))
TURNS = [[(0, 1, 3, 2)[(i - own) % 4] for i in range(4)] for own in range(4)]
TURNS += [[i ^ own for i in range(4)] for own in range(4)]
OCTET_Z = np.array([dz + 2 * k for dz in (0, -1, -1, 0) for k in (0, 2, 3, 1)], np.int32)


def place(z, x, y, c):
    return (((z % NZ) * NX + x % NX) * NY + y % NY) * NC + c % NC


def fetch(value, *offsets, c=0):
    pairs = []
    for iz in range(NZ):
        for ix in range(NX):
            for iy in range(NY):
                for ic in range(NC):
                    z, x, y = offsets[ic % len(offsets)]
                    pairs.append((place(iz + z, ix + x, iy + y, ic + c), place(iz, ix, iy, ic)))
    return lax.ppermute(value, "lat", pairs)


def swap_core(value):
    return fetch(value, (0, 0, 0), c=1)


def pack(pieces):
    rows = [piece.shape[0] for piece in pieces]

    def kernel(*refs):
        at = 0
        for ref, count in zip(refs[:-1], rows):
            refs[-1][at : at + count, :] = ref[...]
            at += count

    return pl.pallas_call(
        kernel,
        out_shape=jax.ShapeDtypeStruct((sum(rows), pieces[0].shape[1]), pieces[0].dtype),
        in_specs=[pl.BlockSpec(memory_space=pltpu.VMEM)] * len(pieces),
        out_specs=pl.BlockSpec(memory_space=pltpu.VMEM),
        compiler_params=pltpu.CompilerParams(vmem_limit_bytes=32 * 1024 * 1024),
    )(*pieces)


def position():
    at = lax.axis_index("lat")
    return at // (NX * NY * NC), at // (NY * NC) % NX, at // NC % NY, at % NC


def by_partner(value):
    near = [value] + [fetch(value, EVEN_Z[k], EVEN_XY[k]) for k in (1, 2, 3)]
    z, x, y, core = position()
    own = jnp.where(core == 0, z // 2, 4 + x // 2 * 2 + y)
    return [lax.select_n(own, *[near[turn[i]] for turn in TURNS]) for i in range(4)]


AROUND = (((1, 1, 0), (-1, -1, 0)), ((1, 0, 0), (-1, 0, 0)), ((0, 1, 0), (0, -1, 0)))


def after(value, *earlier):
    return lax.optimization_barrier((value,) + earlier)


def gather_rows(octet, *beside):
    group = pack([octet] + [fetch(octet, EVEN_XY[k], EVEN_Z[k]) for k in (3, 2, 1)])
    group, *beside = after(group, *beside)
    return [group] + [fetch(group, *to) for to in AROUND], beside


def low(value):
    return value.astype(jnp.bfloat16)


def add(value, arrived):
    return value + arrived.astype(jnp.float32)


def scatter_rows(terms):
    group = terms[:32]
    for k in (3, 2, 1):
        group = add(group, fetch(low(terms[32 * k : 32 * k + 32]), *AROUND[k - 1][::-1]))
    octet = group[0:8]
    for at, k, back in ((3, 1, 2), (2, 2, 1), (1, 3, 3)):
        octet = add(octet, fetch(low(group[8 * at : 8 * at + 8]), EVEN_XY[k], EVEN_Z[back]))
    parts = [part.astype(jnp.float32) for part in by_partner(low(octet))]
    return parts[0] + parts[1] + parts[2] + parts[3]


def swap_pair(value):
    return lax.ppermute(value, "pair", [(0, 1), (1, 0)])


def dot(left, right, over):
    return lax.dot_general(left, right, ((over[:1], over[1:]), ((), ())), preferred_element_type=jnp.float32)


def total_rows(groups):
    rows = pack(groups) if len(groups) > 1 else groups[0]
    return dot(jnp.ones((8, rows.shape[0]), rows.dtype), rows, (1, 0))[0:1]


def on_device(activations, enc_weight, enc_bias, dec_weight, dec_bias, block_list, block_count):
    enc, dec = enc_weight[0], dec_weight[0]
    own = activations[0]
    own_octet, enc_other = after(jnp.concatenate(by_partner(own), axis=0), swap_core(enc))
    act_groups, (dec_other,) = gather_rows(own_octet, swap_core(dec))
    norm_own = jnp.sqrt(jnp.sum(jnp.square(dec.astype(jnp.float32)), axis=1) + epsilon)

    lats = enc.shape[0]
    slots = jnp.arange(block_list.shape[0], dtype=jnp.int32) < block_count[0]
    hits = jnp.arange(2, dtype=jnp.int32)[:, None] == block_list[None, :]
    hits = jnp.any(hits & slots[None, :], axis=1).astype(jnp.float32)[:, None]
    facts = [enc_bias[None, :], jnp.broadcast_to(hits, (2, lats)), norm_own[None, :], jnp.zeros((4, lats), jnp.float32)]
    facts = jnp.concatenate(facts, axis=0)
    facts = jnp.concatenate([facts, swap_core(facts)], axis=1)
    both_enc, both_dec = pack([enc, enc_other]), pack([dec, dec_other])
    z, _, _, core = position()
    kinds = [jnp.tile(jnp.arange(NZ, dtype=jnp.int32), BLK // NZ), jnp.repeat((z + OCTET_Z) % NZ, 8)]
    block = jnp.where(core == 0, kinds[0], kinds[1]) // (NZ // 2)
    live = jnp.where(block[:, None] == 0, facts[1:2], facts[2:3])

    act = pack(act_groups)
    pre_part = dot(act, both_enc, (1, 1))
    act, pre_part = after(act, pre_part)
    act_other = swap_core(act)
    packed = jnp.concatenate([pre_part, jnp.broadcast_to(facts[3:4], (16, 2 * lats))], axis=0)
    packed = add(packed, swap_pair(low(packed)))
    norm_sum = packed[BLK : BLK + 1]
    pre_act = packed[:BLK] + facts[0:1]
    latent_act = jax.nn.softplus(pre_act) * live
    rebuilt = scatter_rows(dot(low(latent_act), both_dec, (1, 0)))

    other_block = jnp.where(core == 0, kinds[1], kinds[0]) // (NZ // 2)
    other_live = jnp.where(other_block[:, None] == 0, facts[1:2, :lats], facts[2:3, :lats])
    live = jnp.concatenate([live[:, :lats], other_live], axis=0)
    pre_act = jnp.concatenate([pre_act[:, :lats], swap_core(pre_act[:, lats:])], axis=0)
    latents = jax.nn.softplus(pre_act) * live
    slope = loss_scale * sparsity * jnp.sum(latents, axis=0) / norm_own
    factor = jax.nn.sigmoid(pre_act) * live
    rebuilt, act, latents, slope, factor = lax.optimization_barrier(
        (rebuilt + dec_bias, pack([act, act_other]), low(latents), slope, factor)
    )
    err_groups, _ = gather_rows(low(loss_scale * (rebuilt - own_octet.astype(jnp.float32))))
    halves = [pack(err_groups), pack([swap_core(group) for group in err_groups])]
    grad_part = jnp.concatenate([dot(half, dec, (1, 1)) for half in halves], axis=0)
    err = pack(halves)
    d_dec = dot(latents, err, (0, 0)) + slope[:, None] * dec.astype(jnp.float32)
    d_dec_bias = total_rows([err])
    arrived, d_dec, d_dec_bias = lax.optimization_barrier((swap_pair(low(grad_part)), low(d_dec), d_dec_bias))
    pre_grad = (add(grad_part, arrived) + loss_scale * sparsity * norm_sum[:, :lats]) * factor
    d_enc = dot(low(pre_grad), act, (0, 0))
    d_enc_bias = jnp.sum(pre_grad, axis=0)
    return low(d_enc)[None], d_dec[None], d_enc_bias, d_dec_bias


def solution(mesh):
    placed = (
        P("pair", "lat", None),
        P("pair", "lat", None),
        P("lat"),
        P("pair", "lat", None),
        P("pair", None),
        P("lat"),
        P("lat"),
    )
    return jax.shard_map(
        on_device,
        mesh=mesh,
        in_specs=placed,
        out_specs=(P("pair", "lat", None), P("pair", "lat", None), P("lat"), P("pair", None)),
        check_vma=False,
    )
```

time: 138 us -> 162 us (1.17)
  starting transfers between devices: 75.1 us -> 91.8 us
  local copies, waits for them, and re-layouts: 0.47 us -> 3.93 us
  Pallas kernels: 1.16 us -> 4.35 us
    ppermute x34 -> x33, starting transfers between devices: 73.5 us -> 90.2 us  [fetch(): return lax.ppermute(value, 'lat', pairs)]
    pallas_call x8 -> x9, Pallas kernels: 1.16 us -> 4.35 us  [pack(): pl.pallas_call(kernel, out_shape=jax.ShapeDtypeStruct((sum(rows), pieces[...]
    unnamed x11 -> x16, local copies, waits for them, and re-layouts: 0.04 us -> 2.93 us
    ppermute x34 -> x33, waiting for transfers between devices: 40.4 us -> 42.4 us  [fetch(): return lax.ppermute(value, 'lat', pairs)]
    dot_general x9 -> x7, matrix products: 10.2 us -> 9.72 us  [dot(): lax.dot_general(left, right, ((over[:1], over[1:]), ((), ())), preferred_...]
  transfers between devices with their start and end apart: 36 -> 35, of which waited for: 20 -> 18; matrix products, arithmetic and copies ran while one was open for 7% -> 7% of each run, Pallas kernels for 0% -> 1%
where the time goes in v3:
time: 162 us
  starting transfers between devices  91.8 us (57%)
  waiting for transfers between devices  44 us (27%)
  matrix products  9.72 us (6%)
  other arithmetic  6.73 us (4%)
  Pallas kernels  4.35 us (3%)
  local copies, waits for them, and re-layouts  3.93 us (2%)
  between operations  1.67 us (1%)
    ppermute x33, starting transfers between devices, fetch(): return lax.ppermute(value, 'lat', pairs)  90.2 us
    ppermute x33, waiting for transfers between devices, fetch(): return lax.ppermute(value, 'lat', pairs)  42.4 us
    dot_general x7, matrix products, dot(): lax.dot_general(left, right, ((over[:1], over[1:]), ((), ())), preferred_...  9.72 us
    pallas_call x9, Pallas kernels, pack(): pl.pallas_call(kernel, out_shape=jax.ShapeDtypeStruct((sum(rows), pieces[...  4.35 us
  transfers between devices with their start and end apart: 35, of which 18 were waited for; matrix products, arithmetic and copies ran while one was open for 7% of the time, Pallas kernels for 1%

profile of v3, /device:TPU:1, one launch (start us, length us, event | category | flops | bytes accessed | tf_op | source)
XLA Modules:
  0.0 162.2 jit_solution(11054196825817743028)
XLA Ops:
  0.7 6.3 %collective-permute-start.1 = (bf16[2,8192]{1,0:T(2,128)(2,1)}, bf16[2,8192]{1,0:T(2,128)(2,1)S(1)}, u32[]{:S(2)}, u32[]{:S(2)}) collective-permute-start(bf16[2,8192]{1,0:T(2,128)(2,1)} %bitcast.45), channel_id=1, source_target_pairs={{64,0},{11,1},{66,2},{9,3},{68,4},{15,5},{70,6},{13,7},{72,8},{3,9... | collective-permute-start | bytes 98312 | tf_op jit(solution)/shard_map/ppermute | solution.py:35
  8.8 2.1 %fusion.2 = f32[128]{0:T(128)S(1)} fusion(bf16[1,128,8192]{2,1,0:T(8,128)(2,1)} %param.11), kind=kLoop, calls=%fused_computation.6 | loop fusion | flops 3145600 | bytes 2097664 | tf_op jit(solution)/shard_map/reduce_sum | solution.py:122
  11.6 5.0 %collective-permute-start.11 = (f32[8,128]{1,0:T(8,128)S(1)}, f32[8,128]{1,0:T(8,128)S(1)}, u32[]{:S(2)}, u32[]{:S(2)}) collective-permute-start(f32[8,128]{1,0:T(8,128)S(1)} %pad_maximum_fusion.5), channel_id=1, source_target_pairs={{1,0},{0,1},{3,2},{2,3},{5,4},{4,5},{7,6},{6,7},{9,8},{8,9},{11,10... | collective-permute-start | bytes 12296 | tf_op jit(solution)/shard_map/ppermute | solution.py:35
  17.6 5.6 %collective-permute-done.3.refs_1_ = bf16[128,8192]{1,0:T(8,128)(2,1)} collective-permute-done((bf16[128,8192]{1,0:T(8,128)(2,1)}, bf16[128,8192]{1,0:T(8,128)(2,1)}, u32[]{:S(2)}, u32[]{:S(2)}) %collective-permute-start.3) | collective-permute-done | bytes 2097184 | tf_op jit(solution)/shard_map/ppermute | solution.py:35
  25.6 3.3 %collective-permute-start.4 = (bf16[8,8192]{1,0:T(8,128)(2,1)S(1)}, bf16[8,8192]{1,0:T(8,128)(2,1)S(1)}, u32[]{:S(2)}, u32[]{:S(2)}) collective-permute-start(bf16[8,8192]{1,0:T(8,128)(2,1)S(1)} %pad_maximum_fusion.1.refs_0_), channel_id=1, source_target_pairs={{10,0},{65,1},{8,2},{67,3},{14,4},{69,5},{12,6},{71,7},{2,8},{73,9... | collective-permute-start | bytes 393224 | tf_op jit(solution)/shard_map/ppermute | solution.py:35
  30.8 3.9 %collective-permute-done.4.refs_1_ = bf16[8,8192]{1,0:T(8,128)(2,1)S(1)} collective-permute-done((bf16[8,8192]{1,0:T(8,128)(2,1)S(1)}, bf16[8,8192]{1,0:T(8,128)(2,1)S(1)}, u32[]{:S(2)}, u32[]{:S(2)}) %collective-permute-start.4) | collective-permute-done | bytes 131104 | tf_op jit(solution)/shard_map/ppermute | solution.py:35
  37.3 4.2 %collective-permute-start.8 = (bf16[32,8192]{1,0:T(8,128)(2,1)S(1)}, bf16[32,8192]{1,0:T(8,128)(2,1)}, u32[]{:S(2)}, u32[]{:S(2)}) collective-permute-start(bf16[32,8192]{1,0:T(8,128)(2,1)S(1)} %shard_map.111.refs_0_), channel_id=1, source_target_pairs={{20,0},{125,1},{22,2},{127,3},{24,4},{113,5},{26,6},{115,7},{28,8}... | collective-permute-start | bytes 1572872 | tf_op jit(solution)/shard_map/ppermute | solution.py:35
  44.0 1.9 %shard_map.113 = bf16[256,8192]{1,0:T(8,128)(2,1)S(1)} custom-call(bf16[128,8192]{1,0:T(8,128)(2,1)S(1)} %bitcast.42, bf16[128,8192]{1,0:T(8,128)(2,1)} %collective-permute-done.3.refs_1_), custom_call_target="tpu_custom_call" | custom-call | tf_op jit(solution)/shard_map/pallas_call | solution.py:51
  46.7 6.8 %collective-permute-done.8.refs_1_ = bf16[32,8192]{1,0:T(8,128)(2,1)} collective-permute-done((bf16[32,8192]{1,0:T(8,128)(2,1)S(1)}, bf16[32,8192]{1,0:T(8,128)(2,1)}, u32[]{:S(2)}, u32[]{:S(2)}) %collective-permute-start.8) | collective-permute-done | bytes 524320 | tf_op jit(solution)/shard_map/ppermute | solution.py:35
  60.8 1.7 %collective-permute-start.13 = (bf16[32,8192]{1,0:T(8,128)(2,1)S(1)}, bf16[32,8192]{1,0:T(8,128)(2,1)S(1)}, u32[]{:S(2)}, u32[]{:S(2)}) collective-permute-start(bf16[32,8192]{1,0:T(8,128)(2,1)S(1)} %get-tuple-element.36), channel_id=1, source_target_pairs={{12,0},{5,1},{14,2},{7,3},{0,4},{9,5},{2,6},{11,7},{4,8},{13,9},{6... | collective-permute-start | bytes 1572872 | tf_op jit(solution)/shard_map/ppermute | solution.py:35
  64.1 1.7 %collective-permute-start.14 = (bf16[32,8192]{1,0:T(8,128)(2,1)S(1)}, bf16[32,8192]{1,0:T(8,128)(2,1)S(1)}, u32[]{:S(2)}, u32[]{:S(2)}) collective-permute-start(bf16[32,8192]{1,0:T(8,128)(2,1)S(1)} %get-tuple-element.38), channel_id=1, source_target_pairs={{112,0},{17,1},{114,2},{19,3},{116,4},{21,5},{118,6},{23,7},{120,8... | collective-permute-start | bytes 1572872 | tf_op jit(solution)/shard_map/ppermute | solution.py:35
  67.2 2.4 %collective-permute-start.22 = (bf16[128,8192]{1,0:T(8,128)(2,1)S(1)}, bf16[128,8192]{1,0:T(8,128)(2,1)S(1)}, u32[]{:S(2)}, u32[]{:S(2)}) collective-permute-start(bf16[128,8192]{1,0:T(8,128)(2,1)S(1)} %shard_map.112.refs_0_), channel_id=1, source_target_pairs={{1,0},{0,1},{3,2},{2,3},{5,4},{4,5},{7,6},{6,7},{9,8},{8,9},{11,10... | collective-permute-start | bytes 6291464 | tf_op jit(solution)/shard_map/ppermute | solution.py:35
  69.7 5.1 %collective-permute-done.13 = bf16[32,8192]{1,0:T(8,128)(2,1)S(1)} collective-permute-done((bf16[32,8192]{1,0:T(8,128)(2,1)S(1)}, bf16[32,8192]{1,0:T(8,128)(2,1)S(1)}, u32[]{:S(2)}, u32[]{:S(2)}) %collective-permute-start.13) | collective-permute-done | bytes 524320 | tf_op jit(solution)/shard_map/ppermute | solution.py:35
  74.8 1.8 %collective-permute-done.14 = bf16[32,8192]{1,0:T(8,128)(2,1)S(1)} collective-permute-done((bf16[32,8192]{1,0:T(8,128)(2,1)S(1)}, bf16[32,8192]{1,0:T(8,128)(2,1)S(1)}, u32[]{:S(2)}, u32[]{:S(2)}) %collective-permute-start.14) | collective-permute-done | bytes 524320 | tf_op jit(solution)/shard_map/ppermute | solution.py:35
  76.9 1.9 %collective-permute-start.16 = (bf16[8,8192]{1,0:T(8,128)(2,1)S(1)}, bf16[8,8192]{1,0:T(8,128)(2,1)S(1)}, u32[]{:S(2)}, u32[]{:S(2)}) collective-permute-start(bf16[8,8192]{1,0:T(8,128)(2,1)S(1)} %get-tuple-element.39), channel_id=1, source_target_pairs={{2,0},{97,1},{0,2},{99,3},{6,4},{101,5},{4,6},{103,7},{10,8},{105,... | collective-permute-start | bytes 393224 | tf_op jit(solution)/shard_map/ppermute | solution.py:35
  78.8 3.1 %collective-permute-start.18 = (bf16[8,8192]{1,0:T(8,128)(2,1)S(1)}, bf16[8,8192]{1,0:T(8,128)(2,1)S(1)}, u32[]{:S(2)}, u32[]{:S(2)}) collective-permute-start(bf16[8,8192]{1,0:T(8,128)(2,1)S(1)} %get-tuple-element.40), channel_id=1, source_target_pairs={{10,0},{65,1},{8,2},{67,3},{14,4},{69,5},{12,6},{71,7},{2,8},{73,9... | collective-permute-start | bytes 393224 | tf_op jit(solution)/shard_map/ppermute | solution.py:35
  81.9 2.0 %collective-permute-start.17 = (bf16[8,8192]{1,0:T(8,128)(2,1)S(1)}, bf16[8,8192]{1,0:T(8,128)(2,1)S(1)}, u32[]{:S(2)}, u32[]{:S(2)}) collective-permute-start(bf16[8,8192]{1,0:T(8,128)(2,1)S(1)} %get-tuple-element.41), channel_id=1, source_target_pairs={{8,0},{33,1},{10,2},{35,3},{12,4},{37,5},{14,6},{39,7},{0,8},{41,9... | collective-permute-start | bytes 393224 | tf_op jit(solution)/shard_map/ppermute | solution.py:35
  84.1 3.4 %collective-permute-done.18 = bf16[8,8192]{1,0:T(8,128)(2,1)S(1)} collective-permute-done((bf16[8,8192]{1,0:T(8,128)(2,1)S(1)}, bf16[8,8192]{1,0:T(8,128)(2,1)S(1)}, u32[]{:S(2)}, u32[]{:S(2)}) %collective-permute-start.18) | collective-permute-done | bytes 131104 | tf_op jit(solution)/shard_map/ppermute | solution.py:35
  88.2 3.9 %collective-permute-start.21 = (bf16[8,8192]{1,0:T(8,128)(2,1)S(1)}, bf16[8,8192]{1,0:T(8,128)(2,1)S(1)}, u32[]{:S(2)}, u32[]{:S(2)}) collective-permute-start(bf16[8,8192]{1,0:T(8,128)(2,1)S(1)} %fusion.7), channel_id=1, source_target_pairs={{32,0},{3,1},{34,2},{1,3},{36,4},{7,5},{38,6},{5,7},{40,8},{11,9},... | collective-permute-start | bytes 393224 | tf_op jit(solution)/shard_map/ppermute | solution.py:35
  95.9 4.0 %collective-permute-done.20 = bf16[8,8192]{1,0:T(8,128)(2,1)S(1)} collective-permute-done((bf16[8,8192]{1,0:T(8,128)(2,1)S(1)}, bf16[8,8192]{1,0:T(8,128)(2,1)S(1)}, u32[]{:S(2)}, u32[]{:S(2)}) %collective-permute-start.20) | collective-permute-done | bytes 131104 | tf_op jit(solution)/shard_map/ppermute | solution.py:35
  100.6 3.9 %collective-permute-start.26 = (bf16[8,8192]{1,0:T(8,128)(2,1)S(1)}, bf16[8,8192]{1,0:T(8,128)(2,1)S(1)}, u32[]{:S(2)}, u32[]{:S(2)}) collective-permute-start(bf16[8,8192]{1,0:T(8,128)(2,1)S(1)} %multiply_convert_fusion.refs_0_), channel_id=1, source_target_pairs={{2,0},{33,1},{0,2},{35,3},{6,4},{37,5},{4,6},{39,7},{10,8},{41,9},... | collective-permute-start | bytes 393224 | tf_op jit(solution)/shard_map/ppermute | solution.py:35
  104.7 3.2 %collective-permute-start.24 = (bf16[8,8192]{1,0:T(8,128)(2,1)S(1)}, bf16[8,8192]{1,0:T(8,128)(2,1)S(1)}, u32[]{:S(2)}, u32[]{:S(2)}) collective-permute-start(bf16[8,8192]{1,0:T(8,128)(2,1)S(1)} %multiply_convert_fusion.refs_0_), channel_id=1, source_target_pairs={{10,0},{65,1},{8,2},{67,3},{14,4},{69,5},{12,6},{71,7},{2,8},{73,9... | collective-permute-start | bytes 393224 | tf_op jit(solution)/shard_map/ppermute | solution.py:35
  108.0 2.7 %collective-permute-done.26.refs_3_ = bf16[8,8192]{1,0:T(8,128)(2,1)S(1)} collective-permute-done((bf16[8,8192]{1,0:T(8,128)(2,1)S(1)}, bf16[8,8192]{1,0:T(8,128)(2,1)S(1)}, u32[]{:S(2)}, u32[]{:S(2)}) %collective-permute-start.26) | collective-permute-done | bytes 131104 | tf_op jit(solution)/shard_map/ppermute | solution.py:35
  110.7 2.5 %collective-permute-done.25.refs_2_ = bf16[8,8192]{1,0:T(8,128)(2,1)S(1)} collective-permute-done((bf16[8,8192]{1,0:T(8,128)(2,1)S(1)}, bf16[8,8192]{1,0:T(8,128)(2,1)S(1)}, u32[]{:S(2)}, u32[]{:S(2)}) %collective-permute-start.25) | collective-permute-done | bytes 131104 | tf_op jit(solution)/shard_map/ppermute | solution.py:35
  114.7 2.1 %collective-permute-start.29 = (bf16[32,8192]{1,0:T(8,128)(2,1)S(1)}, bf16[32,8192]{1,0:T(8,128)(2,1)S(1)}, u32[]{:S(2)}, u32[]{:S(2)}) collective-permute-start(bf16[32,8192]{1,0:T(8,128)(2,1)S(1)} %shard_map.116.refs_0_), channel_id=1, source_target_pairs={{4,0},{13,1},{6,2},{15,3},{8,4},{1,5},{10,6},{3,7},{12,8},{5,9},{1... | collective-permute-start | bytes 1572872 | tf_op jit(solution)/shard_map/ppermute | solution.py:35
  116.8 3.6 %collective-permute-start.28 = (bf16[32,8192]{1,0:T(8,128)(2,1)S(1)}, bf16[32,8192]{1,0:T(8,128)(2,1)S(1)}, u32[]{:S(2)}, u32[]{:S(2)}) collective-permute-start(bf16[32,8192]{1,0:T(8,128)(2,1)S(1)} %shard_map.116.refs_0_), channel_id=1, source_target_pairs={{16,0},{113,1},{18,2},{115,3},{20,4},{117,5},{22,6},{119,7},{24,8}... | collective-permute-start | bytes 1572872 | tf_op jit(solution)/shard_map/ppermute | solution.py:35
  120.4 2.8 %collective-permute-start.27 = (bf16[32,8192]{1,0:T(8,128)(2,1)S(1)}, bf16[32,8192]{1,0:T(8,128)(2,1)S(1)}, u32[]{:S(2)}, u32[]{:S(2)}) collective-permute-start(bf16[32,8192]{1,0:T(8,128)(2,1)S(1)} %shard_map.116.refs_0_), channel_id=1, source_target_pairs={{20,0},{125,1},{22,2},{127,3},{24,4},{113,5},{26,6},{115,7},{28,8}... | collective-permute-start | bytes 1572872 | tf_op jit(solution)/shard_map/ppermute | solution.py:35
  123.1 18.3 %collective-permute-start.30 = (bf16[32,8192]{1,0:T(8,128)(2,1)S(1)}, bf16[32,8192]{1,0:T(8,128)(2,1)S(1)}, u32[]{:S(2)}, u32[]{:S(2)}) collective-permute-start(bf16[32,8192]{1,0:T(8,128)(2,1)S(1)} %shard_map.116.refs_0_), channel_id=1, source_target_pairs={{1,0},{0,1},{3,2},{2,3},{5,4},{4,5},{7,6},{6,7},{9,8},{8,9},{11,10... | collective-permute-start | bytes 1572872 | tf_op jit(solution)/shard_map/ppermute | solution.py:35
  141.4 4.4 %collective-permute-start.33 = (bf16[32,8192]{1,0:T(8,128)(2,1)S(1)}, bf16[32,8192]{1,0:T(8,128)(2,1)S(1)}, u32[]{:S(2)}, u32[]{:S(2)}) collective-permute-start(bf16[32,8192]{1,0:T(8,128)(2,1)S(1)} %collective-permute-done.29.refs_3_), channel_id=1, source_target_pairs={{1,0},{0,1},{3,2},{2,3},{5,4},{4,5},{7,6},{6,7},{9,8},{8,9},{11,10... | collective-permute-start | bytes 1572872 | tf_op jit(solution)/shard_map/ppermute | solution.py:35
  145.9 7.0 %collective-permute-start.31 = (bf16[32,8192]{1,0:T(8,128)(2,1)S(1)}, bf16[32,8192]{1,0:T(8,128)(2,1)S(1)}, u32[]{:S(2)}, u32[]{:S(2)}) collective-permute-start(bf16[32,8192]{1,0:T(8,128)(2,1)S(1)} %collective-permute-done.27.refs_1_), channel_id=1, source_target_pairs={{1,0},{0,1},{3,2},{2,3},{5,4},{4,5},{7,6},{6,7},{9,8},{8,9},{11,10... | collective-permute-start | bytes 1572872 | tf_op jit(solution)/shard_map/ppermute | solution.py:35
  155.7 2.6 %fusion = bf16[128,8192]{1,0:T(8,128)(2,1)} fusion(bf16[256,128]{1,0:T(8,128)(2,1)S(1)} %get-tuple-element.25, bf16[256,8192]{1,0:T(8,128)(2,1)S(1)} %shard_map.119, f32[128]{0:T(128)S(1)} %rsqrt_multiply_fusion, bf16[1,128,8192]{2,1,0:T(8,128)(2,1)S(1)} %copy-done), kind=kOutput, calls=%fused_computation.1 | convolution fusion | flops 541065216 | bytes 8454656 | tf_op jit(solution)/shard_map/dot_general | solution.py:109
  160.1 2.1 %fusion.1 = bf16[1,128,8192]{2,1,0:T(8,128)(2,1)} fusion(bf16[256,8192]{1,0:T(8,128)(2,1)S(1)} %shard_map.115, f32[256,128]{1,0:T(8,128)S(1)} %get-tuple-element.28, bf16[256,128]{1,0:T(8,128)(2,1)S(1)} %collective-permute-done.34, f32[128,128]{1,0:T(8,128)S(1)} %fusion.23, f32[128,128]{1,0:T(8,128)S(1)} %fusion.25, f32[128]{0:T(128)S(1)} %fusion.19), kind=kOutput, calls=%fused_computation.3 | convolution fusion | flops 538116096 | bytes 6619648 | tf_op jit(solution)/shard_map/dot_general | solution.py:109
  (108 shorter events, 35.4 us)
Async XLA Ops:
  0.7 16.1 %collective-permute-start.1 = (bf16[2,8192]{1,0:T(2,128)(2,1)}, bf16[2,8192]{1,0:T(2,128)(2,1)S(1)}, u32[]{:S(2)}, u32[]{:S(2)}) collective-permute-start(bf16[2,8192]{1,0:T(2,128)(2,1)} %bitcast.45), channel_id=1, source_target_pairs={{64,0},{11,1},{66,2},{9,3},{68,4},{15,5},{70,6},{13,7},{72,8},{3,9... | collective-permute-start | bytes 98312 | tf_op jit(solution)/shard_map/ppermute | solution.py:35
  7.0 10.2 %collective-permute-start.2 = (bf16[2,8192]{1,0:T(2,128)(2,1)}, bf16[2,8192]{1,0:T(2,128)(2,1)S(1)}, u32[]{:S(2)}, u32[]{:S(2)}) collective-permute-start(bf16[2,8192]{1,0:T(2,128)(2,1)} %bitcast.46), channel_id=1, source_target_pairs={{32,0},{3,1},{34,2},{1,3},{36,4},{7,5},{38,6},{5,7},{40,8},{11,9},... | collective-permute-start | bytes 98312 | tf_op jit(solution)/shard_map/ppermute | solution.py:35
  7.0 10.2 %collective-permute-start = (bf16[2,8192]{1,0:T(2,128)(2,1)}, bf16[2,8192]{1,0:T(2,128)(2,1)S(1)}, u32[]{:S(2)}, u32[]{:S(2)}) collective-permute-start(bf16[2,8192]{1,0:T(2,128)(2,1)} %bitcast.47), channel_id=1, source_target_pairs={{96,0},{9,1},{98,2},{11,3},{100,4},{13,5},{102,6},{15,7},{104,8},{... | collective-permute-start | bytes 98312 | tf_op jit(solution)/shard_map/ppermute | solution.py:35
  11.6 30.7 %collective-permute-start.11 = (f32[8,128]{1,0:T(8,128)S(1)}, f32[8,128]{1,0:T(8,128)S(1)}, u32[]{:S(2)}, u32[]{:S(2)}) collective-permute-start(f32[8,128]{1,0:T(8,128)S(1)} %pad_maximum_fusion.5), channel_id=1, source_target_pairs={{1,0},{0,1},{3,2},{2,3},{5,4},{4,5},{7,6},{6,7},{9,8},{8,9},{11,10... | collective-permute-start | bytes 12296 | tf_op jit(solution)/shard_map/ppermute | solution.py:35
  16.7 6.5 %collective-permute-start.3 = (bf16[128,8192]{1,0:T(8,128)(2,1)}, bf16[128,8192]{1,0:T(8,128)(2,1)}, u32[]{:S(2)}, u32[]{:S(2)}) collective-permute-start(bf16[128,8192]{1,0:T(8,128)(2,1)} %bitcast.41), channel_id=1, source_target_pairs={{1,0},{0,1},{3,2},{2,3},{5,4},{4,5},{7,6},{6,7},{9,8},{8,9},{11,10... | collective-permute-start | bytes 6291464 | tf_op jit(solution)/shard_map/ppermute | solution.py:35
  16.8 18.0 %collective-permute-start.7 = (bf16[128,8192]{1,0:T(8,128)(2,1)S(1)}, bf16[128,8192]{1,0:T(8,128)(2,1)S(1)}, u32[]{:S(2)}, u32[]{:S(2)}) collective-permute-start(bf16[128,8192]{1,0:T(8,128)(2,1)S(1)} %bitcast.39), channel_id=1, source_target_pairs={{1,0},{0,1},{3,2},{2,3},{5,4},{4,5},{7,6},{6,7},{9,8},{8,9},{11,10... | collective-permute-start | bytes 6291464 | tf_op jit(solution)/shard_map/ppermute | solution.py:35
  23.2 6.2 %collective-permute-start.6 = (bf16[8,8192]{1,0:T(8,128)(2,1)S(1)}, bf16[8,8192]{1,0:T(8,128)(2,1)S(1)}, u32[]{:S(2)}, u32[]{:S(2)}) collective-permute-start(bf16[8,8192]{1,0:T(8,128)(2,1)S(1)} %pad_maximum_fusion.1.refs_0_), channel_id=1, source_target_pairs={{2,0},{33,1},{0,2},{35,3},{6,4},{37,5},{4,6},{39,7},{10,8},{41,9},... | collective-permute-start | bytes 393224 | tf_op jit(solution)/shard_map/ppermute | solution.py:35
  24.3 6.5 %collective-permute-start.5 = (bf16[8,8192]{1,0:T(8,128)(2,1)S(1)}, bf16[8,8192]{1,0:T(8,128)(2,1)S(1)}, u32[]{:S(2)}, u32[]{:S(2)}) collective-permute-start(bf16[8,8192]{1,0:T(8,128)(2,1)S(1)} %pad_maximum_fusion.1.refs_0_), channel_id=1, source_target_pairs={{8,0},{97,1},{10,2},{99,3},{12,4},{101,5},{14,6},{103,7},{0,8},{10... | collective-permute-start | bytes 393224 | tf_op jit(solution)/shard_map/ppermute | solution.py:35
  25.6 9.1 %collective-permute-start.4 = (bf16[8,8192]{1,0:T(8,128)(2,1)S(1)}, bf16[8,8192]{1,0:T(8,128)(2,1)S(1)}, u32[]{:S(2)}, u32[]{:S(2)}) collective-permute-start(bf16[8,8192]{1,0:T(8,128)(2,1)S(1)} %pad_maximum_fusion.1.refs_0_), channel_id=1, source_target_pairs={{10,0},{65,1},{8,2},{67,3},{14,4},{69,5},{12,6},{71,7},{2,8},{73,9... | collective-permute-start | bytes 393224 | tf_op jit(solution)/shard_map/ppermute | solution.py:35
  36.1 9.8 %collective-permute-start.10 = (bf16[32,8192]{1,0:T(8,128)(2,1)S(1)}, bf16[32,8192]{1,0:T(8,128)(2,1)S(1)}, u32[]{:S(2)}, u32[]{:S(2)}) collective-permute-start(bf16[32,8192]{1,0:T(8,128)(2,1)S(1)} %shard_map.111.refs_0_), channel_id=1, source_target_pairs={{4,0},{13,1},{6,2},{15,3},{8,4},{1,5},{10,6},{3,7},{12,8},{5,9},{1... | collective-permute-start | bytes 1572872 | tf_op jit(solution)/shard_map/ppermute | solution.py:35
  37.3 9.4 %collective-permute-start.9 = (bf16[32,8192]{1,0:T(8,128)(2,1)S(1)}, bf16[32,8192]{1,0:T(8,128)(2,1)}, u32[]{:S(2)}, u32[]{:S(2)}) collective-permute-start(bf16[32,8192]{1,0:T(8,128)(2,1)S(1)} %shard_map.111.refs_0_), channel_id=1, source_target_pairs={{16,0},{113,1},{18,2},{115,3},{20,4},{117,5},{22,6},{119,7},{24,8}... | collective-permute-start | bytes 1572872 | tf_op jit(solution)/shard_map/ppermute | solution.py:35
  37.3 16.1 %collective-permute-start.8 = (bf16[32,8192]{1,0:T(8,128)(2,1)S(1)}, bf16[32,8192]{1,0:T(8,128)(2,1)}, u32[]{:S(2)}, u32[]{:S(2)}) collective-permute-start(bf16[32,8192]{1,0:T(8,128)(2,1)S(1)} %shard_map.111.refs_0_), channel_id=1, source_target_pairs={{20,0},{125,1},{22,2},{127,3},{24,4},{113,5},{26,6},{115,7},{28,8}... | collective-permute-start | bytes 1572872 | tf_op jit(solution)/shard_map/ppermute | solution.py:35
  60.8 14.0 %collective-permute-start.13 = (bf16[32,8192]{1,0:T(8,128)(2,1)S(1)}, bf16[32,8192]{1,0:T(8,128)(2,1)S(1)}, u32[]{:S(2)}, u32[]{:S(2)}) collective-permute-start(bf16[32,8192]{1,0:T(8,128)(2,1)S(1)} %get-tuple-element.36), channel_id=1, source_target_pairs={{12,0},{5,1},{14,2},{7,3},{0,4},{9,5},{2,6},{11,7},{4,8},{13,9},{6... | collective-permute-start | bytes 1572872 | tf_op jit(solution)/shard_map/ppermute | solution.py:35
  62.5 12.4 %collective-permute-start.15 = (bf16[32,8192]{1,0:T(8,128)(2,1)S(1)}, bf16[32,8192]{1,0:T(8,128)(2,1)S(1)}, u32[]{:S(2)}, u32[]{:S(2)}) collective-permute-start(bf16[32,8192]{1,0:T(8,128)(2,1)S(1)} %get-tuple-element.37), channel_id=1, source_target_pairs={{124,0},{21,1},{126,2},{23,3},{112,4},{25,5},{114,6},{27,7},{116,8... | collective-permute-start | bytes 1572872 | tf_op jit(solution)/shard_map/ppermute | solution.py:35
  64.1 12.5 %collective-permute-start.14 = (bf16[32,8192]{1,0:T(8,128)(2,1)S(1)}, bf16[32,8192]{1,0:T(8,128)(2,1)S(1)}, u32[]{:S(2)}, u32[]{:S(2)}) collective-permute-start(bf16[32,8192]{1,0:T(8,128)(2,1)S(1)} %get-tuple-element.38), channel_id=1, source_target_pairs={{112,0},{17,1},{114,2},{19,3},{116,4},{21,5},{118,6},{23,7},{120,8... | collective-permute-start | bytes 1572872 | tf_op jit(solution)/shard_map/ppermute | solution.py:35
  67.2 33.1 %collective-permute-start.22 = (bf16[128,8192]{1,0:T(8,128)(2,1)S(1)}, bf16[128,8192]{1,0:T(8,128)(2,1)S(1)}, u32[]{:S(2)}, u32[]{:S(2)}) collective-permute-start(bf16[128,8192]{1,0:T(8,128)(2,1)S(1)} %shard_map.112.refs_0_), channel_id=1, source_target_pairs={{1,0},{0,1},{3,2},{2,3},{5,4},{4,5},{7,6},{6,7},{9,8},{8,9},{11,10... | collective-permute-start | bytes 6291464 | tf_op jit(solution)/shard_map/ppermute | solution.py:35
  69.6 14.3 %collective-permute-start.23 = (f32[128,128]{1,0:T(8,128)S(1)}, f32[128,128]{1,0:T(8,128)S(1)}, u32[]{:S(2)}, u32[]{:S(2)}) collective-permute-start(f32[128,128]{1,0:T(8,128)S(1)} %get-tuple-element.44), channel_id=1, source_target_pairs={{1,0},{0,1},{3,2},{2,3},{5,4},{4,5},{7,6},{6,7},{9,8},{8,9},{11,10... | collective-permute-start | bytes 196616 | tf_op jit(solution)/shard_map/ppermute | solution.py:35
  76.9 7.2 %collective-permute-start.16 = (bf16[8,8192]{1,0:T(8,128)(2,1)S(1)}, bf16[8,8192]{1,0:T(8,128)(2,1)S(1)}, u32[]{:S(2)}, u32[]{:S(2)}) collective-permute-start(bf16[8,8192]{1,0:T(8,128)(2,1)S(1)} %get-tuple-element.39), channel_id=1, source_target_pairs={{2,0},{97,1},{0,2},{99,3},{6,4},{101,5},{4,6},{103,7},{10,8},{105,... | collective-permute-start | bytes 393224 | tf_op jit(solution)/shard_map/ppermute | solution.py:35
  78.8 8.7 %collective-permute-start.18 = (bf16[8,8192]{1,0:T(8,128)(2,1)S(1)}, bf16[8,8192]{1,0:T(8,128)(2,1)S(1)}, u32[]{:S(2)}, u32[]{:S(2)}) collective-permute-start(bf16[8,8192]{1,0:T(8,128)(2,1)S(1)} %get-tuple-element.40), channel_id=1, source_target_pairs={{10,0},{65,1},{8,2},{67,3},{14,4},{69,5},{12,6},{71,7},{2,8},{73,9... | collective-permute-start | bytes 393224 | tf_op jit(solution)/shard_map/ppermute | solution.py:35
  88.2 7.7 %collective-permute-start.21 = (bf16[8,8192]{1,0:T(8,128)(2,1)S(1)}, bf16[8,8192]{1,0:T(8,128)(2,1)S(1)}, u32[]{:S(2)}, u32[]{:S(2)}) collective-permute-start(bf16[8,8192]{1,0:T(8,128)(2,1)S(1)} %fusion.7), channel_id=1, source_target_pairs={{32,0},{3,1},{34,2},{1,3},{36,4},{7,5},{38,6},{5,7},{40,8},{11,9},... | collective-permute-start | bytes 393224 | tf_op jit(solution)/shard_map/ppermute | solution.py:35
  92.1 7.7 %collective-permute-start.20 = (bf16[8,8192]{1,0:T(8,128)(2,1)S(1)}, bf16[8,8192]{1,0:T(8,128)(2,1)S(1)}, u32[]{:S(2)}, u32[]{:S(2)}) collective-permute-start(bf16[8,8192]{1,0:T(8,128)(2,1)S(1)} %fusion.7), channel_id=1, source_target_pairs={{64,0},{11,1},{66,2},{9,3},{68,4},{15,5},{70,6},{13,7},{72,8},{3,9... | collective-permute-start | bytes 393224 | tf_op jit(solution)/shard_map/ppermute | solution.py:35
  93.2 6.8 %collective-permute-start.19 = (bf16[8,8192]{1,0:T(8,128)(2,1)S(1)}, bf16[8,8192]{1,0:T(8,128)(2,1)S(1)}, u32[]{:S(2)}, u32[]{:S(2)}) collective-permute-start(bf16[8,8192]{1,0:T(8,128)(2,1)S(1)} %fusion.7), channel_id=1, source_target_pairs={{96,0},{9,1},{98,2},{11,3},{100,4},{13,5},{102,6},{15,7},{104,8},{... | collective-permute-start | bytes 393224 | tf_op jit(solution)/shard_map/ppermute | solution.py:35
  100.6 10.1 %collective-permute-start.26 = (bf16[8,8192]{1,0:T(8,128)(2,1)S(1)}, bf16[8,8192]{1,0:T(8,128)(2,1)S(1)}, u32[]{:S(2)}, u32[]{:S(2)}) collective-permute-start(bf16[8,8192]{1,0:T(8,128)(2,1)S(1)} %multiply_convert_fusion.refs_0_), channel_id=1, source_target_pairs={{2,0},{33,1},{0,2},{35,3},{6,4},{37,5},{4,6},{39,7},{10,8},{41,9},... | collective-permute-start | bytes 393224 | tf_op jit(solution)/shard_map/ppermute | solution.py:35
  104.5 8.6 %collective-permute-start.25 = (bf16[8,8192]{1,0:T(8,128)(2,1)S(1)}, bf16[8,8192]{1,0:T(8,128)(2,1)S(1)}, u32[]{:S(2)}, u32[]{:S(2)}) collective-permute-start(bf16[8,8192]{1,0:T(8,128)(2,1)S(1)} %multiply_convert_fusion.refs_0_), channel_id=1, source_target_pairs={{8,0},{97,1},{10,2},{99,3},{12,4},{101,5},{14,6},{103,7},{0,8},{10... | collective-permute-start | bytes 393224 | tf_op jit(solution)/shard_map/ppermute | solution.py:35
  104.7 9.9 %collective-permute-start.24 = (bf16[8,8192]{1,0:T(8,128)(2,1)S(1)}, bf16[8,8192]{1,0:T(8,128)(2,1)S(1)}, u32[]{:S(2)}, u32[]{:S(2)}) collective-permute-start(bf16[8,8192]{1,0:T(8,128)(2,1)S(1)} %multiply_convert_fusion.refs_0_), channel_id=1, source_target_pairs={{10,0},{65,1},{8,2},{67,3},{14,4},{69,5},{12,6},{71,7},{2,8},{73,9... | collective-permute-start | bytes 393224 | tf_op jit(solution)/shard_map/ppermute | solution.py:35
  114.7 26.8 %collective-permute-start.29 = (bf16[32,8192]{1,0:T(8,128)(2,1)S(1)}, bf16[32,8192]{1,0:T(8,128)(2,1)S(1)}, u32[]{:S(2)}, u32[]{:S(2)}) collective-permute-start(bf16[32,8192]{1,0:T(8,128)(2,1)S(1)} %shard_map.116.refs_0_), channel_id=1, source_target_pairs={{4,0},{13,1},{6,2},{15,3},{8,4},{1,5},{10,6},{3,7},{12,8},{5,9},{1... | collective-permute-start | bytes 1572872 | tf_op jit(solution)/shard_map/ppermute | solution.py:35
  116.8 29.1 %collective-permute-start.28 = (bf16[32,8192]{1,0:T(8,128)(2,1)S(1)}, bf16[32,8192]{1,0:T(8,128)(2,1)S(1)}, u32[]{:S(2)}, u32[]{:S(2)}) collective-permute-start(bf16[32,8192]{1,0:T(8,128)(2,1)S(1)} %shard_map.116.refs_0_), channel_id=1, source_target_pairs={{16,0},{113,1},{18,2},{115,3},{20,4},{117,5},{22,6},{119,7},{24,8}... | collective-permute-start | bytes 1572872 | tf_op jit(solution)/shard_map/ppermute | solution.py:35
  120.4 25.5 %collective-permute-start.27 = (bf16[32,8192]{1,0:T(8,128)(2,1)S(1)}, bf16[32,8192]{1,0:T(8,128)(2,1)S(1)}, u32[]{:S(2)}, u32[]{:S(2)}) collective-permute-start(bf16[32,8192]{1,0:T(8,128)(2,1)S(1)} %shard_map.116.refs_0_), channel_id=1, source_target_pairs={{20,0},{125,1},{22,2},{127,3},{24,4},{113,5},{26,6},{115,7},{28,8}... | collective-permute-start | bytes 1572872 | tf_op jit(solution)/shard_map/ppermute | solution.py:35
  123.1 30.6 %collective-permute-start.30 = (bf16[32,8192]{1,0:T(8,128)(2,1)S(1)}, bf16[32,8192]{1,0:T(8,128)(2,1)S(1)}, u32[]{:S(2)}, u32[]{:S(2)}) collective-permute-start(bf16[32,8192]{1,0:T(8,128)(2,1)S(1)} %shard_map.116.refs_0_), channel_id=1, source_target_pairs={{1,0},{0,1},{3,2},{2,3},{5,4},{4,5},{7,6},{6,7},{9,8},{8,9},{11,10... | collective-permute-start | bytes 1572872 | tf_op jit(solution)/shard_map/ppermute | solution.py:35
  141.4 12.3 %collective-permute-start.33 = (bf16[32,8192]{1,0:T(8,128)(2,1)S(1)}, bf16[32,8192]{1,0:T(8,128)(2,1)S(1)}, u32[]{:S(2)}, u32[]{:S(2)}) collective-permute-start(bf16[32,8192]{1,0:T(8,128)(2,1)S(1)} %collective-permute-done.29.refs_3_), channel_id=1, source_target_pairs={{1,0},{0,1},{3,2},{2,3},{5,4},{4,5},{7,6},{6,7},{9,8},{8,9},{11,10... | collective-permute-start | bytes 1572872 | tf_op jit(solution)/shard_map/ppermute | solution.py:35
  145.8 8.0 %collective-permute-start.32 = (bf16[32,8192]{1,0:T(8,128)(2,1)S(1)}, bf16[32,8192]{1,0:T(8,128)(2,1)S(1)}, u32[]{:S(2)}, u32[]{:S(2)}) collective-permute-start(bf16[32,8192]{1,0:T(8,128)(2,1)S(1)} %collective-permute-done.28.refs_2_), channel_id=1, source_target_pairs={{1,0},{0,1},{3,2},{2,3},{5,4},{4,5},{7,6},{6,7},{9,8},{8,9},{11,10... | collective-permute-start | bytes 1572872 | tf_op jit(solution)/shard_map/ppermute | solution.py:35
  145.9 8.5 %collective-permute-start.31 = (bf16[32,8192]{1,0:T(8,128)(2,1)S(1)}, bf16[32,8192]{1,0:T(8,128)(2,1)S(1)}, u32[]{:S(2)}, u32[]{:S(2)}) collective-permute-start(bf16[32,8192]{1,0:T(8,128)(2,1)S(1)} %collective-permute-done.27.refs_1_), channel_id=1, source_target_pairs={{1,0},{0,1},{3,2},{2,3},{5,4},{4,5},{7,6},{6,7},{9,8},{8,9},{11,10... | collective-permute-start | bytes 1572872 | tf_op jit(solution)/shard_map/ppermute | solution.py:35
  (11 other events, 145.8 us)

commit v4 on v2

--- a/solution.py
+++ b/solution.py
@@ -72,10 +72,13 @@
 AROUND = (((0, 1, 0), (0, -1, 0)), ((1, 0, 0), (-1, 0, 0)), ((1, 1, 0), (-1, -1, 0)))
 
 
-def gather_rows(octet):
+def gather_rows(octet, beside):
     group = pack([octet] + [fetch(octet, EVEN_XY[k], EVEN_Z[k]) for k in (1, 2, 3)])
     groups = [group] + [fetch(group, *to) for to in AROUND]
-    return groups + [swap_core(each) for each in groups]
+    others = [swap_core(each) for each in groups]
+    half = beside([groups[0], groups[3], others[0], others[3]])
+    others[1], half = lax.optimization_barrier((others[1], half))
+    return groups + others, half
 
 
 def low(value):
@@ -91,11 +94,13 @@
     theirs = low(dot(latent[rows:], dec, (1, 0)))
     mine = dot(latent[:rows], dec, (1, 0))
     sent = low(add(mine[96:], swap_core(theirs[96:])))
-    theirs, sent = lax.optimization_barrier((theirs[:96], sent))
-    rest = add(mine[:96], swap_core(theirs))
-    group = add(rest[:32], fetch(sent, *AROUND[2][::-1]))
-    group = add(group, fetch(low(rest[64:]), *AROUND[1][::-1]))
-    group = add(group, fetch(low(rest[32:64]), *AROUND[0][::-1]))
+    next_to, _ = lax.optimization_barrier((swap_core(theirs[32:96]), sent))
+    last, next_to = lax.optimization_barrier((theirs[:32], next_to))
+    rest = add(mine[32:96], next_to)
+    group = add(mine[:32], swap_core(last))
+    group = add(group, fetch(sent, *AROUND[2][::-1]))
+    group = add(group, fetch(low(rest[32:]), *AROUND[1][::-1]))
+    group = add(group, fetch(low(rest[:32]), *AROUND[0][::-1]))
     octet = group[0:8]
     for k, back in ((3, 3), (2, 1), (1, 2)):
         octet = add(octet, fetch(low(group[8 * k : 8 * k + 8]), EVEN_XY[k], EVEN_Z[back]))
@@ -111,13 +116,18 @@
     return lax.dot_general(left, right, ((over[:1], over[1:]), ((), ())), preferred_element_type=jnp.float32)
 
 
+def total_rows(groups):
+    rows = pack(groups)
+    return dot(jnp.ones((8, rows.shape[0]), rows.dtype), rows, (1, 0))[0:1]
+
+
 def on_device(activations, enc_weight, enc_bias, dec_weight, dec_bias, block_list, block_count):
     enc, dec = enc_weight[0], dec_weight[0]
     own = activations[0]
     tokens = 2 * BLK
+    own_octet = jnp.concatenate(by_partner(own), axis=0)
     norm_own = jnp.sqrt(jnp.sum(jnp.square(dec.astype(jnp.float32)), axis=1) + epsilon)
-    own_octet = jnp.concatenate(by_partner(own), axis=0)
-    act_groups = gather_rows(own_octet)
+    act_groups, norm_own = gather_rows(own_octet, lambda _: norm_own)
 
     slots = jnp.arange(block_list.shape[0], dtype=jnp.int32) < block_count[0]
     z, _, _, core = position()
@@ -139,21 +149,18 @@
     latent_low = low(latent_act)
 
     rebuilt = scatter_rows(latent_low, dec) + dec_bias
-    err_groups = gather_rows(low(loss_scale * (rebuilt - own_octet.astype(jnp.float32))))
+    slope = loss_scale * sparsity * jnp.sum(latent_act, axis=0) / norm_own
+    factor, slope = lax.optimization_barrier((jax.nn.sigmoid(pre_act) * live, slope))
+    err_groups, bias_part = gather_rows(low(loss_scale * (rebuilt - own_octet.astype(jnp.float32))), total_rows)
 
     err_halves = [pack(err_groups[:4]), pack(err_groups[4:])]
     grad_part = jnp.concatenate([dot(half, dec, (1, 1)) for half in err_halves], axis=0)
     err = pack(err_halves)
-    act_total = jnp.sum(latent_act, axis=0)
-    d_dec = dot(latent_low, err, (0, 0))
-    d_dec = d_dec + (loss_scale * sparsity * act_total / norm_own)[:, None] * dec.astype(jnp.float32)
-    d_dec_bias = dot(jnp.ones((8, tokens), jnp.bfloat16), err, (1, 0))[0:1]
+    d_dec = dot(latent_low, err, (0, 0)) + slope[:, None] * dec.astype(jnp.float32)
+    d_dec_bias = bias_part + total_rows([err_groups[k] for k in (1, 2, 5, 6)])
     arrived, d_dec, d_dec_bias = lax.optimization_barrier((swap_pair(low(grad_part)), low(d_dec), d_dec_bias))
-    grad_sum = add(grad_part, arrived)
-    grad_latent = (grad_sum + loss_scale * sparsity * norm_sum) * live
-    pre_grad = grad_latent * jax.nn.sigmoid(pre_act)
+    pre_grad = (add(grad_part, arrived) + loss_scale * sparsity * norm_sum) * factor
     pre_low = low(pre_grad)
-
     d_enc = dot(pre_low, act, (0, 0))
     d_enc_bias = jnp.sum(pre_grad, axis=0)
     return low(d_enc)[None], d_dec[None], d_enc_bias, d_dec_bias

time: 138 us -> 138 us (level)
    ppermute x34 -> x35, starting transfers between devices: 73.5 us -> 72.6 us  [fetch(): return lax.ppermute(value, 'lat', pairs)]
    ppermute x34 -> x35, waiting for transfers between devices: 40.4 us -> 41 us  [fetch(): return lax.ppermute(value, 'lat', pairs)]
    dot_general x9 -> x10, matrix products: 10.2 us -> 9.69 us  [dot(): lax.dot_general(left, right, ((over[:1], over[1:]), ((), ())), preferred_...]
  transfers between devices with their start and end apart: 36 -> 37, of which waited for: 20 -> 19; matrix products, arithmetic and copies ran while one was open for 7% -> 7% of each run, Pallas kernels for 0% -> 1%
where the time goes in v4:
time: 138 us; the launch traced here: 137 us
  starting transfers between devices  74.2 us (54%)
  waiting for transfers between devices  43.4 us (31%)
  matrix products  9.69 us (7%)
  other arithmetic  6.56 us (5%)
  between operations  1.64 us (1%)
  Pallas kernels  1.43 us (1%)
    ppermute x35, starting transfers between devices, fetch(): return lax.ppermute(value, 'lat', pairs)  72.6 us
    ppermute x35, waiting for transfers between devices, fetch(): return lax.ppermute(value, 'lat', pairs)  41 us
    dot_general x10, matrix products, dot(): lax.dot_general(left, right, ((over[:1], over[1:]), ((), ())), preferred_...  9.69 us
  transfers between devices with their start and end apart: 37, of which 19 were waited for; matrix products, arithmetic and copies ran while one was open for 7% of the time, Pallas kernels for 1%

profile of v4, /device:TPU:1, one launch (start us, length us, event | category | flops | bytes accessed | tf_op | source)
XLA Modules:
  0.0 137.3 jit_solution(6496102176136265806)
XLA Ops:
  0.6 6.3 %collective-permute-start.1 = (bf16[2,8192]{1,0:T(2,128)(2,1)}, bf16[2,8192]{1,0:T(2,128)(2,1)S(1)}, u32[]{:S(2)}, u32[]{:S(2)}) collective-permute-start(bf16[2,8192]{1,0:T(2,128)(2,1)} %bitcast.40), channel_id=1, source_target_pairs={{64,0},{11,1},{66,2},{9,3},{68,4},{15,5},{70,6},{13,7},{72,8},{3,9... | collective-permute-start | bytes 98312 | tf_op jit(solution)/shard_map/ppermute | solution.py:35
  8.8 2.8 %collective-permute-done.2 = bf16[2,8192]{1,0:T(2,128)(2,1)S(1)} collective-permute-done((bf16[2,8192]{1,0:T(2,128)(2,1)}, bf16[2,8192]{1,0:T(2,128)(2,1)S(1)}, u32[]{:S(2)}, u32[]{:S(2)}) %collective-permute-start.2) | collective-permute-done | bytes 32800 | tf_op jit(solution)/shard_map/ppermute | solution.py:35
  12.8 6.9 %collective-permute-start.5 = (bf16[8,8192]{1,0:T(8,128)(2,1)S(1)}, bf16[8,8192]{1,0:T(8,128)(2,1)S(1)}, u32[]{:S(2)}, u32[]{:S(2)}) collective-permute-start(bf16[8,8192]{1,0:T(8,128)(2,1)S(1)} %pad_maximum_fusion.1.refs_0_), channel_id=1, source_target_pairs={{10,0},{65,1},{8,2},{67,3},{14,4},{69,5},{12,6},{71,7},{2,8},{73,9... | collective-permute-start | bytes 393224 | tf_op jit(solution)/shard_map/ppermute | solution.py:35
  20.8 2.4 %collective-permute-start.3 = (bf16[8,8192]{1,0:T(8,128)(2,1)S(1)}, bf16[8,8192]{1,0:T(8,128)(2,1)S(1)}, u32[]{:S(2)}, u32[]{:S(2)}) collective-permute-start(bf16[8,8192]{1,0:T(8,128)(2,1)S(1)} %pad_maximum_fusion.1.refs_0_), channel_id=1, source_target_pairs={{2,0},{33,1},{0,2},{35,3},{6,4},{37,5},{4,6},{39,7},{10,8},{41,9},... | collective-permute-start | bytes 393224 | tf_op jit(solution)/shard_map/ppermute | solution.py:35
  23.4 2.9 %collective-permute-done.4.refs_2_ = bf16[8,8192]{1,0:T(8,128)(2,1)S(1)} collective-permute-done((bf16[8,8192]{1,0:T(8,128)(2,1)S(1)}, bf16[8,8192]{1,0:T(8,128)(2,1)S(1)}, u32[]{:S(2)}, u32[]{:S(2)}) %collective-permute-start.4) | collective-permute-done | bytes 131104 | tf_op jit(solution)/shard_map/ppermute | solution.py:35
  28.9 2.1 %fusion.2 = f32[128]{0:T(128)S(1)} fusion(bf16[1,128,8192]{2,1,0:T(8,128)(2,1)} %param.11), kind=kLoop, calls=%fused_computation.7 | loop fusion | flops 3145600 | bytes 2097664 | tf_op jit(solution)/shard_map/reduce_sum | solution.py:129
  31.0 6.0 %collective-permute-start.9 = (bf16[32,8192]{1,0:T(8,128)(2,1)S(1)}, bf16[32,8192]{1,0:T(8,128)(2,1)S(1)}, u32[]{:S(2)}, u32[]{:S(2)}) collective-permute-start(bf16[32,8192]{1,0:T(8,128)(2,1)S(1)} %shard_map.111.refs_0_), channel_id=1, source_target_pairs={{1,0},{0,1},{3,2},{2,3},{5,4},{4,5},{7,6},{6,7},{9,8},{8,9},{11,10... | collective-permute-start | bytes 1572872 | tf_op jit(solution)/shard_map/ppermute | solution.py:35
  38.5 1.7 %collective-permute-start.12 = (bf16[32,8192]{1,0:T(8,128)(2,1)S(1)}, bf16[32,8192]{1,0:T(8,128)(2,1)S(1)}, u32[]{:S(2)}, u32[]{:S(2)}) collective-permute-start(bf16[32,8192]{1,0:T(8,128)(2,1)S(1)} %collective-permute-done.8.refs_3_), channel_id=1, source_target_pairs={{1,0},{0,1},{3,2},{2,3},{5,4},{4,5},{7,6},{6,7},{9,8},{8,9},{11,10... | collective-permute-start | bytes 1572872 | tf_op jit(solution)/shard_map/ppermute | solution.py:35
  40.2 2.0 %collective-permute-done.7.refs_2_ = bf16[32,8192]{1,0:T(8,128)(2,1)S(1)} collective-permute-done((bf16[32,8192]{1,0:T(8,128)(2,1)S(1)}, bf16[32,8192]{1,0:T(8,128)(2,1)S(1)}, u32[]{:S(2)}, u32[]{:S(2)}) %collective-permute-start.7) | collective-permute-done | bytes 524320 | tf_op jit(solution)/shard_map/ppermute | solution.py:35
  42.2 4.5 %collective-permute-start.11 = (bf16[32,8192]{1,0:T(8,128)(2,1)S(1)}, bf16[32,8192]{1,0:T(8,128)(2,1)S(1)}, u32[]{:S(2)}, u32[]{:S(2)}) collective-permute-start(bf16[32,8192]{1,0:T(8,128)(2,1)S(1)} %collective-permute-done.7.refs_2_), channel_id=1, source_target_pairs={{1,0},{0,1},{3,2},{2,3},{5,4},{4,5},{7,6},{6,7},{9,8},{8,9},{11,10... | collective-permute-start | bytes 1572872 | tf_op jit(solution)/shard_map/ppermute | solution.py:35
  51.0 2.3 %collective-permute-done.13 = bf16[264,128]{1,0:T(8,128)(2,1)S(1)} collective-permute-done((bf16[264,128]{1,0:T(8,128)(2,1)S(1)}, bf16[264,128]{1,0:T(8,128)(2,1)S(1)}, u32[]{:S(2)}, u32[]{:S(2)}) %collective-permute-start.13) | collective-permute-done | bytes 67616 | tf_op jit(solution)/shard_map/ppermute | solution.py:112
  54.3 1.6 %collective-permute-start.15 = (bf16[32,8192]{1,0:T(8,128)(2,1)S(1)}, bf16[32,8192]{1,0:T(8,128)(2,1)S(1)}, u32[]{:S(2)}, u32[]{:S(2)}) collective-permute-start(bf16[32,8192]{1,0:T(8,128)(2,1)S(1)} %get-tuple-element.34), channel_id=1, source_target_pairs={{1,0},{0,1},{3,2},{2,3},{5,4},{4,5},{7,6},{6,7},{9,8},{8,9},{11,10... | collective-permute-start | bytes 1572872 | tf_op jit(solution)/shard_map/ppermute | solution.py:35
  57.5 3.9 %collective-permute-start.17 = (bf16[32,8192]{1,0:T(8,128)(2,1)S(1)}, bf16[32,8192]{1,0:T(8,128)(2,1)S(1)}, u32[]{:S(2)}, u32[]{:S(2)}) collective-permute-start(bf16[32,8192]{1,0:T(8,128)(2,1)S(1)} %fusion.15), channel_id=1, source_target_pairs={{124,0},{21,1},{126,2},{23,3},{112,4},{25,5},{114,6},{27,7},{116,8... | collective-permute-start | bytes 1572872 | tf_op jit(solution)/shard_map/ppermute | solution.py:35
  63.7 3.8 %collective-permute-done.17 = bf16[32,8192]{1,0:T(8,128)(2,1)S(1)} collective-permute-done((bf16[32,8192]{1,0:T(8,128)(2,1)S(1)}, bf16[32,8192]{1,0:T(8,128)(2,1)S(1)}, u32[]{:S(2)}, u32[]{:S(2)}) %collective-permute-start.17) | collective-permute-done | bytes 524320 | tf_op jit(solution)/shard_map/ppermute | solution.py:35
  67.6 5.6 %collective-permute-done.18 = bf16[32,8192]{1,0:T(8,128)(2,1)S(1)} collective-permute-done((bf16[32,8192]{1,0:T(8,128)(2,1)S(1)}, bf16[32,8192]{1,0:T(8,128)(2,1)S(1)}, u32[]{:S(2)}, u32[]{:S(2)}) %collective-permute-start.18) | collective-permute-done | bytes 524320 | tf_op jit(solution)/shard_map/ppermute | solution.py:35
  73.5 4.5 %collective-permute-start.20 = (bf16[8,8192]{1,0:T(8,128)(2,1)S(1)}, bf16[8,8192]{1,0:T(8,128)(2,1)S(1)}, u32[]{:S(2)}, u32[]{:S(2)}) collective-permute-start(bf16[8,8192]{1,0:T(8,128)(2,1)S(1)} %get-tuple-element.38), channel_id=1, source_target_pairs={{10,0},{65,1},{8,2},{67,3},{14,4},{69,5},{12,6},{71,7},{2,8},{73,9... | collective-permute-start | bytes 393224 | tf_op jit(solution)/shard_map/ppermute | solution.py:35
  78.1 3.6 %collective-permute-start.21 = (bf16[8,8192]{1,0:T(8,128)(2,1)S(1)}, bf16[8,8192]{1,0:T(8,128)(2,1)S(1)}, u32[]{:S(2)}, u32[]{:S(2)}) collective-permute-start(bf16[8,8192]{1,0:T(8,128)(2,1)S(1)} %get-tuple-element.40), channel_id=1, source_target_pairs={{8,0},{33,1},{10,2},{35,3},{12,4},{37,5},{14,6},{39,7},{0,8},{41,9... | collective-permute-start | bytes 393224 | tf_op jit(solution)/shard_map/ppermute | solution.py:35
  81.6 2.7 %collective-permute-done.22 = bf16[8,8192]{1,0:T(8,128)(2,1)S(1)} collective-permute-done((bf16[8,8192]{1,0:T(8,128)(2,1)S(1)}, bf16[8,8192]{1,0:T(8,128)(2,1)S(1)}, u32[]{:S(2)}, u32[]{:S(2)}) %collective-permute-start.22) | collective-permute-done | bytes 131104 | tf_op jit(solution)/shard_map/ppermute | solution.py:35
  84.4 2.1 %collective-permute-done.21 = bf16[8,8192]{1,0:T(8,128)(2,1)S(1)} collective-permute-done((bf16[8,8192]{1,0:T(8,128)(2,1)S(1)}, bf16[8,8192]{1,0:T(8,128)(2,1)S(1)}, u32[]{:S(2)}, u32[]{:S(2)}) %collective-permute-start.21) | collective-permute-done | bytes 131104 | tf_op jit(solution)/shard_map/ppermute | solution.py:35
  87.2 2.5 %collective-permute-start.24 = (bf16[8,8192]{1,0:T(8,128)(2,1)S(1)}, bf16[8,8192]{1,0:T(8,128)(2,1)S(1)}, u32[]{:S(2)}, u32[]{:S(2)}) collective-permute-start(bf16[8,8192]{1,0:T(8,128)(2,1)S(1)} %fusion.21), channel_id=1, source_target_pairs={{64,0},{11,1},{66,2},{9,3},{68,4},{15,5},{70,6},{13,7},{72,8},{3,9... | collective-permute-start | bytes 393224 | tf_op jit(solution)/shard_map/ppermute | solution.py:35
  89.6 2.6 %collective-permute-start.23 = (bf16[8,8192]{1,0:T(8,128)(2,1)S(1)}, bf16[8,8192]{1,0:T(8,128)(2,1)S(1)}, u32[]{:S(2)}, u32[]{:S(2)}) collective-permute-start(bf16[8,8192]{1,0:T(8,128)(2,1)S(1)} %fusion.21), channel_id=1, source_target_pairs={{96,0},{9,1},{98,2},{11,3},{100,4},{13,5},{102,6},{15,7},{104,8},{... | collective-permute-start | bytes 393224 | tf_op jit(solution)/shard_map/ppermute | solution.py:35
  92.3 2.6 %collective-permute-done.24 = bf16[8,8192]{1,0:T(8,128)(2,1)S(1)} collective-permute-done((bf16[8,8192]{1,0:T(8,128)(2,1)S(1)}, bf16[8,8192]{1,0:T(8,128)(2,1)S(1)}, u32[]{:S(2)}, u32[]{:S(2)}) %collective-permute-start.24) | collective-permute-done | bytes 131104 | tf_op jit(solution)/shard_map/ppermute | solution.py:35
  96.5 3.7 %collective-permute-start.28 = (bf16[8,8192]{1,0:T(8,128)(2,1)S(1)}, bf16[8,8192]{1,0:T(8,128)(2,1)S(1)}, u32[]{:S(2)}, u32[]{:S(2)}) collective-permute-start(bf16[8,8192]{1,0:T(8,128)(2,1)S(1)} %multiply_convert_fusion.refs_0_), channel_id=1, source_target_pairs={{10,0},{65,1},{8,2},{67,3},{14,4},{69,5},{12,6},{71,7},{2,8},{73,9... | collective-permute-start | bytes 393224 | tf_op jit(solution)/shard_map/ppermute | solution.py:35
  100.2 2.1 %collective-permute-start.27 = (bf16[8,8192]{1,0:T(8,128)(2,1)S(1)}, bf16[8,8192]{1,0:T(8,128)(2,1)S(1)}, u32[]{:S(2)}, u32[]{:S(2)}) collective-permute-start(bf16[8,8192]{1,0:T(8,128)(2,1)S(1)} %multiply_convert_fusion.refs_0_), channel_id=1, source_target_pairs={{8,0},{97,1},{10,2},{99,3},{12,4},{101,5},{14,6},{103,7},{0,8},{10... | collective-permute-start | bytes 393224 | tf_op jit(solution)/shard_map/ppermute | solution.py:35
  104.5 4.1 %collective-permute-done.27.refs_2_ = bf16[8,8192]{1,0:T(8,128)(2,1)S(1)} collective-permute-done((bf16[8,8192]{1,0:T(8,128)(2,1)S(1)}, bf16[8,8192]{1,0:T(8,128)(2,1)S(1)}, u32[]{:S(2)}, u32[]{:S(2)}) %collective-permute-start.27) | collective-permute-done | bytes 131104 | tf_op jit(solution)/shard_map/ppermute | solution.py:35
  109.4 2.1 %collective-permute-start.30 = (bf16[32,8192]{1,0:T(8,128)(2,1)S(1)}, bf16[32,8192]{1,0:T(8,128)(2,1)S(1)}, u32[]{:S(2)}, u32[]{:S(2)}) collective-permute-start(bf16[32,8192]{1,0:T(8,128)(2,1)S(1)} %shard_map.115.refs_0_), channel_id=1, source_target_pairs={{16,0},{113,1},{18,2},{115,3},{20,4},{117,5},{22,6},{119,7},{24,8}... | collective-permute-start | bytes 1572872 | tf_op jit(solution)/shard_map/ppermute | solution.py:35
  111.6 5.4 %collective-permute-start.32 = (bf16[32,8192]{1,0:T(8,128)(2,1)S(1)}, bf16[32,8192]{1,0:T(8,128)(2,1)S(1)}, u32[]{:S(2)}, u32[]{:S(2)}) collective-permute-start(bf16[32,8192]{1,0:T(8,128)(2,1)S(1)} %shard_map.115.refs_0_), channel_id=1, source_target_pairs={{1,0},{0,1},{3,2},{2,3},{5,4},{4,5},{7,6},{6,7},{9,8},{8,9},{11,10... | collective-permute-start | bytes 1572872 | tf_op jit(solution)/shard_map/ppermute | solution.py:35
  117.0 3.2 %collective-permute-done.31.refs_3_.refs_1_ = bf16[32,8192]{1,0:T(8,128)(2,1)S(1)} collective-permute-done((bf16[32,8192]{1,0:T(8,128)(2,1)S(1)}, bf16[32,8192]{1,0:T(8,128)(2,1)S(1)}, u32[]{:S(2)}, u32[]{:S(2)}) %collective-permute-start.31) | collective-permute-done | bytes 524320 | tf_op jit(solution)/shard_map/ppermute | solution.py:35
  121.7 2.8 %collective-permute-done.30.refs_2_.refs_1_ = bf16[32,8192]{1,0:T(8,128)(2,1)S(1)} collective-permute-done((bf16[32,8192]{1,0:T(8,128)(2,1)S(1)}, bf16[32,8192]{1,0:T(8,128)(2,1)S(1)}, u32[]{:S(2)}, u32[]{:S(2)}) %collective-permute-start.30) | collective-permute-done | bytes 524320 | tf_op jit(solution)/shard_map/ppermute | solution.py:35
  124.6 1.9 %collective-permute-start.35 = (bf16[32,8192]{1,0:T(8,128)(2,1)S(1)}, bf16[32,8192]{1,0:T(8,128)(2,1)S(1)}, u32[]{:S(2)}, u32[]{:S(2)}) collective-permute-start(bf16[32,8192]{1,0:T(8,128)(2,1)S(1)} %collective-permute-done.30.refs_2_.refs_1_), channel_id=1, source_target_pairs={{1,0},{0,1},{3,2},{2,3},{5,4},{4,5},{7,6},{6,7},{9,8},{8,9},{11,10... | collective-permute-start | bytes 1572872 | tf_op jit(solution)/shard_map/ppermute | solution.py:35
  130.9 2.6 %fusion = bf16[128,8192]{1,0:T(8,128)(2,1)} fusion(bf16[256,128]{1,0:T(8,128)(2,1)S(1)} %get-tuple-element.41, bf16[256,8192]{1,0:T(8,128)(2,1)S(1)} %shard_map.119, bf16[1,128,8192]{2,1,0:T(8,128)(2,1)S(1)} %copy-done.1, f32[128]{0:T(128)S(1)} %multiply_divide_fusion), kind=kOutput, calls=%fused_computation.1 | convolution fusion | flops 541065216 | bytes 8454656 | tf_op jit(solution)/shard_map/dot_general | solution.py:116
  135.2 2.1 %fusion.1 = bf16[1,128,8192]{2,1,0:T(8,128)(2,1)} fusion(bf16[256,8192]{1,0:T(8,128)(2,1)S(1)} %shard_map.114, f32[256,128]{1,0:T(8,128)S(1)} %get-tuple-element.28, bf16[256,128]{1,0:T(8,128)(2,1)S(1)} %collective-permute-done.36, f32[128,128]{1,0:T(8,128)S(1)} %fusion.4, f32[128,128]{1,0:T(8,128)S(1)} %fusion.6, f32[128]{0:T(128)S(1)} %fusion.31), kind=kOutput, calls=%fused_computation.4 | convolution fusion | flops 538116096 | bytes 6619648 | tf_op jit(solution)/shard_map/dot_general | solution.py:116
  (105 shorter events, 30.1 us)
Async XLA Ops:
  0.6 8.1 %collective-permute-start.1 = (bf16[2,8192]{1,0:T(2,128)(2,1)}, bf16[2,8192]{1,0:T(2,128)(2,1)S(1)}, u32[]{:S(2)}, u32[]{:S(2)}) collective-permute-start(bf16[2,8192]{1,0:T(2,128)(2,1)} %bitcast.40), channel_id=1, source_target_pairs={{64,0},{11,1},{66,2},{9,3},{68,4},{15,5},{70,6},{13,7},{72,8},{3,9... | collective-permute-start | bytes 98312 | tf_op jit(solution)/shard_map/ppermute | solution.py:35
  6.9 4.7 %collective-permute-start.2 = (bf16[2,8192]{1,0:T(2,128)(2,1)}, bf16[2,8192]{1,0:T(2,128)(2,1)S(1)}, u32[]{:S(2)}, u32[]{:S(2)}) collective-permute-start(bf16[2,8192]{1,0:T(2,128)(2,1)} %bitcast.41), channel_id=1, source_target_pairs={{32,0},{3,1},{34,2},{1,3},{36,4},{7,5},{38,6},{5,7},{40,8},{11,9},... | collective-permute-start | bytes 98312 | tf_op jit(solution)/shard_map/ppermute | solution.py:35
  7.0 4.6 %collective-permute-start = (bf16[2,8192]{1,0:T(2,128)(2,1)}, bf16[2,8192]{1,0:T(2,128)(2,1)S(1)}, u32[]{:S(2)}, u32[]{:S(2)}) collective-permute-start(bf16[2,8192]{1,0:T(2,128)(2,1)} %bitcast.42), channel_id=1, source_target_pairs={{96,0},{9,1},{98,2},{11,3},{100,4},{13,5},{102,6},{15,7},{104,8},{... | collective-permute-start | bytes 98312 | tf_op jit(solution)/shard_map/ppermute | solution.py:35
  12.8 10.6 %collective-permute-start.5 = (bf16[8,8192]{1,0:T(8,128)(2,1)S(1)}, bf16[8,8192]{1,0:T(8,128)(2,1)S(1)}, u32[]{:S(2)}, u32[]{:S(2)}) collective-permute-start(bf16[8,8192]{1,0:T(8,128)(2,1)S(1)} %pad_maximum_fusion.1.refs_0_), channel_id=1, source_target_pairs={{10,0},{65,1},{8,2},{67,3},{14,4},{69,5},{12,6},{71,7},{2,8},{73,9... | collective-permute-start | bytes 393224 | tf_op jit(solution)/shard_map/ppermute | solution.py:35
  19.6 6.7 %collective-permute-start.4 = (bf16[8,8192]{1,0:T(8,128)(2,1)S(1)}, bf16[8,8192]{1,0:T(8,128)(2,1)S(1)}, u32[]{:S(2)}, u32[]{:S(2)}) collective-permute-start(bf16[8,8192]{1,0:T(8,128)(2,1)S(1)} %pad_maximum_fusion.1.refs_0_), channel_id=1, source_target_pairs={{8,0},{97,1},{10,2},{99,3},{12,4},{101,5},{14,6},{103,7},{0,8},{10... | collective-permute-start | bytes 393224 | tf_op jit(solution)/shard_map/ppermute | solution.py:35
  20.8 6.1 %collective-permute-start.3 = (bf16[8,8192]{1,0:T(8,128)(2,1)S(1)}, bf16[8,8192]{1,0:T(8,128)(2,1)S(1)}, u32[]{:S(2)}, u32[]{:S(2)}) collective-permute-start(bf16[8,8192]{1,0:T(8,128)(2,1)S(1)} %pad_maximum_fusion.1.refs_0_), channel_id=1, source_target_pairs={{2,0},{33,1},{0,2},{35,3},{6,4},{37,5},{4,6},{39,7},{10,8},{41,9},... | collective-permute-start | bytes 393224 | tf_op jit(solution)/shard_map/ppermute | solution.py:35
  27.0 11.5 %collective-permute-start.8 = (bf16[32,8192]{1,0:T(8,128)(2,1)S(1)}, bf16[32,8192]{1,0:T(8,128)(2,1)S(1)}, u32[]{:S(2)}, u32[]{:S(2)}) collective-permute-start(bf16[32,8192]{1,0:T(8,128)(2,1)S(1)} %shard_map.111.refs_0_), channel_id=1, source_target_pairs={{20,0},{125,1},{22,2},{127,3},{24,4},{113,5},{26,6},{115,7},{28,8}... | collective-permute-start | bytes 1572872 | tf_op jit(solution)/shard_map/ppermute | solution.py:35
  28.0 14.2 %collective-permute-start.7 = (bf16[32,8192]{1,0:T(8,128)(2,1)S(1)}, bf16[32,8192]{1,0:T(8,128)(2,1)S(1)}, u32[]{:S(2)}, u32[]{:S(2)}) collective-permute-start(bf16[32,8192]{1,0:T(8,128)(2,1)S(1)} %shard_map.111.refs_0_), channel_id=1, source_target_pairs={{16,0},{113,1},{18,2},{115,3},{20,4},{117,5},{22,6},{119,7},{24,8}... | collective-permute-start | bytes 1572872 | tf_op jit(solution)/shard_map/ppermute | solution.py:35
  28.6 18.1 %collective-permute-start.6 = (bf16[32,8192]{1,0:T(8,128)(2,1)S(1)}, bf16[32,8192]{1,0:T(8,128)(2,1)S(1)}, u32[]{:S(2)}, u32[]{:S(2)}) collective-permute-start(bf16[32,8192]{1,0:T(8,128)(2,1)S(1)} %shard_map.111.refs_0_), channel_id=1, source_target_pairs={{4,0},{13,1},{6,2},{15,3},{8,4},{1,5},{10,6},{3,7},{12,8},{5,9},{1... | collective-permute-start | bytes 1572872 | tf_op jit(solution)/shard_map/ppermute | solution.py:35
  31.0 18.0 %collective-permute-start.9 = (bf16[32,8192]{1,0:T(8,128)(2,1)S(1)}, bf16[32,8192]{1,0:T(8,128)(2,1)S(1)}, u32[]{:S(2)}, u32[]{:S(2)}) collective-permute-start(bf16[32,8192]{1,0:T(8,128)(2,1)S(1)} %shard_map.111.refs_0_), channel_id=1, source_target_pairs={{1,0},{0,1},{3,2},{2,3},{5,4},{4,5},{7,6},{6,7},{9,8},{8,9},{11,10... | collective-permute-start | bytes 1572872 | tf_op jit(solution)/shard_map/ppermute | solution.py:35
  38.5 10.5 %collective-permute-start.12 = (bf16[32,8192]{1,0:T(8,128)(2,1)S(1)}, bf16[32,8192]{1,0:T(8,128)(2,1)S(1)}, u32[]{:S(2)}, u32[]{:S(2)}) collective-permute-start(bf16[32,8192]{1,0:T(8,128)(2,1)S(1)} %collective-permute-done.8.refs_3_), channel_id=1, source_target_pairs={{1,0},{0,1},{3,2},{2,3},{5,4},{4,5},{7,6},{6,7},{9,8},{8,9},{11,10... | collective-permute-start | bytes 1572872 | tf_op jit(solution)/shard_map/ppermute | solution.py:35
  42.2 6.8 %collective-permute-start.11 = (bf16[32,8192]{1,0:T(8,128)(2,1)S(1)}, bf16[32,8192]{1,0:T(8,128)(2,1)S(1)}, u32[]{:S(2)}, u32[]{:S(2)}) collective-permute-start(bf16[32,8192]{1,0:T(8,128)(2,1)S(1)} %collective-permute-done.7.refs_2_), channel_id=1, source_target_pairs={{1,0},{0,1},{3,2},{2,3},{5,4},{4,5},{7,6},{6,7},{9,8},{8,9},{11,10... | collective-permute-start | bytes 1572872 | tf_op jit(solution)/shard_map/ppermute | solution.py:35
  55.9 5.5 %collective-permute-start.14 = (bf16[64,8192]{1,0:T(8,128)(2,1)S(1)}, bf16[64,8192]{1,0:T(8,128)(2,1)S(1)}, u32[]{:S(2)}, u32[]{:S(2)}) collective-permute-start(bf16[64,8192]{1,0:T(8,128)(2,1)S(1)} %slice.86), channel_id=1, source_target_pairs={{1,0},{0,1},{3,2},{2,3},{5,4},{4,5},{7,6},{6,7},{9,8},{8,9},{11,10... | collective-permute-start | bytes 3145736 | tf_op jit(solution)/shard_map/ppermute | solution.py:35
  57.5 10.1 %collective-permute-start.17 = (bf16[32,8192]{1,0:T(8,128)(2,1)S(1)}, bf16[32,8192]{1,0:T(8,128)(2,1)S(1)}, u32[]{:S(2)}, u32[]{:S(2)}) collective-permute-start(bf16[32,8192]{1,0:T(8,128)(2,1)S(1)} %fusion.15), channel_id=1, source_target_pairs={{124,0},{21,1},{126,2},{23,3},{112,4},{25,5},{114,6},{27,7},{116,8... | collective-permute-start | bytes 1572872 | tf_op jit(solution)/shard_map/ppermute | solution.py:35
  61.4 6.2 %collective-permute-start.16 = (bf16[32,8192]{1,0:T(8,128)(2,1)S(1)}, bf16[32,8192]{1,0:T(8,128)(2,1)S(1)}, u32[]{:S(2)}, u32[]{:S(2)}) collective-permute-start(bf16[32,8192]{1,0:T(8,128)(2,1)S(1)} %get-tuple-element.22), channel_id=1, source_target_pairs={{1,0},{0,1},{3,2},{2,3},{5,4},{4,5},{7,6},{6,7},{9,8},{8,9},{11,10... | collective-permute-start | bytes 1572872 | tf_op jit(solution)/shard_map/ppermute | solution.py:35
  61.7 11.5 %collective-permute-start.18 = (bf16[32,8192]{1,0:T(8,128)(2,1)S(1)}, bf16[32,8192]{1,0:T(8,128)(2,1)S(1)}, u32[]{:S(2)}, u32[]{:S(2)}) collective-permute-start(bf16[32,8192]{1,0:T(8,128)(2,1)S(1)} %get-tuple-element.36), channel_id=1, source_target_pairs={{112,0},{17,1},{114,2},{19,3},{116,4},{21,5},{118,6},{23,7},{120,8... | collective-permute-start | bytes 1572872 | tf_op jit(solution)/shard_map/ppermute | solution.py:35
  62.1 11.1 %collective-permute-start.19 = (bf16[32,8192]{1,0:T(8,128)(2,1)S(1)}, bf16[32,8192]{1,0:T(8,128)(2,1)S(1)}, u32[]{:S(2)}, u32[]{:S(2)}) collective-permute-start(bf16[32,8192]{1,0:T(8,128)(2,1)S(1)} %get-tuple-element.37), channel_id=1, source_target_pairs={{12,0},{5,1},{14,2},{7,3},{0,4},{9,5},{2,6},{11,7},{4,8},{13,9},{6... | collective-permute-start | bytes 1572872 | tf_op jit(solution)/shard_map/ppermute | solution.py:35
  73.5 8.1 %collective-permute-start.20 = (bf16[8,8192]{1,0:T(8,128)(2,1)S(1)}, bf16[8,8192]{1,0:T(8,128)(2,1)S(1)}, u32[]{:S(2)}, u32[]{:S(2)}) collective-permute-start(bf16[8,8192]{1,0:T(8,128)(2,1)S(1)} %get-tuple-element.38), channel_id=1, source_target_pairs={{10,0},{65,1},{8,2},{67,3},{14,4},{69,5},{12,6},{71,7},{2,8},{73,9... | collective-permute-start | bytes 393224 | tf_op jit(solution)/shard_map/ppermute | solution.py:35
  78.0 6.3 %collective-permute-start.22 = (bf16[8,8192]{1,0:T(8,128)(2,1)S(1)}, bf16[8,8192]{1,0:T(8,128)(2,1)S(1)}, u32[]{:S(2)}, u32[]{:S(2)}) collective-permute-start(bf16[8,8192]{1,0:T(8,128)(2,1)S(1)} %get-tuple-element.39), channel_id=1, source_target_pairs={{2,0},{97,1},{0,2},{99,3},{6,4},{101,5},{4,6},{103,7},{10,8},{105,... | collective-permute-start | bytes 393224 | tf_op jit(solution)/shard_map/ppermute | solution.py:35
  78.1 8.4 %collective-permute-start.21 = (bf16[8,8192]{1,0:T(8,128)(2,1)S(1)}, bf16[8,8192]{1,0:T(8,128)(2,1)S(1)}, u32[]{:S(2)}, u32[]{:S(2)}) collective-permute-start(bf16[8,8192]{1,0:T(8,128)(2,1)S(1)} %get-tuple-element.40), channel_id=1, source_target_pairs={{8,0},{33,1},{10,2},{35,3},{12,4},{37,5},{14,6},{39,7},{0,8},{41,9... | collective-permute-start | bytes 393224 | tf_op jit(solution)/shard_map/ppermute | solution.py:35
  86.5 5.7 %collective-permute-start.25 = (bf16[8,8192]{1,0:T(8,128)(2,1)S(1)}, bf16[8,8192]{1,0:T(8,128)(2,1)S(1)}, u32[]{:S(2)}, u32[]{:S(2)}) collective-permute-start(bf16[8,8192]{1,0:T(8,128)(2,1)S(1)} %fusion.21), channel_id=1, source_target_pairs={{32,0},{3,1},{34,2},{1,3},{36,4},{7,5},{38,6},{5,7},{40,8},{11,9},... | collective-permute-start | bytes 393224 | tf_op jit(solution)/shard_map/ppermute | solution.py:35
  87.2 7.7 %collective-permute-start.24 = (bf16[8,8192]{1,0:T(8,128)(2,1)S(1)}, bf16[8,8192]{1,0:T(8,128)(2,1)S(1)}, u32[]{:S(2)}, u32[]{:S(2)}) collective-permute-start(bf16[8,8192]{1,0:T(8,128)(2,1)S(1)} %fusion.21), channel_id=1, source_target_pairs={{64,0},{11,1},{66,2},{9,3},{68,4},{15,5},{70,6},{13,7},{72,8},{3,9... | collective-permute-start | bytes 393224 | tf_op jit(solution)/shard_map/ppermute | solution.py:35
  89.6 6.4 %collective-permute-start.23 = (bf16[8,8192]{1,0:T(8,128)(2,1)S(1)}, bf16[8,8192]{1,0:T(8,128)(2,1)S(1)}, u32[]{:S(2)}, u32[]{:S(2)}) collective-permute-start(bf16[8,8192]{1,0:T(8,128)(2,1)S(1)} %fusion.21), channel_id=1, source_target_pairs={{96,0},{9,1},{98,2},{11,3},{100,4},{13,5},{102,6},{15,7},{104,8},{... | collective-permute-start | bytes 393224 | tf_op jit(solution)/shard_map/ppermute | solution.py:35
  96.5 8.0 %collective-permute-start.28 = (bf16[8,8192]{1,0:T(8,128)(2,1)S(1)}, bf16[8,8192]{1,0:T(8,128)(2,1)S(1)}, u32[]{:S(2)}, u32[]{:S(2)}) collective-permute-start(bf16[8,8192]{1,0:T(8,128)(2,1)S(1)} %multiply_convert_fusion.refs_0_), channel_id=1, source_target_pairs={{10,0},{65,1},{8,2},{67,3},{14,4},{69,5},{12,6},{71,7},{2,8},{73,9... | collective-permute-start | bytes 393224 | tf_op jit(solution)/shard_map/ppermute | solution.py:35
  100.2 8.3 %collective-permute-start.27 = (bf16[8,8192]{1,0:T(8,128)(2,1)S(1)}, bf16[8,8192]{1,0:T(8,128)(2,1)S(1)}, u32[]{:S(2)}, u32[]{:S(2)}) collective-permute-start(bf16[8,8192]{1,0:T(8,128)(2,1)S(1)} %multiply_convert_fusion.refs_0_), channel_id=1, source_target_pairs={{8,0},{97,1},{10,2},{99,3},{12,4},{101,5},{14,6},{103,7},{0,8},{10... | collective-permute-start | bytes 393224 | tf_op jit(solution)/shard_map/ppermute | solution.py:35
  102.4 6.2 %collective-permute-start.26 = (bf16[8,8192]{1,0:T(8,128)(2,1)S(1)}, bf16[8,8192]{1,0:T(8,128)(2,1)S(1)}, u32[]{:S(2)}, u32[]{:S(2)}) collective-permute-start(bf16[8,8192]{1,0:T(8,128)(2,1)S(1)} %multiply_convert_fusion.refs_0_), channel_id=1, source_target_pairs={{2,0},{33,1},{0,2},{35,3},{6,4},{37,5},{4,6},{39,7},{10,8},{41,9},... | collective-permute-start | bytes 393224 | tf_op jit(solution)/shard_map/ppermute | solution.py:35
  108.6 11.5 %collective-permute-start.31 = (bf16[32,8192]{1,0:T(8,128)(2,1)S(1)}, bf16[32,8192]{1,0:T(8,128)(2,1)S(1)}, u32[]{:S(2)}, u32[]{:S(2)}) collective-permute-start(bf16[32,8192]{1,0:T(8,128)(2,1)S(1)} %shard_map.115.refs_0_), channel_id=1, source_target_pairs={{20,0},{125,1},{22,2},{127,3},{24,4},{113,5},{26,6},{115,7},{28,8}... | collective-permute-start | bytes 1572872 | tf_op jit(solution)/shard_map/ppermute | solution.py:35
  109.4 15.1 %collective-permute-start.30 = (bf16[32,8192]{1,0:T(8,128)(2,1)S(1)}, bf16[32,8192]{1,0:T(8,128)(2,1)S(1)}, u32[]{:S(2)}, u32[]{:S(2)}) collective-permute-start(bf16[32,8192]{1,0:T(8,128)(2,1)S(1)} %shard_map.115.refs_0_), channel_id=1, source_target_pairs={{16,0},{113,1},{18,2},{115,3},{20,4},{117,5},{22,6},{119,7},{24,8}... | collective-permute-start | bytes 1572872 | tf_op jit(solution)/shard_map/ppermute | solution.py:35
  111.5 14.9 %collective-permute-start.29 = (bf16[32,8192]{1,0:T(8,128)(2,1)S(1)}, bf16[32,8192]{1,0:T(8,128)(2,1)S(1)}, u32[]{:S(2)}, u32[]{:S(2)}) collective-permute-start(bf16[32,8192]{1,0:T(8,128)(2,1)S(1)} %shard_map.115.refs_0_), channel_id=1, source_target_pairs={{4,0},{13,1},{6,2},{15,3},{8,4},{1,5},{10,6},{3,7},{12,8},{5,9},{1... | collective-permute-start | bytes 1572872 | tf_op jit(solution)/shard_map/ppermute | solution.py:35
  111.6 16.5 %collective-permute-start.32 = (bf16[32,8192]{1,0:T(8,128)(2,1)S(1)}, bf16[32,8192]{1,0:T(8,128)(2,1)S(1)}, u32[]{:S(2)}, u32[]{:S(2)}) collective-permute-start(bf16[32,8192]{1,0:T(8,128)(2,1)S(1)} %shard_map.115.refs_0_), channel_id=1, source_target_pairs={{1,0},{0,1},{3,2},{2,3},{5,4},{4,5},{7,6},{6,7},{9,8},{8,9},{11,10... | collective-permute-start | bytes 1572872 | tf_op jit(solution)/shard_map/ppermute | solution.py:35
  120.2 7.9 %collective-permute-start.34 = (bf16[32,8192]{1,0:T(8,128)(2,1)S(1)}, bf16[32,8192]{1,0:T(8,128)(2,1)S(1)}, u32[]{:S(2)}, u32[]{:S(2)}) collective-permute-start(bf16[32,8192]{1,0:T(8,128)(2,1)S(1)} %collective-permute-done.31.refs_3_.refs_1_), channel_id=1, source_target_pairs={{1,0},{0,1},{3,2},{2,3},{5,4},{4,5},{7,6},{6,7},{9,8},{8,9},{11,10... | collective-permute-start | bytes 1572872 | tf_op jit(solution)/shard_map/ppermute | solution.py:35
  129.9 4.8 %collective-permute-start.36 = (bf16[256,128]{1,0:T(8,128)(2,1)S(1)}, bf16[256,128]{1,0:T(8,128)(2,1)S(1)}, u32[]{:S(2)}, u32[]{:S(2)}) collective-permute-start(bf16[256,128]{1,0:T(8,128)(2,1)S(1)} %fusion.23), channel_id=1, source_target_pairs={{0,128},{128,0},{1,129},{129,1},{2,130},{130,2},{3,131},{131,3},{4... | collective-permute-start | bytes 196616 | tf_op jit(solution)/shard_map/ppermute | solution.py:112
  (10 other events, 102.4 us)

commit v5 on v2

--- a/solution.py
+++ b/solution.py
@@ -17,7 +17,7 @@
 EVEN_XY = ((0, 0, 0), (0, 0, 1), (0, 2, 0), (0, 2, 1))
 TURNS = [[(0, 1, 3, 2)[(i - own) % 4] for i in range(4)] for own in range(4)]
 TURNS += [[i ^ own for i in range(4)] for own in range(4)]
-OCTET_Z = np.array([dz + 2 * k for dz in (0, 0, -1, -1) for k in (0, 1, 3, 2)], np.int32)
+OCTET_Z = np.array([dz + 2 * k for dz in (0, 0, -1, 1) for k in (0, 1, 3, 2)], np.int32)
 
 
 def place(z, x, y, c):
@@ -69,7 +69,7 @@
     return [lax.select_n(own, *[near[turn[i]] for turn in TURNS]) for i in range(4)]
 
 
-AROUND = (((0, 1, 0), (0, -1, 0)), ((1, 0, 0), (-1, 0, 0)), ((1, 1, 0), (-1, -1, 0)))
+AROUND = (((0, 1, 0), (0, -1, 0)), ((1, 0, 0), (-1, 0, 0)), ((-1, 1, 0), (1, -1, 0)))
 
 
 def gather_rows(octet):

time: 138 us -> 141 us (1.022)
  starting transfers between devices: 75.1 us -> 84.5 us
  waiting for transfers between devices: 42.8 us -> 36.3 us
    ppermute x34, starting transfers between devices: 73.5 us -> 83.2 us  [fetch(): return lax.ppermute(value, 'lat', pairs)]
    ppermute x34, waiting for transfers between devices: 40.4 us -> 33.9 us  [fetch(): return lax.ppermute(value, 'lat', pairs)]
  transfers between devices with their start and end apart: 36 -> 36, of which waited for: 20 -> 18; matrix products, arithmetic and copies ran while one was open for 7% -> 7% of each run, Pallas kernels for 0% -> 0%
where the time goes in v5:
time: 141 us; the launch traced here: 140 us
  starting transfers between devices  84.5 us (60%)
  waiting for transfers between devices  36.3 us (26%)
  matrix products  10.2 us (7%)
  other arithmetic  6.16 us (4%)
  between operations  1.66 us (1%)
    ppermute x34, starting transfers between devices, fetch(): return lax.ppermute(value, 'lat', pairs)  83.2 us
    ppermute x34, waiting for transfers between devices, fetch(): return lax.ppermute(value, 'lat', pairs)  33.9 us
    dot_general x9, matrix products, dot(): lax.dot_general(left, right, ((over[:1], over[1:]), ((), ())), preferred_...  10.2 us
  transfers between devices with their start and end apart: 36, of which 18 were waited for; matrix products, arithmetic and copies ran while one was open for 7% of the time, Pallas kernels for 0%

profile of v5, /device:TPU:1, one launch (start us, length us, event | category | flops | bytes accessed | tf_op | source)
XLA Modules:
  0.0 140.4 jit_solution(14049103080821880153)
XLA Ops:
  0.6 6.3 %collective-permute-start.1 = (bf16[2,8192]{1,0:T(2,128)(2,1)}, bf16[2,8192]{1,0:T(2,128)(2,1)S(1)}, u32[]{:S(2)}, u32[]{:S(2)}) collective-permute-start(bf16[2,8192]{1,0:T(2,128)(2,1)} %bitcast.40), channel_id=1, source_target_pairs={{64,0},{11,1},{66,2},{9,3},{68,4},{15,5},{70,6},{13,7},{72,8},{3,9... | collective-permute-start | bytes 98312 | tf_op jit(solution)/shard_map/ppermute | solution.py:35
  8.8 2.8 %collective-permute-done.2 = bf16[2,8192]{1,0:T(2,128)(2,1)S(1)} collective-permute-done((bf16[2,8192]{1,0:T(2,128)(2,1)}, bf16[2,8192]{1,0:T(2,128)(2,1)S(1)}, u32[]{:S(2)}, u32[]{:S(2)}) %collective-permute-start.2) | collective-permute-done | bytes 32800 | tf_op jit(solution)/shard_map/ppermute | solution.py:35
  12.8 6.9 %collective-permute-start.5 = (bf16[8,8192]{1,0:T(8,128)(2,1)S(1)}, bf16[8,8192]{1,0:T(8,128)(2,1)S(1)}, u32[]{:S(2)}, u32[]{:S(2)}) collective-permute-start(bf16[8,8192]{1,0:T(8,128)(2,1)S(1)} %pad_maximum_fusion.1.refs_0_), channel_id=1, source_target_pairs={{10,0},{65,1},{8,2},{67,3},{14,4},{69,5},{12,6},{71,7},{2,8},{73,9... | collective-permute-start | bytes 393224 | tf_op jit(solution)/shard_map/ppermute | solution.py:35
  20.8 2.4 %collective-permute-start.3 = (bf16[8,8192]{1,0:T(8,128)(2,1)S(1)}, bf16[8,8192]{1,0:T(8,128)(2,1)S(1)}, u32[]{:S(2)}, u32[]{:S(2)}) collective-permute-start(bf16[8,8192]{1,0:T(8,128)(2,1)S(1)} %pad_maximum_fusion.1.refs_0_), channel_id=1, source_target_pairs={{2,0},{33,1},{0,2},{35,3},{6,4},{37,5},{4,6},{39,7},{10,8},{41,9},... | collective-permute-start | bytes 393224 | tf_op jit(solution)/shard_map/ppermute | solution.py:35
  23.4 2.9 %collective-permute-done.4.refs_2_ = bf16[8,8192]{1,0:T(8,128)(2,1)S(1)} collective-permute-done((bf16[8,8192]{1,0:T(8,128)(2,1)S(1)}, bf16[8,8192]{1,0:T(8,128)(2,1)S(1)}, u32[]{:S(2)}, u32[]{:S(2)}) %collective-permute-start.4) | collective-permute-done | bytes 131104 | tf_op jit(solution)/shard_map/ppermute | solution.py:35
  27.0 2.5 %collective-permute-start.8 = (bf16[32,8192]{1,0:T(8,128)(2,1)S(1)}, bf16[32,8192]{1,0:T(8,128)(2,1)S(1)}, u32[]{:S(2)}, u32[]{:S(2)}) collective-permute-start(bf16[32,8192]{1,0:T(8,128)(2,1)S(1)} %shard_map.111.refs_0_), channel_id=1, source_target_pairs={{116,0},{29,1},{118,2},{31,3},{120,4},{17,5},{122,6},{19,7},{124,8... | collective-permute-start | bytes 1572872 | tf_op jit(solution)/shard_map/ppermute | solution.py:35
  29.7 2.1 %fusion.2 = f32[128]{0:T(128)S(1)} fusion(bf16[1,128,8192]{2,1,0:T(8,128)(2,1)} %param.11), kind=kLoop, calls=%fused_computation.7 | loop fusion | flops 3145600 | bytes 2097664 | tf_op jit(solution)/shard_map/reduce_sum | solution.py:118
  31.8 6.4 %collective-permute-start.9 = (bf16[32,8192]{1,0:T(8,128)(2,1)S(1)}, bf16[32,8192]{1,0:T(8,128)(2,1)S(1)}, u32[]{:S(2)}, u32[]{:S(2)}) collective-permute-start(bf16[32,8192]{1,0:T(8,128)(2,1)S(1)} %shard_map.111.refs_0_), channel_id=1, source_target_pairs={{1,0},{0,1},{3,2},{2,3},{5,4},{4,5},{7,6},{6,7},{9,8},{8,9},{11,10... | collective-permute-start | bytes 1572872 | tf_op jit(solution)/shard_map/ppermute | solution.py:35
  38.1 6.9 %collective-permute-start.12 = (bf16[32,8192]{1,0:T(8,128)(2,1)S(1)}, bf16[32,8192]{1,0:T(8,128)(2,1)S(1)}, u32[]{:S(2)}, u32[]{:S(2)}) collective-permute-start(bf16[32,8192]{1,0:T(8,128)(2,1)S(1)} %collective-permute-done.8.refs_3_), channel_id=1, source_target_pairs={{1,0},{0,1},{3,2},{2,3},{5,4},{4,5},{7,6},{6,7},{9,8},{8,9},{11,10... | collective-permute-start | bytes 1572872 | tf_op jit(solution)/shard_map/ppermute | solution.py:35
  45.0 3.2 %collective-permute-start.10 = (bf16[32,8192]{1,0:T(8,128)(2,1)S(1)}, bf16[32,8192]{1,0:T(8,128)(2,1)S(1)}, u32[]{:S(2)}, u32[]{:S(2)}) collective-permute-start(bf16[32,8192]{1,0:T(8,128)(2,1)S(1)} %collective-permute-done.6.refs_1_), channel_id=1, source_target_pairs={{1,0},{0,1},{3,2},{2,3},{5,4},{4,5},{7,6},{6,7},{9,8},{8,9},{11,10... | collective-permute-start | bytes 1572872 | tf_op jit(solution)/shard_map/ppermute | solution.py:35
  51.7 2.4 %collective-permute-done.13 = bf16[264,128]{1,0:T(8,128)(2,1)S(1)} collective-permute-done((bf16[264,128]{1,0:T(8,128)(2,1)S(1)}, bf16[264,128]{1,0:T(8,128)(2,1)S(1)}, u32[]{:S(2)}, u32[]{:S(2)}) %collective-permute-start.13) | collective-permute-done | bytes 67616 | tf_op jit(solution)/shard_map/ppermute | solution.py:107
  55.0 1.6 %collective-permute-start.14 = (bf16[32,8192]{1,0:T(8,128)(2,1)S(1)}, bf16[32,8192]{1,0:T(8,128)(2,1)S(1)}, u32[]{:S(2)}, u32[]{:S(2)}) collective-permute-start(bf16[32,8192]{1,0:T(8,128)(2,1)S(1)} %slice.77), channel_id=1, source_target_pairs={{1,0},{0,1},{3,2},{2,3},{5,4},{4,5},{7,6},{6,7},{9,8},{8,9},{11,10... | collective-permute-start | bytes 1572872 | tf_op jit(solution)/shard_map/ppermute | solution.py:35
  58.7 2.7 %collective-permute-start.16 = (bf16[32,8192]{1,0:T(8,128)(2,1)S(1)}, bf16[32,8192]{1,0:T(8,128)(2,1)S(1)}, u32[]{:S(2)}, u32[]{:S(2)}) collective-permute-start(bf16[32,8192]{1,0:T(8,128)(2,1)S(1)} %fusion.16), channel_id=1, source_target_pairs={{28,0},{117,1},{30,2},{119,3},{16,4},{121,5},{18,6},{123,7},{20,8}... | collective-permute-start | bytes 1572872 | tf_op jit(solution)/shard_map/ppermute | solution.py:35
  62.3 2.2 %collective-permute-start.17 = (bf16[32,8192]{1,0:T(8,128)(2,1)S(1)}, bf16[32,8192]{1,0:T(8,128)(2,1)S(1)}, u32[]{:S(2)}, u32[]{:S(2)}) collective-permute-start(bf16[32,8192]{1,0:T(8,128)(2,1)S(1)} %get-tuple-element.24), channel_id=1, source_target_pairs={{112,0},{17,1},{114,2},{19,3},{116,4},{21,5},{118,6},{23,7},{120,8... | collective-permute-start | bytes 1572872 | tf_op jit(solution)/shard_map/ppermute | solution.py:35
  65.2 6.2 %collective-permute-done.16 = bf16[32,8192]{1,0:T(8,128)(2,1)S(1)} collective-permute-done((bf16[32,8192]{1,0:T(8,128)(2,1)S(1)}, bf16[32,8192]{1,0:T(8,128)(2,1)S(1)}, u32[]{:S(2)}, u32[]{:S(2)}) %collective-permute-start.16) | collective-permute-done | bytes 524320 | tf_op jit(solution)/shard_map/ppermute | solution.py:35
  71.3 1.7 %collective-permute-done.17 = bf16[32,8192]{1,0:T(8,128)(2,1)S(1)} collective-permute-done((bf16[32,8192]{1,0:T(8,128)(2,1)S(1)}, bf16[32,8192]{1,0:T(8,128)(2,1)S(1)}, u32[]{:S(2)}, u32[]{:S(2)}) %collective-permute-start.17) | collective-permute-done | bytes 524320 | tf_op jit(solution)/shard_map/ppermute | solution.py:35
  73.0 2.2 %collective-permute-done.18 = bf16[32,8192]{1,0:T(8,128)(2,1)S(1)} collective-permute-done((bf16[32,8192]{1,0:T(8,128)(2,1)S(1)}, bf16[32,8192]{1,0:T(8,128)(2,1)S(1)}, u32[]{:S(2)}, u32[]{:S(2)}) %collective-permute-start.18) | collective-permute-done | bytes 524320 | tf_op jit(solution)/shard_map/ppermute | solution.py:35
  75.5 4.3 %collective-permute-start.19 = (bf16[8,8192]{1,0:T(8,128)(2,1)S(1)}, bf16[8,8192]{1,0:T(8,128)(2,1)S(1)}, u32[]{:S(2)}, u32[]{:S(2)}) collective-permute-start(bf16[8,8192]{1,0:T(8,128)(2,1)S(1)} %get-tuple-element.26), channel_id=1, source_target_pairs={{10,0},{65,1},{8,2},{67,3},{14,4},{69,5},{12,6},{71,7},{2,8},{73,9... | collective-permute-start | bytes 393224 | tf_op jit(solution)/shard_map/ppermute | solution.py:35
  79.9 3.6 %collective-permute-start.20 = (bf16[8,8192]{1,0:T(8,128)(2,1)S(1)}, bf16[8,8192]{1,0:T(8,128)(2,1)S(1)}, u32[]{:S(2)}, u32[]{:S(2)}) collective-permute-start(bf16[8,8192]{1,0:T(8,128)(2,1)S(1)} %get-tuple-element.28), channel_id=1, source_target_pairs={{8,0},{33,1},{10,2},{35,3},{12,4},{37,5},{14,6},{39,7},{0,8},{41,9... | collective-permute-start | bytes 393224 | tf_op jit(solution)/shard_map/ppermute | solution.py:35
  83.5 2.6 %collective-permute-done.19 = bf16[8,8192]{1,0:T(8,128)(2,1)S(1)} collective-permute-done((bf16[8,8192]{1,0:T(8,128)(2,1)S(1)}, bf16[8,8192]{1,0:T(8,128)(2,1)S(1)}, u32[]{:S(2)}, u32[]{:S(2)}) %collective-permute-start.19) | collective-permute-done | bytes 131104 | tf_op jit(solution)/shard_map/ppermute | solution.py:35
  88.6 3.3 %collective-permute-start.23 = (bf16[8,8192]{1,0:T(8,128)(2,1)S(1)}, bf16[8,8192]{1,0:T(8,128)(2,1)S(1)}, u32[]{:S(2)}, u32[]{:S(2)}) collective-permute-start(bf16[8,8192]{1,0:T(8,128)(2,1)S(1)} %fusion.19), channel_id=1, source_target_pairs={{64,0},{11,1},{66,2},{9,3},{68,4},{15,5},{70,6},{13,7},{72,8},{3,9... | collective-permute-start | bytes 393224 | tf_op jit(solution)/shard_map/ppermute | solution.py:35
  93.2 3.2 %collective-permute-done.23 = bf16[8,8192]{1,0:T(8,128)(2,1)S(1)} collective-permute-done((bf16[8,8192]{1,0:T(8,128)(2,1)S(1)}, bf16[8,8192]{1,0:T(8,128)(2,1)S(1)}, u32[]{:S(2)}, u32[]{:S(2)}) %collective-permute-start.23) | collective-permute-done | bytes 131104 | tf_op jit(solution)/shard_map/ppermute | solution.py:35
  97.8 2.9 %collective-permute-start.27 = (bf16[8,8192]{1,0:T(8,128)(2,1)S(1)}, bf16[8,8192]{1,0:T(8,128)(2,1)S(1)}, u32[]{:S(2)}, u32[]{:S(2)}) collective-permute-start(bf16[8,8192]{1,0:T(8,128)(2,1)S(1)} %multiply_convert_fusion.refs_0_), channel_id=1, source_target_pairs={{10,0},{65,1},{8,2},{67,3},{14,4},{69,5},{12,6},{71,7},{2,8},{73,9... | collective-permute-start | bytes 393224 | tf_op jit(solution)/shard_map/ppermute | solution.py:35
  100.7 2.0 %collective-permute-start.26 = (bf16[8,8192]{1,0:T(8,128)(2,1)S(1)}, bf16[8,8192]{1,0:T(8,128)(2,1)S(1)}, u32[]{:S(2)}, u32[]{:S(2)}) collective-permute-start(bf16[8,8192]{1,0:T(8,128)(2,1)S(1)} %multiply_convert_fusion.refs_0_), channel_id=1, source_target_pairs={{8,0},{97,1},{10,2},{99,3},{12,4},{101,5},{14,6},{103,7},{0,8},{10... | collective-permute-start | bytes 393224 | tf_op jit(solution)/shard_map/ppermute | solution.py:35
  105.8 3.3 %collective-permute-done.26.refs_2_ = bf16[8,8192]{1,0:T(8,128)(2,1)S(1)} collective-permute-done((bf16[8,8192]{1,0:T(8,128)(2,1)S(1)}, bf16[8,8192]{1,0:T(8,128)(2,1)S(1)}, u32[]{:S(2)}, u32[]{:S(2)}) %collective-permute-start.26) | collective-permute-done | bytes 131104 | tf_op jit(solution)/shard_map/ppermute | solution.py:35
  109.2 2.3 %collective-permute-start.30 = (bf16[32,8192]{1,0:T(8,128)(2,1)S(1)}, bf16[32,8192]{1,0:T(8,128)(2,1)S(1)}, u32[]{:S(2)}, u32[]{:S(2)}) collective-permute-start(bf16[32,8192]{1,0:T(8,128)(2,1)S(1)} %shard_map.115.refs_0_), channel_id=1, source_target_pairs={{116,0},{29,1},{118,2},{31,3},{120,4},{17,5},{122,6},{19,7},{124,8... | collective-permute-start | bytes 1572872 | tf_op jit(solution)/shard_map/ppermute | solution.py:35
  112.6 5.5 %collective-permute-start.31 = (bf16[32,8192]{1,0:T(8,128)(2,1)S(1)}, bf16[32,8192]{1,0:T(8,128)(2,1)S(1)}, u32[]{:S(2)}, u32[]{:S(2)}) collective-permute-start(bf16[32,8192]{1,0:T(8,128)(2,1)S(1)} %shard_map.115.refs_0_), channel_id=1, source_target_pairs={{1,0},{0,1},{3,2},{2,3},{5,4},{4,5},{7,6},{6,7},{9,8},{8,9},{11,10... | collective-permute-start | bytes 1572872 | tf_op jit(solution)/shard_map/ppermute | solution.py:35
  118.1 2.2 %collective-permute-done.30.refs_3_ = bf16[32,8192]{1,0:T(8,128)(2,1)S(1)} collective-permute-done((bf16[32,8192]{1,0:T(8,128)(2,1)S(1)}, bf16[32,8192]{1,0:T(8,128)(2,1)S(1)}, u32[]{:S(2)}, u32[]{:S(2)}) %collective-permute-start.30) | collective-permute-done | bytes 524320 | tf_op jit(solution)/shard_map/ppermute | solution.py:35
  120.3 6.6 %collective-permute-start.34 = (bf16[32,8192]{1,0:T(8,128)(2,1)S(1)}, bf16[32,8192]{1,0:T(8,128)(2,1)S(1)}, u32[]{:S(2)}, u32[]{:S(2)}) collective-permute-start(bf16[32,8192]{1,0:T(8,128)(2,1)S(1)} %collective-permute-done.30.refs_3_), channel_id=1, source_target_pairs={{1,0},{0,1},{3,2},{2,3},{5,4},{4,5},{7,6},{6,7},{9,8},{8,9},{11,10... | collective-permute-start | bytes 1572872 | tf_op jit(solution)/shard_map/ppermute | solution.py:35
  126.9 3.5 %collective-permute-start.32 = (bf16[32,8192]{1,0:T(8,128)(2,1)S(1)}, bf16[32,8192]{1,0:T(8,128)(2,1)S(1)}, u32[]{:S(2)}, u32[]{:S(2)}) collective-permute-start(bf16[32,8192]{1,0:T(8,128)(2,1)S(1)} %collective-permute-done.28.refs_1_), channel_id=1, source_target_pairs={{1,0},{0,1},{3,2},{2,3},{5,4},{4,5},{7,6},{6,7},{9,8},{8,9},{11,10... | collective-permute-start | bytes 1572872 | tf_op jit(solution)/shard_map/ppermute | solution.py:35
  133.8 2.6 %fusion = bf16[128,8192]{1,0:T(8,128)(2,1)} fusion(bf16[256,128]{1,0:T(8,128)(2,1)S(1)} %get-tuple-element.30, bf16[256,8192]{1,0:T(8,128)(2,1)S(1)} %shard_map.118, bf16[1,128,8192]{2,1,0:T(8,128)(2,1)S(1)} %copy-done.1, f32[128]{0:T(128)S(1)} %rsqrt_multiply_fusion), kind=kOutput, calls=%fused_computation.1 | convolution fusion | flops 541065216 | bytes 8454656 | tf_op jit(solution)/shard_map/dot_general | solution.py:111
  138.3 2.1 %fusion.1 = bf16[1,128,8192]{2,1,0:T(8,128)(2,1)} fusion(bf16[256,8192]{1,0:T(8,128)(2,1)S(1)} %shard_map.114, bf16[256,128]{1,0:T(8,128)(2,1)S(1)} %get-tuple-element.19), kind=kOutput, calls=%fused_computation.4 | convolution fusion | flops 537919488 | bytes 6356992 | tf_op jit(solution)/shard_map/dot_general | solution.py:111
  (99 shorter events, 27.3 us)
Async XLA Ops:
  0.6 8.1 %collective-permute-start.1 = (bf16[2,8192]{1,0:T(2,128)(2,1)}, bf16[2,8192]{1,0:T(2,128)(2,1)S(1)}, u32[]{:S(2)}, u32[]{:S(2)}) collective-permute-start(bf16[2,8192]{1,0:T(2,128)(2,1)} %bitcast.40), channel_id=1, source_target_pairs={{64,0},{11,1},{66,2},{9,3},{68,4},{15,5},{70,6},{13,7},{72,8},{3,9... | collective-permute-start | bytes 98312 | tf_op jit(solution)/shard_map/ppermute | solution.py:35
  6.9 4.7 %collective-permute-start.2 = (bf16[2,8192]{1,0:T(2,128)(2,1)}, bf16[2,8192]{1,0:T(2,128)(2,1)S(1)}, u32[]{:S(2)}, u32[]{:S(2)}) collective-permute-start(bf16[2,8192]{1,0:T(2,128)(2,1)} %bitcast.41), channel_id=1, source_target_pairs={{32,0},{3,1},{34,2},{1,3},{36,4},{7,5},{38,6},{5,7},{40,8},{11,9},... | collective-permute-start | bytes 98312 | tf_op jit(solution)/shard_map/ppermute | solution.py:35
  7.0 4.6 %collective-permute-start = (bf16[2,8192]{1,0:T(2,128)(2,1)}, bf16[2,8192]{1,0:T(2,128)(2,1)S(1)}, u32[]{:S(2)}, u32[]{:S(2)}) collective-permute-start(bf16[2,8192]{1,0:T(2,128)(2,1)} %bitcast.42), channel_id=1, source_target_pairs={{96,0},{9,1},{98,2},{11,3},{100,4},{13,5},{102,6},{15,7},{104,8},{... | collective-permute-start | bytes 98312 | tf_op jit(solution)/shard_map/ppermute | solution.py:35
  12.8 10.6 %collective-permute-start.5 = (bf16[8,8192]{1,0:T(8,128)(2,1)S(1)}, bf16[8,8192]{1,0:T(8,128)(2,1)S(1)}, u32[]{:S(2)}, u32[]{:S(2)}) collective-permute-start(bf16[8,8192]{1,0:T(8,128)(2,1)S(1)} %pad_maximum_fusion.1.refs_0_), channel_id=1, source_target_pairs={{10,0},{65,1},{8,2},{67,3},{14,4},{69,5},{12,6},{71,7},{2,8},{73,9... | collective-permute-start | bytes 393224 | tf_op jit(solution)/shard_map/ppermute | solution.py:35
  19.6 6.7 %collective-permute-start.4 = (bf16[8,8192]{1,0:T(8,128)(2,1)S(1)}, bf16[8,8192]{1,0:T(8,128)(2,1)S(1)}, u32[]{:S(2)}, u32[]{:S(2)}) collective-permute-start(bf16[8,8192]{1,0:T(8,128)(2,1)S(1)} %pad_maximum_fusion.1.refs_0_), channel_id=1, source_target_pairs={{8,0},{97,1},{10,2},{99,3},{12,4},{101,5},{14,6},{103,7},{0,8},{10... | collective-permute-start | bytes 393224 | tf_op jit(solution)/shard_map/ppermute | solution.py:35
  20.8 6.1 %collective-permute-start.3 = (bf16[8,8192]{1,0:T(8,128)(2,1)S(1)}, bf16[8,8192]{1,0:T(8,128)(2,1)S(1)}, u32[]{:S(2)}, u32[]{:S(2)}) collective-permute-start(bf16[8,8192]{1,0:T(8,128)(2,1)S(1)} %pad_maximum_fusion.1.refs_0_), channel_id=1, source_target_pairs={{2,0},{33,1},{0,2},{35,3},{6,4},{37,5},{4,6},{39,7},{10,8},{41,9},... | collective-permute-start | bytes 393224 | tf_op jit(solution)/shard_map/ppermute | solution.py:35
  27.0 11.2 %collective-permute-start.8 = (bf16[32,8192]{1,0:T(8,128)(2,1)S(1)}, bf16[32,8192]{1,0:T(8,128)(2,1)S(1)}, u32[]{:S(2)}, u32[]{:S(2)}) collective-permute-start(bf16[32,8192]{1,0:T(8,128)(2,1)S(1)} %shard_map.111.refs_0_), channel_id=1, source_target_pairs={{116,0},{29,1},{118,2},{31,3},{120,4},{17,5},{122,6},{19,7},{124,8... | collective-permute-start | bytes 1572872 | tf_op jit(solution)/shard_map/ppermute | solution.py:35
  29.5 15.6 %collective-permute-start.7 = (bf16[32,8192]{1,0:T(8,128)(2,1)S(1)}, bf16[32,8192]{1,0:T(8,128)(2,1)S(1)}, u32[]{:S(2)}, u32[]{:S(2)}) collective-permute-start(bf16[32,8192]{1,0:T(8,128)(2,1)S(1)} %shard_map.111.refs_0_), channel_id=1, source_target_pairs={{16,0},{113,1},{18,2},{115,3},{20,4},{117,5},{22,6},{119,7},{24,8}... | collective-permute-start | bytes 1572872 | tf_op jit(solution)/shard_map/ppermute | solution.py:35
  29.5 15.6 %collective-permute-start.6 = (bf16[32,8192]{1,0:T(8,128)(2,1)S(1)}, bf16[32,8192]{1,0:T(8,128)(2,1)S(1)}, u32[]{:S(2)}, u32[]{:S(2)}) collective-permute-start(bf16[32,8192]{1,0:T(8,128)(2,1)S(1)} %shard_map.111.refs_0_), channel_id=1, source_target_pairs={{4,0},{13,1},{6,2},{15,3},{8,4},{1,5},{10,6},{3,7},{12,8},{5,9},{1... | collective-permute-start | bytes 1572872 | tf_op jit(solution)/shard_map/ppermute | solution.py:35
  31.8 17.4 %collective-permute-start.9 = (bf16[32,8192]{1,0:T(8,128)(2,1)S(1)}, bf16[32,8192]{1,0:T(8,128)(2,1)S(1)}, u32[]{:S(2)}, u32[]{:S(2)}) collective-permute-start(bf16[32,8192]{1,0:T(8,128)(2,1)S(1)} %shard_map.111.refs_0_), channel_id=1, source_target_pairs={{1,0},{0,1},{3,2},{2,3},{5,4},{4,5},{7,6},{6,7},{9,8},{8,9},{11,10... | collective-permute-start | bytes 1572872 | tf_op jit(solution)/shard_map/ppermute | solution.py:35
  38.1 11.0 %collective-permute-start.12 = (bf16[32,8192]{1,0:T(8,128)(2,1)S(1)}, bf16[32,8192]{1,0:T(8,128)(2,1)S(1)}, u32[]{:S(2)}, u32[]{:S(2)}) collective-permute-start(bf16[32,8192]{1,0:T(8,128)(2,1)S(1)} %collective-permute-done.8.refs_3_), channel_id=1, source_target_pairs={{1,0},{0,1},{3,2},{2,3},{5,4},{4,5},{7,6},{6,7},{9,8},{8,9},{11,10... | collective-permute-start | bytes 1572872 | tf_op jit(solution)/shard_map/ppermute | solution.py:35
  45.0 4.8 %collective-permute-start.10 = (bf16[32,8192]{1,0:T(8,128)(2,1)S(1)}, bf16[32,8192]{1,0:T(8,128)(2,1)S(1)}, u32[]{:S(2)}, u32[]{:S(2)}) collective-permute-start(bf16[32,8192]{1,0:T(8,128)(2,1)S(1)} %collective-permute-done.6.refs_1_), channel_id=1, source_target_pairs={{1,0},{0,1},{3,2},{2,3},{5,4},{4,5},{7,6},{6,7},{9,8},{8,9},{11,10... | collective-permute-start | bytes 1572872 | tf_op jit(solution)/shard_map/ppermute | solution.py:35
  58.7 12.6 %collective-permute-start.16 = (bf16[32,8192]{1,0:T(8,128)(2,1)S(1)}, bf16[32,8192]{1,0:T(8,128)(2,1)S(1)}, u32[]{:S(2)}, u32[]{:S(2)}) collective-permute-start(bf16[32,8192]{1,0:T(8,128)(2,1)S(1)} %fusion.16), channel_id=1, source_target_pairs={{28,0},{117,1},{30,2},{119,3},{16,4},{121,5},{18,6},{123,7},{20,8}... | collective-permute-start | bytes 1572872 | tf_op jit(solution)/shard_map/ppermute | solution.py:35
  62.3 10.8 %collective-permute-start.17 = (bf16[32,8192]{1,0:T(8,128)(2,1)S(1)}, bf16[32,8192]{1,0:T(8,128)(2,1)S(1)}, u32[]{:S(2)}, u32[]{:S(2)}) collective-permute-start(bf16[32,8192]{1,0:T(8,128)(2,1)S(1)} %get-tuple-element.24), channel_id=1, source_target_pairs={{112,0},{17,1},{114,2},{19,3},{116,4},{21,5},{118,6},{23,7},{120,8... | collective-permute-start | bytes 1572872 | tf_op jit(solution)/shard_map/ppermute | solution.py:35
  64.4 10.9 %collective-permute-start.18 = (bf16[32,8192]{1,0:T(8,128)(2,1)S(1)}, bf16[32,8192]{1,0:T(8,128)(2,1)S(1)}, u32[]{:S(2)}, u32[]{:S(2)}) collective-permute-start(bf16[32,8192]{1,0:T(8,128)(2,1)S(1)} %get-tuple-element.25), channel_id=1, source_target_pairs={{12,0},{5,1},{14,2},{7,3},{0,4},{9,5},{2,6},{11,7},{4,8},{13,9},{6... | collective-permute-start | bytes 1572872 | tf_op jit(solution)/shard_map/ppermute | solution.py:35
  75.5 10.5 %collective-permute-start.19 = (bf16[8,8192]{1,0:T(8,128)(2,1)S(1)}, bf16[8,8192]{1,0:T(8,128)(2,1)S(1)}, u32[]{:S(2)}, u32[]{:S(2)}) collective-permute-start(bf16[8,8192]{1,0:T(8,128)(2,1)S(1)} %get-tuple-element.26), channel_id=1, source_target_pairs={{10,0},{65,1},{8,2},{67,3},{14,4},{69,5},{12,6},{71,7},{2,8},{73,9... | collective-permute-start | bytes 393224 | tf_op jit(solution)/shard_map/ppermute | solution.py:35
  79.9 7.5 %collective-permute-start.21 = (bf16[8,8192]{1,0:T(8,128)(2,1)S(1)}, bf16[8,8192]{1,0:T(8,128)(2,1)S(1)}, u32[]{:S(2)}, u32[]{:S(2)}) collective-permute-start(bf16[8,8192]{1,0:T(8,128)(2,1)S(1)} %get-tuple-element.27), channel_id=1, source_target_pairs={{2,0},{97,1},{0,2},{99,3},{6,4},{101,5},{4,6},{103,7},{10,8},{105,... | collective-permute-start | bytes 393224 | tf_op jit(solution)/shard_map/ppermute | solution.py:35
  79.9 7.5 %collective-permute-start.20 = (bf16[8,8192]{1,0:T(8,128)(2,1)S(1)}, bf16[8,8192]{1,0:T(8,128)(2,1)S(1)}, u32[]{:S(2)}, u32[]{:S(2)}) collective-permute-start(bf16[8,8192]{1,0:T(8,128)(2,1)S(1)} %get-tuple-element.28), channel_id=1, source_target_pairs={{8,0},{33,1},{10,2},{35,3},{12,4},{37,5},{14,6},{39,7},{0,8},{41,9... | collective-permute-start | bytes 393224 | tf_op jit(solution)/shard_map/ppermute | solution.py:35
  87.4 5.7 %collective-permute-start.24 = (bf16[8,8192]{1,0:T(8,128)(2,1)S(1)}, bf16[8,8192]{1,0:T(8,128)(2,1)S(1)}, u32[]{:S(2)}, u32[]{:S(2)}) collective-permute-start(bf16[8,8192]{1,0:T(8,128)(2,1)S(1)} %fusion.19), channel_id=1, source_target_pairs={{32,0},{3,1},{34,2},{1,3},{36,4},{7,5},{38,6},{5,7},{40,8},{11,9},... | collective-permute-start | bytes 393224 | tf_op jit(solution)/shard_map/ppermute | solution.py:35
  88.6 7.7 %collective-permute-start.23 = (bf16[8,8192]{1,0:T(8,128)(2,1)S(1)}, bf16[8,8192]{1,0:T(8,128)(2,1)S(1)}, u32[]{:S(2)}, u32[]{:S(2)}) collective-permute-start(bf16[8,8192]{1,0:T(8,128)(2,1)S(1)} %fusion.19), channel_id=1, source_target_pairs={{64,0},{11,1},{66,2},{9,3},{68,4},{15,5},{70,6},{13,7},{72,8},{3,9... | collective-permute-start | bytes 393224 | tf_op jit(solution)/shard_map/ppermute | solution.py:35
  92.0 5.3 %collective-permute-start.22 = (bf16[8,8192]{1,0:T(8,128)(2,1)S(1)}, bf16[8,8192]{1,0:T(8,128)(2,1)S(1)}, u32[]{:S(2)}, u32[]{:S(2)}) collective-permute-start(bf16[8,8192]{1,0:T(8,128)(2,1)S(1)} %fusion.19), channel_id=1, source_target_pairs={{96,0},{9,1},{98,2},{11,3},{100,4},{13,5},{102,6},{15,7},{104,8},{... | collective-permute-start | bytes 393224 | tf_op jit(solution)/shard_map/ppermute | solution.py:35
  97.8 8.0 %collective-permute-start.27 = (bf16[8,8192]{1,0:T(8,128)(2,1)S(1)}, bf16[8,8192]{1,0:T(8,128)(2,1)S(1)}, u32[]{:S(2)}, u32[]{:S(2)}) collective-permute-start(bf16[8,8192]{1,0:T(8,128)(2,1)S(1)} %multiply_convert_fusion.refs_0_), channel_id=1, source_target_pairs={{10,0},{65,1},{8,2},{67,3},{14,4},{69,5},{12,6},{71,7},{2,8},{73,9... | collective-permute-start | bytes 393224 | tf_op jit(solution)/shard_map/ppermute | solution.py:35
  100.7 8.4 %collective-permute-start.26 = (bf16[8,8192]{1,0:T(8,128)(2,1)S(1)}, bf16[8,8192]{1,0:T(8,128)(2,1)S(1)}, u32[]{:S(2)}, u32[]{:S(2)}) collective-permute-start(bf16[8,8192]{1,0:T(8,128)(2,1)S(1)} %multiply_convert_fusion.refs_0_), channel_id=1, source_target_pairs={{8,0},{97,1},{10,2},{99,3},{12,4},{101,5},{14,6},{103,7},{0,8},{10... | collective-permute-start | bytes 393224 | tf_op jit(solution)/shard_map/ppermute | solution.py:35
  102.7 6.4 %collective-permute-start.25 = (bf16[8,8192]{1,0:T(8,128)(2,1)S(1)}, bf16[8,8192]{1,0:T(8,128)(2,1)S(1)}, u32[]{:S(2)}, u32[]{:S(2)}) collective-permute-start(bf16[8,8192]{1,0:T(8,128)(2,1)S(1)} %multiply_convert_fusion.refs_0_), channel_id=1, source_target_pairs={{2,0},{33,1},{0,2},{35,3},{6,4},{37,5},{4,6},{39,7},{10,8},{41,9},... | collective-permute-start | bytes 393224 | tf_op jit(solution)/shard_map/ppermute | solution.py:35
  109.2 11.2 %collective-permute-start.30 = (bf16[32,8192]{1,0:T(8,128)(2,1)S(1)}, bf16[32,8192]{1,0:T(8,128)(2,1)S(1)}, u32[]{:S(2)}, u32[]{:S(2)}) collective-permute-start(bf16[32,8192]{1,0:T(8,128)(2,1)S(1)} %shard_map.115.refs_0_), channel_id=1, source_target_pairs={{116,0},{29,1},{118,2},{31,3},{120,4},{17,5},{122,6},{19,7},{124,8... | collective-permute-start | bytes 1572872 | tf_op jit(solution)/shard_map/ppermute | solution.py:35
  111.5 15.4 %collective-permute-start.29 = (bf16[32,8192]{1,0:T(8,128)(2,1)S(1)}, bf16[32,8192]{1,0:T(8,128)(2,1)S(1)}, u32[]{:S(2)}, u32[]{:S(2)}) collective-permute-start(bf16[32,8192]{1,0:T(8,128)(2,1)S(1)} %shard_map.115.refs_0_), channel_id=1, source_target_pairs={{16,0},{113,1},{18,2},{115,3},{20,4},{117,5},{22,6},{119,7},{24,8}... | collective-permute-start | bytes 1572872 | tf_op jit(solution)/shard_map/ppermute | solution.py:35
  112.6 14.3 %collective-permute-start.28 = (bf16[32,8192]{1,0:T(8,128)(2,1)S(1)}, bf16[32,8192]{1,0:T(8,128)(2,1)S(1)}, u32[]{:S(2)}, u32[]{:S(2)}) collective-permute-start(bf16[32,8192]{1,0:T(8,128)(2,1)S(1)} %shard_map.115.refs_0_), channel_id=1, source_target_pairs={{4,0},{13,1},{6,2},{15,3},{8,4},{1,5},{10,6},{3,7},{12,8},{5,9},{1... | collective-permute-start | bytes 1572872 | tf_op jit(solution)/shard_map/ppermute | solution.py:35
  112.6 18.7 %collective-permute-start.31 = (bf16[32,8192]{1,0:T(8,128)(2,1)S(1)}, bf16[32,8192]{1,0:T(8,128)(2,1)S(1)}, u32[]{:S(2)}, u32[]{:S(2)}) collective-permute-start(bf16[32,8192]{1,0:T(8,128)(2,1)S(1)} %shard_map.115.refs_0_), channel_id=1, source_target_pairs={{1,0},{0,1},{3,2},{2,3},{5,4},{4,5},{7,6},{6,7},{9,8},{8,9},{11,10... | collective-permute-start | bytes 1572872 | tf_op jit(solution)/shard_map/ppermute | solution.py:35
  120.3 11.0 %collective-permute-start.34 = (bf16[32,8192]{1,0:T(8,128)(2,1)S(1)}, bf16[32,8192]{1,0:T(8,128)(2,1)S(1)}, u32[]{:S(2)}, u32[]{:S(2)}) collective-permute-start(bf16[32,8192]{1,0:T(8,128)(2,1)S(1)} %collective-permute-done.30.refs_3_), channel_id=1, source_target_pairs={{1,0},{0,1},{3,2},{2,3},{5,4},{4,5},{7,6},{6,7},{9,8},{8,9},{11,10... | collective-permute-start | bytes 1572872 | tf_op jit(solution)/shard_map/ppermute | solution.py:35
  126.9 4.4 %collective-permute-start.33 = (bf16[32,8192]{1,0:T(8,128)(2,1)S(1)}, bf16[32,8192]{1,0:T(8,128)(2,1)S(1)}, u32[]{:S(2)}, u32[]{:S(2)}) collective-permute-start(bf16[32,8192]{1,0:T(8,128)(2,1)S(1)} %collective-permute-done.29.refs_2_), channel_id=1, source_target_pairs={{1,0},{0,1},{3,2},{2,3},{5,4},{4,5},{7,6},{6,7},{9,8},{8,9},{11,10... | collective-permute-start | bytes 1572872 | tf_op jit(solution)/shard_map/ppermute | solution.py:35
  126.9 5.1 %collective-permute-start.32 = (bf16[32,8192]{1,0:T(8,128)(2,1)S(1)}, bf16[32,8192]{1,0:T(8,128)(2,1)S(1)}, u32[]{:S(2)}, u32[]{:S(2)}) collective-permute-start(bf16[32,8192]{1,0:T(8,128)(2,1)S(1)} %collective-permute-done.28.refs_1_), channel_id=1, source_target_pairs={{1,0},{0,1},{3,2},{2,3},{5,4},{4,5},{7,6},{6,7},{9,8},{8,9},{11,10... | collective-permute-start | bytes 1572872 | tf_op jit(solution)/shard_map/ppermute | solution.py:35
  133.1 4.6 %collective-permute-start.35 = (bf16[256,128]{1,0:T(8,128)(2,1)S(1)}, bf16[256,128]{1,0:T(8,128)(2,1)S(1)}, u32[]{:S(2)}, u32[]{:S(2)}) collective-permute-start(bf16[256,128]{1,0:T(8,128)(2,1)S(1)} %fusion.21), channel_id=1, source_target_pairs={{0,128},{128,0},{1,129},{129,1},{2,130},{130,2},{3,131},{131,3},{4... | collective-permute-start | bytes 196616 | tf_op jit(solution)/shard_map/ppermute | solution.py:107
  (9 other events, 90.9 us)
